TPU v7x, 32 devices: a whole 2x2x4 slice. The times are simulated.
32 devices in a mesh: cuts: 2 (over core), tile: 16 (over z, y, x).
Axes of the slice: x: 2, y: 2, z: 4, core: 2. Of those that a mesh axis runs over, the one named last changes fastest.
Arguments:
- object_slices: float32 [2, 2, 2048, 4096], P('cuts', None, None, 'tile'), may hold values from -5 to 5
- probe_field: float32 [2, 256, 256], replicated, may hold values from -4 to 4
- slice_phase: float32 [2, 256, 256], P('cuts'), may hold values from -3.140625 to 3.140625
- intensity: float32 [16, 8, 256, 256], P('tile'), may hold values from 0 to 1
- counts: int32 [16], P('tile'), may hold values from 1 to 6, as said below
- chosen: int32 [16, 6], P('tile'), may hold values from 0 to 7, as said below
- row_offset: int32 [16, 8], P('tile'), may hold values from 0 to 1792
- column_offset: int32 [16, 8], P('tile'), may hold values from 0 to 255
Outputs:
- object_grad: float32 [2, 2, 2048, 4096], P('cuts', None, None, 'tile')
Inputs may be any that keep to these rules, and one draw needn't show every extreme that they name: `counts`: live slots of a tile; some tile has exactly 6. `chosen`: distinct within a tile.
All inputs are finite; a program needn't handle non-finite values.
Results may differ from a plain program's by a relative error of at most 0.039.
Values may be sent and summed in bfloat16 or wider, within the bound.
No kernel may reach another device: no remote copies, remote signals or barrier semaphores. Data moves between devices by JAX's collectives and lax.ppermute only.
A program may use at most 128 MiB of HBM per device.

v0:
```python
import jax
import jax.numpy as jnp
from jax import lax
from jax.sharding import PartitionSpec as P


def from_behind(value, axis, steps):
    count = lax.axis_size(axis)
    first, last = (max(0, -steps), min(count, count - steps))
    return lax.ppermute(value, axis, [(source, source + steps) for source in range(first, last)])


def make_table(length, direction):
    index = jnp.arange(length, dtype=jnp.int32)
    product = index[:, None] * index[None, :] % length
    angle = product.astype(jnp.float32) * (2.0 * jnp.pi / length)
    scale = length ** (-0.5)
    cosine = jnp.cos(angle) * scale
    sine = direction * jnp.sin(angle) * scale
    matrix = jnp.stack([jnp.stack([cosine, sine]), jnp.stack([-sine, cosine])])
    return matrix.astype(jnp.bfloat16)


def transform(field, matrix):
    halfway = jnp.einsum(
        "bcnm,cdmk->bdnk", field.astype(jnp.bfloat16), matrix, preferred_element_type=jnp.float32
    )
    return jnp.einsum(
        "cdkn,bcnm->bdkm", matrix, halfway.astype(jnp.bfloat16), preferred_element_type=jnp.float32
    )


def rotate(field, cosine, sine):
    real_part = field[:, 0]
    imag_part = field[:, 1]
    return jnp.stack(
        [real_part * cosine - imag_part * sine, real_part * sine + imag_part * cosine], axis=1
    )


def complex_mul(left, right):
    return jnp.stack(
        [
            left[:, 0] * right[:, 0] - left[:, 1] * right[:, 1],
            left[:, 0] * right[:, 1] + left[:, 1] * right[:, 0],
        ],
        axis=1,
    )


def conj_mul(left, right):
    return jnp.stack(
        [
            left[:, 0] * right[:, 0] + left[:, 1] * right[:, 1],
            left[:, 0] * right[:, 1] - left[:, 1] * right[:, 0],
        ],
        axis=1,
    )


def deposit(canvas, pieces, row_starts, col_starts):
    extent = pieces.shape[1:]
    for slot_index in range(pieces.shape[0]):
        corner = (0, 0, row_starts[slot_index], col_starts[slot_index])
        current = lax.dynamic_slice(canvas, corner, extent)
        canvas = lax.dynamic_update_slice(canvas, current + pieces[slot_index], corner)
    return canvas


def on_device(
    object_slices, probe_field, slice_phase, intensity, counts, chosen, row_offset, column_offset
):
    slice_count, _, height, breadth = object_slices.shape
    pattern = probe_field.shape[-1]
    slot_count = chosen.shape[1]
    cut_index = lax.axis_index("cuts")
    cut_total = lax.axis_size("cuts")
    forward_table = make_table(pattern, -1.0)
    inverse_table = make_table(pattern, 1.0)
    cosines = jnp.cos(slice_phase)
    sines = jnp.sin(slice_phase)
    picked = chosen[0]
    onehot = picked[:, None] == jnp.arange(row_offset.shape[1], dtype=jnp.int32)[None, :]
    row_starts = jnp.sum(jnp.where(onehot, row_offset[0][None, :], 0), axis=1)
    col_starts = jnp.sum(jnp.where(onehot, column_offset[0][None, :], 0), axis=1)
    is_live = jnp.arange(slot_count, dtype=jnp.int32) < counts[0]
    measured = jnp.take(intensity[0], picked, axis=0)
    extent = (slice_count, 2, pattern, pattern)
    neighbour = from_behind(object_slices.astype(jnp.bfloat16), "tile", -1).astype(
        object_slices.dtype
    )
    extended = jnp.concatenate([object_slices, neighbour], axis=3)

    def single(row_start, col_start):
        return lax.dynamic_slice(extended, (0, 0, row_start, col_start), extent)

    patches = jax.vmap(single)(row_starts, col_starts)
    groups = 1
    per_group = slot_count // groups
    turns = groups + cut_total - 1
    start_wave = jnp.broadcast_to(probe_field, (per_group, 2, pattern, pattern))

    def forward_turn(turn_index, carried):
        incoming, saved_in, saved_out = carried
        group_index = turn_index - cut_index
        is_valid = (group_index >= 0) & (group_index < groups)
        first_slot = jnp.clip(group_index, 0, groups - 1) * per_group
        current = jnp.where(cut_index == 0, start_wave, incoming.astype(jnp.float32))
        inputs = [current]
        product = complex_mul(current, patches[:, 0])
        spectrum = rotate(transform(product, forward_table), cosines[0], sines[0])
        outgoing = transform(spectrum, inverse_table).astype(jnp.bfloat16)
        stacked = jnp.stack(inputs, axis=1)
        previous_in = saved_in
        saved_in = lax.dynamic_update_slice_in_dim(
            saved_in, jnp.where(is_valid, stacked, previous_in), first_slot, 0
        )
        previous_out = saved_out
        saved_out = jnp.where(is_valid, outgoing, previous_out)
        incoming = from_behind(outgoing, "cuts", 1)
        return (incoming, saved_in, saved_out)

    forward_start = (
        jnp.zeros((per_group, 2, pattern, pattern), jnp.bfloat16),
        jnp.zeros((slot_count, slice_count, 2, pattern, pattern), jnp.float32),
        jnp.zeros((slot_count, 2, pattern, pattern), jnp.bfloat16),
    )
    _, saved_in, saved_out = lax.fori_loop(0, turns, forward_turn, forward_start)
    exit_wave = saved_out.astype(jnp.float32)
    power = exit_wave[:, 0] * exit_wave[:, 0] + exit_wave[:, 1] * exit_wave[:, 1]
    residual = jnp.where(
        is_live[:, None, None, None], 2.0 * (power - measured)[:, None] * exit_wave, 0.0
    )

    def backward_turn(turn_index, carried):
        incoming, slice_grads = carried
        group_index = turn_index - (cut_total - 1 - cut_index)
        is_valid = (group_index >= 0) & (group_index < groups)
        first_slot = jnp.clip(group_index, 0, groups - 1) * per_group
        cotangent = jnp.where(cut_index == cut_total - 1, residual, incoming.astype(jnp.float32))
        grads = [None] * slice_count
        for slice_index in reversed(range(slice_count)):
            spectrum = rotate(
                transform(cotangent, forward_table), cosines[slice_index], -sines[slice_index]
            )
            spread = transform(spectrum, inverse_table)
            grads[slice_index] = conj_mul(saved_in[:, slice_index], spread)
            cotangent = conj_mul(patches[:, slice_index], spread)
        stacked = jnp.stack(grads, axis=1)
        previous = slice_grads
        slice_grads = lax.dynamic_update_slice_in_dim(
            slice_grads, jnp.where(is_valid, stacked, previous), first_slot, 0
        )
        incoming = from_behind(cotangent.astype(jnp.bfloat16), "cuts", -1)
        return (incoming, slice_grads)

    backward_start = (
        jnp.zeros((per_group, 2, pattern, pattern), jnp.bfloat16),
        jnp.zeros((slot_count, slice_count, 2, pattern, pattern), jnp.float32),
    )
    _, slice_grads = lax.fori_loop(0, turns, backward_turn, backward_start)
    empty_canvas = jnp.zeros((slice_count, 2, height, 2 * breadth), jnp.float32)
    canvas = deposit(empty_canvas, slice_grads, row_starts, col_starts)
    carried = from_behind(canvas[..., breadth:].astype(jnp.bfloat16), "tile", 1).astype(jnp.float32)
    object_grad = canvas[..., :breadth] + carried
    return object_grad


def solution(mesh):
    return jax.shard_map(
        on_device,
        mesh=mesh,
        in_specs=(
            P("cuts", None, None, "tile"),
            P(),
            P("cuts", None, None),
            P("tile", None, None, None),
            P("tile"),
            P("tile", None),
            P("tile", None),
            P("tile", None),
        ),
        out_specs=P("cuts", None, None, "tile"),
        check_vma=False,
    )
```

profile of v0, /device:TPU:17, one launch (start us, length us, event | category | flops | bytes accessed | tf_op | source)
XLA Modules:
  0.0 307.0 jit_solution(4268787903401569933)
XLA Ops:
  0.0 3.9 %convert_element_type.165 = bf16[1,2,2048,256]{3,2,1,0:T(8,128)(2,1)} convert(f32[1,2,2048,256]{3,2,1,0:T(8,128)} %param.12) | non-fusion elementwise | flops 1048576 | bytes 6291456 | tf_op jit(solution)/shard_map/convert_element_type | solution.py:89
  3.9 4.0 %collective-permute-start.2 = (bf16[1,2,2048,256]{3,2,1,0:T(8,128)(2,1)}, bf16[1,2,2048,256]{3,2,1,0:T(8,128)(2,1)}, u32[]{:S(2)}, u32[]{:S(2)}) collective-permute-start(bf16[1,2,2048,256]{3,2,1,0:T(8,128)(2,1)} %convert_element_type.165), channel_id=1, source_target_pairs={{1,0},{2,1},{3,2},{4,3},{5,4},{6,5},{7,6},{8,7},{9,8},{10,9},{11,1... | collective-permute-start | bytes 6291464 | tf_op jit(solution)/shard_map/ppermute | solution.py:10
  25.7 1.3 multiply_convert_fusion
  30.6 1.8 gather_fusion
  40.8 11.8 %collective-permute-done.2 = bf16[1,2,2048,256]{3,2,1,0:T(8,128)(2,1)} collective-permute-done((bf16[1,2,2048,256]{3,2,1,0:T(8,128)(2,1)}, bf16[1,2,2048,256]{3,2,1,0:T(8,128)(2,1)}, u32[]{:S(2)}, u32[]{:S(2)}) %collective-permute-start.2) | collective-permute-done | bytes 2097184 | tf_op jit(solution)/shard_map/ppermute | solution.py:10
  52.6 1.9 convert_element_type.166
  54.5 4.6 %pad_maximum_fusion.1 = f32[1,2,2048,512]{3,2,1,0:T(8,128)} fusion(f32[1,2,2048,256]{3,2,1,0:T(8,128)S(1)} %convert_element_type.166, f32[1,2,2048,256]{3,2,1,0:T(8,128)S(1)} %copy-done.3), kind=kLoop, calls=%fused_computation.52 | loop fusion | flops 2097152 | bytes 16777216 | tf_op jit(solution)/shard_map/concatenate | solution.py:92
  59.1 23.6 %while.38 = (s32[]{:T(128)}, f32[1,2,2048,512]{3,2,1,0:T(8,128)}, s32[6,4]{0,1:T(4,128)S(1)}, f32[6,1,2,256,256]{4,3,2,1,0:T(8,128)}, s32[]{:T(128)}) while((s32[]{:T(128)}, f32[1,2,2048,512]{3,2,1,0:T(8,128)}, s32[6,4]{0,1:T(4,128)S(1)}, f32[6,1,2,256,256]{4,3,2,1,0:T(8,128)}, s32[]{:T(128)}) %tuple.132), condition=%wide.while_cond, body=%wide.while_body.sunk | while | flops 2 | bytes 1050225 | solution.py:95
  59.7 3.3 %bitcast_dynamic-update-slice_fusion.2 = f32[6,1,2,256,256]{4,3,2,1,0:T(8,128)} fusion(f32[6,1,2,256,256]{4,3,2,1,0:T(8,128)} %get-tuple-element.975, s32[]{:T(128)} %get-tuple-element.972, f32[1,2,2048,512]{3,2,1,0:T(8,128)} %get-tuple-element.978, s32[]{:T(128)} %bitcast.260, s32[]{:T(128)} %bitcast.261), kind=kLoop, calls=%fused_computation.2.clone.1 | loop fusion | bytes 1050112 | tf_op jit(solution)/shard_map/vmap()/gather
  63.6 3.3 %bitcast_dynamic-update-slice_fusion.2 = f32[6,1,2,256,256]{4,3,2,1,0:T(8,128)} fusion(f32[6,1,2,256,256]{4,3,2,1,0:T(8,128)} %get-tuple-element.975, s32[]{:T(128)} %get-tuple-element.972, f32[1,2,2048,512]{3,2,1,0:T(8,128)} %get-tuple-element.978, s32[]{:T(128)} %bitcast.260, s32[]{:T(128)} %bitcast.261), kind=kLoop, calls=%fused_computation.2.clone.1 | loop fusion | bytes 1050112 | tf_op jit(solution)/shard_map/vmap()/gather
  67.6 3.4 %bitcast_dynamic-update-slice_fusion.2 = f32[6,1,2,256,256]{4,3,2,1,0:T(8,128)} fusion(f32[6,1,2,256,256]{4,3,2,1,0:T(8,128)} %get-tuple-element.975, s32[]{:T(128)} %get-tuple-element.972, f32[1,2,2048,512]{3,2,1,0:T(8,128)} %get-tuple-element.978, s32[]{:T(128)} %bitcast.260, s32[]{:T(128)} %bitcast.261), kind=kLoop, calls=%fused_computation.2.clone.1 | loop fusion | bytes 1050112 | tf_op jit(solution)/shard_map/vmap()/gather
  71.5 3.3 %bitcast_dynamic-update-slice_fusion.2 = f32[6,1,2,256,256]{4,3,2,1,0:T(8,128)} fusion(f32[6,1,2,256,256]{4,3,2,1,0:T(8,128)} %get-tuple-element.975, s32[]{:T(128)} %get-tuple-element.972, f32[1,2,2048,512]{3,2,1,0:T(8,128)} %get-tuple-element.978, s32[]{:T(128)} %bitcast.260, s32[]{:T(128)} %bitcast.261), kind=kLoop, calls=%fused_computation.2.clone.1 | loop fusion | bytes 1050112 | tf_op jit(solution)/shard_map/vmap()/gather
  75.5 3.3 %bitcast_dynamic-update-slice_fusion.2 = f32[6,1,2,256,256]{4,3,2,1,0:T(8,128)} fusion(f32[6,1,2,256,256]{4,3,2,1,0:T(8,128)} %get-tuple-element.975, s32[]{:T(128)} %get-tuple-element.972, f32[1,2,2048,512]{3,2,1,0:T(8,128)} %get-tuple-element.978, s32[]{:T(128)} %bitcast.260, s32[]{:T(128)} %bitcast.261), kind=kLoop, calls=%fused_computation.2.clone.1 | loop fusion | bytes 1050112 | tf_op jit(solution)/shard_map/vmap()/gather
  79.4 3.3 %bitcast_dynamic-update-slice_fusion.2 = f32[6,1,2,256,256]{4,3,2,1,0:T(8,128)} fusion(f32[6,1,2,256,256]{4,3,2,1,0:T(8,128)} %get-tuple-element.975, s32[]{:T(128)} %get-tuple-element.972, f32[1,2,2048,512]{3,2,1,0:T(8,128)} %get-tuple-element.978, s32[]{:T(128)} %bitcast.260, s32[]{:T(128)} %bitcast.261), kind=kLoop, calls=%fused_computation.2.clone.1 | loop fusion | bytes 1050112 | tf_op jit(solution)/shard_map/vmap()/gather
  82.7 3.5 %copy.53 = f32[6,1,2,256,256]{3,4,2,0,1:T(8,128)} copy(f32[6,1,2,256,256]{4,3,2,1,0:T(8,128)} %get-tuple-element.655) | data formatting | bytes 6291456
  86.4 44.5 %while.39 = (s32[]{:T(128)}, bf16[6,2,256,256]{2,3,1,0:T(8,128)(2,1)S(1)}, f32[6,1,2,256,256]{4,3,2,0,1:T(8,128)}, bf16[6,2,256,256]{2,3,1,0:T(8,128)(2,1)}, pre...) while((s32[]{:T(128)}, ...), condition=%wide.region_3.4_spmd.clone, body=%wide.region_2.3_spmd.clone.sunk | while | flops 3242459136 | bytes 48234716 | solution.py:128
  87.1 1.4 convert_select_fusion.2
  88.5 2.4 subtract_convert_fusion.7
  90.9 4.7 %convolution_bitcast_fusion.6 = f32[6,2,256,256]{2,3,1,0:T(8,128)} fusion(bf16[6,1,256,256]{3,2,1,0:T(8,128)(2,1)S(1)} %get-tuple-element.943, bf16[6,1,256,256]{3,2,1,0:T(8,128)(2,1)S(1)} %get-tuple-element.944, bf16[2,2,256,256]{3,2,0,1:T(8,128)(2,1)} %get-tuple-element.1016), kind=kOutput, calls=%fused_computation.9.clone.1 | convolution fusion | flops 1614544896 | bytes 5242880 | tf_op jit(solution)/shard_map/while/body/eval_jaxpr/cdkn,bcnm->bdkm/dot_general | solution.py:28
  95.6 2.3 subtract_convert_fusion.8
  98.0 4.7 %select_select_fusion.2 = (bf16[6,2,256,256]{2,3,1,0:T(8,128)(2,1)}, bf16[6,2,256,256]{2,3,1,0:T(8,128)(2,1)}) fusion(bf16[6,2,256,256]{2,3,1,0:T(8,128)(2,1)} %get-tuple-element.999, pred[]{:T(512)S(6)} %compare.27, pred[]{:T(512)S(6)} %and.108, bf16[2,2,256,256]{3,2,0,1:T(8,128)(2,1)} %get-tuple-element.1019, ...), kind=kOutput, calls=%fused_computation.18.clone.1 | convolution fusion | flops 1616904192 | bytes 6815746 | tf_op jit(solution)/shard_map/while/body/eval_jaxpr/cdkn,bcnm->bdkm/dot_general | solution.py:28
  104.0 3.2 %bitcast_select_fusion.3 = f32[6,1,2,256,256]{4,3,2,0,1:T(8,128)} fusion(f32[6,1,2,256,256]{4,3,2,0,1:T(8,128)} %get-tuple-element.998, pred[]{:T(512)S(6)} %compare.27, pred[]{:T(512)S(6)} %and.108, bf16[6,2,256,256]{3,2,1,0:T(8,128)(2,1)S(1)} %copy.94, f32[2,256,256]{2,1,0:T(8,128)} %get-tuple-element.1021, pred[]{:T(512)} %get-tuple-element.1014), kind=kLoop, calls=%fused_computation.4.clone.1 | loop fusion | flops 3145728 | bytes 8388611 | tf_op jit(solution)/shard_map/while/body/eval_jaxpr/jit(_where)/select_n | solution.py:116
  107.2 1.4 collective-permute-done
  109.3 1.4 convert_select_fusion.2
  110.7 2.4 subtract_convert_fusion.7
  113.1 4.7 %convolution_bitcast_fusion.6 = f32[6,2,256,256]{2,3,1,0:T(8,128)} fusion(bf16[6,1,256,256]{3,2,1,0:T(8,128)(2,1)S(1)} %get-tuple-element.943, bf16[6,1,256,256]{3,2,1,0:T(8,128)(2,1)S(1)} %get-tuple-element.944, bf16[2,2,256,256]{3,2,0,1:T(8,128)(2,1)} %get-tuple-element.1016), kind=kOutput, calls=%fused_computation.9.clone.1 | convolution fusion | flops 1614544896 | bytes 5242880 | tf_op jit(solution)/shard_map/while/body/eval_jaxpr/cdkn,bcnm->bdkm/dot_general | solution.py:28
  117.8 2.3 subtract_convert_fusion.8
  120.1 5.2 %select_select_fusion.2 = (bf16[6,2,256,256]{2,3,1,0:T(8,128)(2,1)}, bf16[6,2,256,256]{2,3,1,0:T(8,128)(2,1)}) fusion(bf16[6,2,256,256]{2,3,1,0:T(8,128)(2,1)} %get-tuple-element.999, pred[]{:T(512)S(6)} %compare.27, pred[]{:T(512)S(6)} %and.108, bf16[2,2,256,256]{3,2,0,1:T(8,128)(2,1)} %get-tuple-element.1019, ...), kind=kOutput, calls=%fused_computation.18.clone.1 | convolution fusion | flops 1616904192 | bytes 6815746 | tf_op jit(solution)/shard_map/while/body/eval_jaxpr/cdkn,bcnm->bdkm/dot_general | solution.py:28
  126.7 4.2 %bitcast_select_fusion.3 = f32[6,1,2,256,256]{4,3,2,0,1:T(8,128)} fusion(f32[6,1,2,256,256]{4,3,2,0,1:T(8,128)} %get-tuple-element.998, pred[]{:T(512)S(6)} %compare.27, pred[]{:T(512)S(6)} %and.108, bf16[6,2,256,256]{3,2,1,0:T(8,128)(2,1)S(1)} %copy.94, f32[2,256,256]{2,1,0:T(8,128)} %get-tuple-element.1021, pred[]{:T(512)} %get-tuple-element.1014), kind=kLoop, calls=%fused_computation.4.clone.1 | loop fusion | flops 3145728 | bytes 8388611 | tf_op jit(solution)/shard_map/while/body/eval_jaxpr/jit(_where)/select_n | solution.py:116
  130.9 1.7 copy.52
  134.4 1.7 multiply_select_fusion
  136.1 2.8 copy.54
  138.9 2.4 copy.56
  141.3 1.4 broadcast.335
  142.7 48.6 %while.40 = (s32[]{:T(128)}, bf16[6,2,256,256]{2,3,1,0:T(8,128)(2,1)}, f32[6,1,2,256,256]{3,4,2,0,1:T(8,128)}, f32[6,1,2,256,256]{3,4,2,0,1:T(8,128)}, pred[]{:T...) while((s32[]{:T(128)}, ...), condition=%wide.region_5.6_spmd.clone, body=%wide.region_4.5_spmd.clone.sunk | while | flops 3239313408 | bytes 50331864 | solution.py:161
  142.7 4.0 %convolution_bitcast_fusion.7 = f32[6,2,256,256]{2,3,1,0:T(8,128)S(1)} fusion(bf16[6,2,256,256]{2,3,1,0:T(8,128)(2,1)} %get-tuple-element.1057, bf16[6,2,256,256]{2,3,1,0:T(8,128)(2,1)} %get-tuple-element.1039, pred[]{:T(512)} %get-tuple-element.1056, bf16[2,2,256,256]{3,2,0,1:T(8,128)(2,1)} %get-tuple-element.1058), kind=kOutput, calls=%fused_computation.34.clone.1 | convolution fusion | flops 1612972032 | bytes 6815745 | tf_op jit(solution)/shard_map/while/body/eval_jaxpr/cdkn,bcnm->bdkm/dot_general | solution.py:28
  146.7 2.5 subtract_convert_fusion.9
  149.2 5.2 %convolution_bitcast_fusion.8 = f32[6,2,256,256]{2,3,1,0:T(8,128)} fusion(bf16[6,1,256,256]{2,3,1,0:T(8,128)(2,1)} %get-tuple-element.961, bf16[6,1,256,256]{2,3,1,0:T(8,128)(2,1)} %get-tuple-element.962, bf16[2,2,256,256]{3,2,0,1:T(8,128)(2,1)} %get-tuple-element.1061), kind=kOutput, calls=%fused_computation.33.clone.1 | convolution fusion | flops 1614544896 | bytes 5242880 | tf_op jit(solution)/shard_map/while/body/eval_jaxpr/cdkn,bcnm->bdkm/dot_general | solution.py:28
  154.4 4.7 %multiply_add_fusion.2 = (f32[6,1,256,256]{2,3,1,0:T(8,128)S(1)}, f32[6,1,256,256]{2,3,1,0:T(8,128)S(1)}, bf16[6,1,256,256]{2,3,1,0:T(8,128)(2,1)S(1)}, bf16[6,1,256,256]{2,3,1,0:T(8,128)(2,1)S(1)}) fusion(f32[6,2,256,256]{2,3,1,0:T(8,128)} %bitcast.290, f32[6,2,256,256]{2,3,1,0:T(8,128)} %convolution_bitcast_fusion.8, f32[6,2,256,256]{2,3,1,0:T(8,128)} %bitcast.293), kind=kLoop, calls=%fused_computation.43.clone.1 | loop fusion | flops 5505024 | bytes 14155776 | tf_op jit(solution)/shard_map/while/body/eval_jaxpr/add | solution.py:54
  160.4 3.9 %collective-permute-start.1 = (bf16[6,2,256,256]{2,3,1,0:T(8,128)(2,1)}, bf16[6,2,256,256]{2,3,1,0:T(8,128)(2,1)}, u32[]{:S(2)}, u32[]{:S(2)}) collective-permute-start(bf16[6,2,256,256]{2,3,1,0:T(8,128)(2,1)} %pad_maximum_fusion.9), channel_id=1, source_target_pairs={{16,0},{17,1},{18,2},{19,3},{20,4},{21,5},{22,6},{23,7},{24,8},{25... | collective-permute-start | bytes 4718600 | tf_op jit(solution)/shard_map/while/body/eval_jaxpr/ppermute | solution.py:10
  164.3 2.1 fusion.89
  166.4 4.0 %convolution_bitcast_fusion.7 = f32[6,2,256,256]{2,3,1,0:T(8,128)S(1)} fusion(bf16[6,2,256,256]{2,3,1,0:T(8,128)(2,1)} %get-tuple-element.1057, bf16[6,2,256,256]{2,3,1,0:T(8,128)(2,1)} %get-tuple-element.1039, pred[]{:T(512)} %get-tuple-element.1056, bf16[2,2,256,256]{3,2,0,1:T(8,128)(2,1)} %get-tuple-element.1058), kind=kOutput, calls=%fused_computation.34.clone.1 | convolution fusion | flops 1612972032 | bytes 6815745 | tf_op jit(solution)/shard_map/while/body/eval_jaxpr/cdkn,bcnm->bdkm/dot_general | solution.py:28
  170.4 2.5 subtract_convert_fusion.9
  172.9 5.2 %convolution_bitcast_fusion.8 = f32[6,2,256,256]{2,3,1,0:T(8,128)} fusion(bf16[6,1,256,256]{2,3,1,0:T(8,128)(2,1)} %get-tuple-element.961, bf16[6,1,256,256]{2,3,1,0:T(8,128)(2,1)} %get-tuple-element.962, bf16[2,2,256,256]{3,2,0,1:T(8,128)(2,1)} %get-tuple-element.1061), kind=kOutput, calls=%fused_computation.33.clone.1 | convolution fusion | flops 1614544896 | bytes 5242880 | tf_op jit(solution)/shard_map/while/body/eval_jaxpr/cdkn,bcnm->bdkm/dot_general | solution.py:28
  178.2 4.7 %multiply_add_fusion.2 = (f32[6,1,256,256]{2,3,1,0:T(8,128)S(1)}, f32[6,1,256,256]{2,3,1,0:T(8,128)S(1)}, bf16[6,1,256,256]{2,3,1,0:T(8,128)(2,1)S(1)}, bf16[6,1,256,256]{2,3,1,0:T(8,128)(2,1)S(1)}) fusion(f32[6,2,256,256]{2,3,1,0:T(8,128)} %bitcast.290, f32[6,2,256,256]{2,3,1,0:T(8,128)} %convolution_bitcast_fusion.8, f32[6,2,256,256]{2,3,1,0:T(8,128)} %bitcast.293), kind=kLoop, calls=%fused_computation.43.clone.1 | loop fusion | flops 5505024 | bytes 14155776 | tf_op jit(solution)/shard_map/while/body/eval_jaxpr/add | solution.py:54
  184.2 3.1 collective-permute-start.1
  187.2 4.0 %fusion.89 = f32[6,1,2,256,256]{3,4,2,0,1:T(8,128)} fusion(f32[6,1,256,256]{2,3,1,0:T(8,128)S(1)} %get-tuple-element.965, f32[6,1,256,256]{2,3,1,0:T(8,128)S(1)} %get-tuple-element.966, f32[6,1,2,256,256]{3,4,2,0,1:T(8,128)} %get-tuple-element.1040, pred[]{:T(512)S(6)} %compare.28, pred[]{:T(512)S(6)} %and.109), kind=kLoop, calls=%fused_computation.29.clone.1 | loop fusion | flops 2359296 | bytes 9437186 | tf_op jit(solution)/shard_map/while/body/eval_jaxpr/jit(_where)/select_n | solution.py:152
  191.3 2.4 copy.57
  194.5 4.3 %broadcast_in_dim.63 = f32[1,2,2048,512]{3,2,1,0:T(8,128)} broadcast(f32[]{:T(128)} %constant.97.clone.1), dimensions={} | broadcast | bytes 8388612 | tf_op jit(solution)/shard_map/broadcast_in_dim | solution.py:162
  198.8 6.7 %dynamic_update_slice.24 = f32[1,2,2048,512]{3,2,1,0:T(8,128)} dynamic-update-slice(f32[1,2,2048,512]{3,2,1,0:T(8,128)} %broadcast_in_dim.63, f32[1,2,256,256]{3,2,1,0:T(8,128)} %slice_bitcast_fusion.5, s32[]{:T(128)} %constant.98.clone.1, s32[]{:T(128)} %constant.98.clone.1, s32[]{:T(128)S(6)} %select_n.255, s32[]{:T(128)S(6)} %select_n.256) | dynamic-update-slice | bytes 1048580 | tf_op jit(solution)/shard_map/dynamic_update_slice | solution.py:66
  205.5 2.1 fusion.45
  207.6 6.6 %dynamic_update_slice.25 = f32[1,2,2048,512]{3,2,1,0:T(8,128)} dynamic-update-slice(f32[1,2,2048,512]{3,2,1,0:T(8,128)} %dynamic_update_slice.24, f32[1,2,256,256]{3,2,1,0:T(8,128)} %fusion.45, s32[]{:T(128)} %constant.98.clone.1, s32[]{:T(128)} %constant.98.clone.1, s32[]{:T(128)S(6)} %select_n.257, s32[]{:T(128)S(6)} %select_n.258) | dynamic-update-slice | bytes 1048580 | tf_op jit(solution)/shard_map/dynamic_update_slice | solution.py:66
  214.2 2.1 fusion.44
  216.3 6.7 %dynamic_update_slice.26 = f32[1,2,2048,512]{3,2,1,0:T(8,128)} dynamic-update-slice(f32[1,2,2048,512]{3,2,1,0:T(8,128)} %dynamic_update_slice.25, f32[1,2,256,256]{3,2,1,0:T(8,128)} %fusion.44, s32[]{:T(128)} %constant.98.clone.1, s32[]{:T(128)} %constant.98.clone.1, s32[]{:T(128)S(6)} %select_n.259, s32[]{:T(128)S(6)} %select_n.260) | dynamic-update-slice | bytes 1048580 | tf_op jit(solution)/shard_map/dynamic_update_slice | solution.py:66
  223.0 2.1 fusion.43
  225.2 6.6 %dynamic_update_slice.27 = f32[1,2,2048,512]{3,2,1,0:T(8,128)} dynamic-update-slice(f32[1,2,2048,512]{3,2,1,0:T(8,128)} %dynamic_update_slice.26, f32[1,2,256,256]{3,2,1,0:T(8,128)} %fusion.43, s32[]{:T(128)} %constant.98.clone.1, s32[]{:T(128)} %constant.98.clone.1, s32[]{:T(128)S(6)} %select_n.261, s32[]{:T(128)S(6)} %select_n.262) | dynamic-update-slice | bytes 1048580 | tf_op jit(solution)/shard_map/dynamic_update_slice | solution.py:66
  231.7 2.1 fusion.42
  233.9 6.7 %dynamic_update_slice.28 = f32[1,2,2048,512]{3,2,1,0:T(8,128)} dynamic-update-slice(f32[1,2,2048,512]{3,2,1,0:T(8,128)} %dynamic_update_slice.27, f32[1,2,256,256]{3,2,1,0:T(8,128)} %fusion.42, s32[]{:T(128)} %constant.98.clone.1, s32[]{:T(128)} %constant.98.clone.1, s32[]{:T(128)S(6)} %select_n.263, s32[]{:T(128)S(6)} %select_n.264) | dynamic-update-slice | bytes 1048580 | tf_op jit(solution)/shard_map/dynamic_update_slice | solution.py:66
  240.6 2.1 fusion.41
  242.8 6.6 %dynamic_update_slice.29 = f32[1,2,2048,512]{3,2,1,0:T(8,128)} dynamic-update-slice(f32[1,2,2048,512]{3,2,1,0:T(8,128)} %dynamic_update_slice.28, f32[1,2,256,256]{3,2,1,0:T(8,128)} %fusion.41, s32[]{:T(128)} %constant.98.clone.1, s32[]{:T(128)} %constant.98.clone.1, s32[]{:T(128)S(6)} %select_n.265, s32[]{:T(128)S(6)} %select_n.266) | dynamic-update-slice | bytes 1048580 | tf_op jit(solution)/shard_map/dynamic_update_slice | solution.py:66
  249.4 2.4 slice.346
  251.8 2.4 collective-permute-start.3
  254.2 48.0 %collective-permute-done.3 = bf16[1,2,2048,256]{3,2,1,0:T(8,128)(2,1)S(1)} collective-permute-done((bf16[1,2,2048,256]{3,2,1,0:T(8,128)(2,1)S(1)}, bf16[1,2,2048,256]{3,2,1,0:T(8,128)(2,1)S(1)}, u32[]{:S(2)}, u32[]{:S(2)}) %collective-permute-start.3) | collective-permute-done | bytes 2097184 | tf_op jit(solution)/shard_map/ppermute | solution.py:10
  302.2 4.9 %slice_add_fusion = f32[1,2,2048,256]{3,2,1,0:T(8,128)} fusion(f32[1,2,2048,512]{3,2,1,0:T(8,128)} %dynamic_update_slice.29, bf16[1,2,2048,256]{3,2,1,0:T(8,128)(2,1)S(1)} %collective-permute-done.3), kind=kLoop, calls=%fused_computation.54 | loop fusion | flops 2097152 | bytes 10485760 | tf_op jit(solution)/shard_map/add | solution.py:165
  (68 shorter events, 19.5 us)
Async XLA Ops:
  0.0 30.6 %copy-start = (f32[1,8,256,256]{3,2,1,0:T(8,128)S(1)}, f32[1,8,256,256]{3,2,1,0:T(8,128)}, u32[]{:S(2)}) copy-start(f32[1,8,256,256]{3,2,1,0:T(8,128)} %param.15) | copy-start | bytes 6291460
  0.0 7.9 %copy-start.9 = (s32[1,6]{1,0:T(1,128)S(1)}, s32[1,6]{1,0:T(1,128)}, u32[]{:S(2)}) copy-start(s32[1,6]{1,0:T(1,128)} %param.17) | copy-start | bytes 76
  0.0 7.9 %copy-start.7 = (s32[1,8]{1,0:T(1,128)S(1)}, s32[1,8]{1,0:T(1,128)}, u32[]{:S(2)}) copy-start(s32[1,8]{1,0:T(1,128)} %param.18) | copy-start | bytes 100
  0.0 7.9 %copy-start.8 = (s32[1,8]{1,0:T(1,128)S(1)}, s32[1,8]{1,0:T(1,128)}, u32[]{:S(2)}) copy-start(s32[1,8]{1,0:T(1,128)} %param.19) | copy-start | bytes 100
  3.9 48.7 %collective-permute-start.2 = (bf16[1,2,2048,256]{3,2,1,0:T(8,128)(2,1)}, bf16[1,2,2048,256]{3,2,1,0:T(8,128)(2,1)}, u32[]{:S(2)}, u32[]{:S(2)}) collective-permute-start(bf16[1,2,2048,256]{3,2,1,0:T(8,128)(2,1)} %convert_element_type.165), channel_id=1, source_target_pairs={{1,0},{2,1},{3,2},{4,3},{5,4},{6,5},{7,6},{8,7},{9,8},{10,9},{11,1... | collective-permute-start | bytes 6291464 | tf_op jit(solution)/shard_map/ppermute | solution.py:10
  27.0 1.0 copy-start.6
  29.8 2.6 copy-start.4
  40.8 13.8 %copy-start.3 = (f32[1,2,2048,256]{3,2,1,0:T(8,128)S(1)}, f32[1,2,2048,256]{3,2,1,0:T(8,128)}, u32[]{:S(2)}) copy-start(f32[1,2,2048,256]{3,2,1,0:T(8,128)} %param.12) | copy-start | bytes 12582916
  102.7 5.9 %collective-permute-start = (bf16[6,2,256,256]{2,3,1,0:T(8,128)(2,1)}, bf16[6,2,256,256]{2,3,1,0:T(8,128)(2,1)S(1)}, u32[]{:S(2)}, u32[]{:S(2)}) collective-permute-start(bf16[6,2,256,256]{2,3,1,0:T(8,128)(2,1)} %get-tuple-element.947), channel_id=1, source_target_pairs={{0,16},{1,17},{2,18},{3,19},{4,20},{5,21},{6,22},{7,23},{8,24},{9,... | collective-permute-start | bytes 4718600 | tf_op jit(solution)/shard_map/while/body/eval_jaxpr/ppermute | solution.py:10
  125.4 5.5 %collective-permute-start = (bf16[6,2,256,256]{2,3,1,0:T(8,128)(2,1)}, bf16[6,2,256,256]{2,3,1,0:T(8,128)(2,1)S(1)}, u32[]{:S(2)}, u32[]{:S(2)}) collective-permute-start(bf16[6,2,256,256]{2,3,1,0:T(8,128)(2,1)} %get-tuple-element.947), channel_id=1, source_target_pairs={{0,16},{1,17},{2,18},{3,19},{4,20},{5,21},{6,22},{7,23},{8,24},{9,... | collective-permute-start | bytes 4718600 | tf_op jit(solution)/shard_map/while/body/eval_jaxpr/ppermute | solution.py:10
  132.6 1.4 copy-start.5
  136.1 2.8 copy-start.2
  160.4 6.0 %collective-permute-start.1 = (bf16[6,2,256,256]{2,3,1,0:T(8,128)(2,1)}, bf16[6,2,256,256]{2,3,1,0:T(8,128)(2,1)}, u32[]{:S(2)}, u32[]{:S(2)}) collective-permute-start(bf16[6,2,256,256]{2,3,1,0:T(8,128)(2,1)} %pad_maximum_fusion.9), channel_id=1, source_target_pairs={{16,0},{17,1},{18,2},{19,3},{20,4},{21,5},{22,6},{23,7},{24,8},{25... | collective-permute-start | bytes 4718600 | tf_op jit(solution)/shard_map/while/body/eval_jaxpr/ppermute | solution.py:10
  184.2 7.1 %collective-permute-start.1 = (bf16[6,2,256,256]{2,3,1,0:T(8,128)(2,1)}, bf16[6,2,256,256]{2,3,1,0:T(8,128)(2,1)}, u32[]{:S(2)}, u32[]{:S(2)}) collective-permute-start(bf16[6,2,256,256]{2,3,1,0:T(8,128)(2,1)} %pad_maximum_fusion.9), channel_id=1, source_target_pairs={{16,0},{17,1},{18,2},{19,3},{20,4},{21,5},{22,6},{23,7},{24,8},{25... | collective-permute-start | bytes 4718600 | tf_op jit(solution)/shard_map/while/body/eval_jaxpr/ppermute | solution.py:10
  251.8 50.4 %collective-permute-start.3 = (bf16[1,2,2048,256]{3,2,1,0:T(8,128)(2,1)S(1)}, bf16[1,2,2048,256]{3,2,1,0:T(8,128)(2,1)S(1)}, u32[]{:S(2)}, u32[]{:S(2)}) collective-permute-start(bf16[1,2,2048,256]{3,2,1,0:T(8,128)(2,1)S(1)} %slice.346), channel_id=1, source_target_pairs={{0,1},{1,2},{2,3},{3,4},{4,5},{5,6},{6,7},{7,8},{8,9},{9,10},{10,1... | collective-permute-start | bytes 6291464 | tf_op jit(solution)/shard_map/ppermute | solution.py:10
  302.2 4.9 %copy-start.1 = (f32[1,8,256,256]{3,2,1,0:T(8,128)S(1)}, f32[1,8,256,256]{3,2,1,0:T(8,128)}, u32[]{:S(2)}) copy-start(f32[1,8,256,256]{3,2,1,0:T(8,128)} %param.15) | copy-start | bytes 6291460
where the time goes:
time: 310 us; the launch traced here: 307 us
  local copies, waits for them, and re-layouts  92.2 us (30%)
  other arithmetic  76.5 us (25%)
  waiting for transfers between devices  61.3 us (20%)
  matrix products  37.8 us (12%)
  between operations  23.3 us (8%)
  starting transfers between devices  15.8 us (5%)
    ppermute x6, waiting for transfers between devices, from_behind(): lax.ppermute(value, axis, [(source, source + steps) for source in range(f...  61.3 us
    dynamic_update_slice x6, local copies, waits for them, and re-layouts, deposit(): lax.dynamic_update_slice(canvas, current + pieces[slot_index], corner)  39.8 us
    dot_general x8, matrix products, transform(): jnp.einsum('cdkn,bcnm->bdkm', matrix, halfway.astype(jnp.bfloat16), prefe...  37.8 us
    gather x18, local copies, waits for them, and re-layouts  23.6 us
    another operation x10, other arithmetic  17.8 us
    ppermute x6, starting transfers between devices, from_behind(): lax.ppermute(value, axis, [(source, source + steps) for source in range(f...  15.8 us
    unnamed x25, local copies, waits for them, and re-layouts  10.8 us
    add x5, other arithmetic, deposit(): current + pieces[slot_index]  10.7 us
  transfers between devices with their start and end apart: 6, of which 4 were waited for; matrix products, arithmetic and copies ran while one was open for 8% of the time, Pallas kernels for 0%

commit v1 on v0

v1 whole, which is shorter than its diff:
```python
import functools

import jax
import jax.numpy as jnp
import ml_dtypes
import numpy as np
from jax import lax
from jax.experimental import pallas as pl
from jax.experimental.pallas import tpu as pltpu
from jax.sharding import PartitionSpec as P

F32 = jnp.float32
BF16 = jnp.bfloat16
EXTRA = 8
LIMIT = 48 * 1024 * 1024


def send(value, flip, steps):
    cores, count = lax.axis_size("cuts"), lax.axis_size("tile")
    first, last = max(0, -steps), min(count, count - steps)
    pairs = [
        (core * count + tile, (core ^ flip) * count + tile + steps)
        for core in range(cores)
        for tile in range(first, last)
    ]
    return lax.ppermute(value, ("cuts", "tile"), pairs)


def make_tables(length):
    index = np.arange(length, dtype=np.int32)
    product = index[:, None] * index[None, :] % length
    angle = product.astype(np.float32) * np.float32(2.0 * np.pi / length)
    scale = np.float32(length ** (-0.5))
    cosine = (np.cos(angle) * scale).astype(ml_dtypes.bfloat16)
    sine = (-np.sin(angle) * scale).astype(ml_dtypes.bfloat16)
    one = np.concatenate(
        [np.concatenate([cosine, sine], 1), np.concatenate([-sine, cosine], 1)], 0
    )
    two = np.concatenate(
        [np.concatenate([cosine, -sine], 1), np.concatenate([sine, cosine], 1)], 0
    )
    return jnp.asarray(one), jnp.asarray(two)


class Plan:
    def __init__(self, ref, slots, scan, width):
        assert slots == 6
        self.ref, self.slots, self.scan, self.width = ref, slots, scan, width
        live = ref[0]
        final = ref[1 + slots + 2 * scan] > 0
        self.live = live
        cols = [ref[1 + slots + scan + ref[1 + slot]] for slot in range(slots)]
        here = [(2 * pair < live) for pair in range(3)]
        fits = [
            final | (2 * pair + 1 >= live) | (cols[2 * pair] + cols[2 * pair + 1] <= width)
            for pair in range(3)
        ]
        is_a = [jnp.where(here[pair] & fits[pair], 1, 0) for pair in range(3)]
        is_b = [jnp.where(here[pair] & jnp.logical_not(fits[pair]), 1, 0) for pair in range(3)]
        count_a, count_b = sum(is_a), sum(is_b)

        def chosen(flags):
            first = jnp.where(flags[0] > 0, 0, jnp.where(flags[1] > 0, 1, 2))
            second = jnp.where((flags[0] > 0) & (flags[1] > 0), 1, 2)
            return first, second

        def bins(flags, count, spill):
            first, second = chosen(flags)
            lone = jnp.where(spill, 4, -1)
            return {
                (0, 0): jnp.where(count >= 1, 2 * first, lone),
                (1, 0): jnp.where(
                    count >= 2, 2 * second, jnp.where(count == 1, 2 * first + 1, jnp.where(spill, 5, -1))
                ),
                (0, 1): jnp.where(count >= 2, 2 * first + 1, -1),
                (1, 1): jnp.where(count >= 2, 2 * second + 1, -1),
            }

        self.bins = {
            "A": bins(is_a, count_a, count_b == 3),
            "B": bins(is_b, count_b, (count_a == 3) & jnp.logical_not(final)),
        }
        third = (count_a == 3) & final
        self.bins["A"][(0, 2)] = jnp.where(third, 4, -1)
        self.bins["A"][(1, 2)] = jnp.where(third, 5, -1)

    def item(self, kind, core, place):
        table = self.bins[kind]
        slot = jnp.where(core == 0, table[(0, place)], table[(1, place)])
        valid = (slot >= 0) & (slot < self.live)
        position = self.ref[1 + jnp.where(valid, slot, 0)]
        row = self.ref[1 + self.slots + position]
        col = self.ref[1 + self.slots + self.scan + position]
        return valid, position, row, col


def turn(value, amount, width):
    return pltpu.roll(value, lax.rem(amount, width), 1)


def rows_down(value, shift):
    span, width = value.shape
    tiles = value.reshape(span // EXTRA, EXTRA, width)
    rolled = pltpu.roll(tiles, lax.rem(EXTRA - shift, EXTRA), 1)
    row = lax.broadcasted_iota(jnp.int32, (span // EXTRA - 1, EXTRA, width), 1)
    moved = jnp.where(row < EXTRA - shift, rolled[:-1], rolled[1:])
    return moved.reshape(span - EXTRA, width)


def rows_up(value, shift):
    height, width = value.shape
    tiles = value.reshape(height // EXTRA, EXTRA, width)
    rolled = pltpu.roll(tiles, lax.rem(shift, EXTRA), 1)
    blank = jnp.zeros((1, EXTRA, width), value.dtype)
    row = lax.broadcasted_iota(jnp.int32, (height // EXTRA + 1, EXTRA, width), 1)
    moved = jnp.where(
        row >= shift, jnp.concatenate([rolled, blank], 0), jnp.concatenate([blank, rolled], 0)
    )
    return moved.reshape(height + EXTRA, width)


def columns(shape):
    return lax.broadcasted_iota(jnp.int32, shape, 1)


def window_copy(source, target, sem, row, height, span):
    start = jnp.minimum(row // EXTRA * EXTRA, height - span)
    start = pl.multiple_of(start, EXTRA)
    copy = pltpu.make_async_copy(source.at[0, :, pl.ds(start, span), :], target, sem)
    return copy, row - start


def pages_kernel(kind, sizes, idx_ref, own_ref, object_ref, *rest):
    slots, scan, width, height = sizes
    if kind == "B":
        intensity_ref, straight_ref, cross_ref, window, levels, sems, level_sems = rest
    else:
        straight_ref, cross_ref, window, sems = rest
    span = window.shape[2]
    core = own_ref[2 + slots + 2 * scan]
    plan = Plan(idx_ref, slots, scan, width)
    items, copies = [], []
    for group, owner in enumerate((core, 1 - core)):
        for place in range(2):
            entry = plan.item(kind, owner, place)
            copy, shift = window_copy(
                object_ref, window.at[2 * group + place], sems.at[2 * group + place], entry[2], height, span
            )
            copy.start()
            items.append(entry + (shift,))
            copies.append(copy)
    level_copies = []
    if kind == "B":
        for place in range(2):
            copy = pltpu.make_async_copy(
                intensity_ref.at[0, items[place][1]], levels.at[place], level_sems.at[place]
            )
            copy.start()
            level_copies.append(copy)
    lane = columns((width, width))
    for group, out_ref in enumerate((straight_ref, cross_ref)):
        live0, _, _, col0, shift0 = items[2 * group]
        live1, _, _, col1, shift1 = items[2 * group + 1]
        copies[2 * group].wait()
        copies[2 * group + 1].wait()
        if kind == "A":
            mask0 = live0 & (lane < col0)
            mask1 = live1 & (lane >= width - col1)
        else:
            mask0 = live0 & (lane >= col0)
            mask1 = live1 & (lane < width - col1)
        for plane in range(2):
            first = rows_down(window[2 * group, plane], shift0)
            second = turn(rows_down(window[2 * group + 1, plane], shift1), width - col1, width)
            page = jnp.where(mask0, first, jnp.where(mask1, second, 0.0))
            out_ref[plane] = page.astype(BF16)
    for place, copy in enumerate(level_copies):
        copy.wait()
        straight_ref[2 + place] = levels[place].astype(BF16)


def parts_kernel(kind, places, sizes, idx_ref, own_ref, object_ref, self_ref, swap_ref, window, sems):
    slots, scan, width, height = sizes
    span = window.shape[2]
    core = own_ref[2 + slots + 2 * scan]
    plan = Plan(idx_ref, slots, scan, width)
    items, copies = [], []
    for group, owner in enumerate((core, 1 - core)):
        for place in range(places):
            entry = plan.item(kind, owner, place)
            at = places * group + place
            copy, shift = window_copy(object_ref, window.at[at], sems.at[at], entry[2], height, span)
            copy.start()
            items.append(entry + (shift,))
            copies.append(copy)
    lane = columns((width, width))
    for group, out_ref in enumerate((self_ref, swap_ref)):
        for place in range(places):
            at = places * group + place
            _, _, _, col, shift = items[at]
            copies[at].wait()
            mask = lane < width - col if kind == "A" else lane >= width - col
            for plane in range(2):
                rolled = turn(rows_down(window[at, plane], shift), width - col, width)
                out_ref[place, plane] = jnp.where(mask, rolled, 0.0).astype(BF16)


def waves_kernel(kind, places, sizes, *refs):
    slots, scan, width, height = sizes
    (idx_ref, own_ref, straight_ref, cross_ref, self_ref, swap_ref, cs_ref, cs_other_ref, probe_ref,
     one_ref, two_ref) = refs[:11]
    rest = refs[11:]
    if kind == "A":
        intensity_ref, rest = rest[0], rest[1:]
    (back_straight, back_cross, out_self, out_swap, phase, patch, wave, grads, field, half, levels) = rest[:11]
    if kind == "A":
        level_sems = rest[11]
    core = own_ref[2 + slots + 2 * scan]
    other = 1 - core
    plan = Plan(idx_ref, slots, scan, width)
    lane = columns((width, width))
    phase[core] = cs_ref[...]
    phase[other] = cs_other_ref[...]

    def foreign_mask(col, in_tile):
        if kind == "A":
            return lane < col if in_tile else lane >= width - col
        return lane >= col if in_tile else lane < width - col

    def propagate(adjoint, which, finish):
        sign = -1.0 if adjoint else 1.0
        for item in range(2):
            product = jnp.dot(field[item], one_ref[...], preferred_element_type=F32)
            half[item, :width] = product[:, :width].astype(BF16)
            half[item, width:] = product[:, width:].astype(BF16)
        for item in range(2):
            spectrum = jnp.dot(two_ref[...], half[item], preferred_element_type=F32)
            real, imag = spectrum[:width], spectrum[width:]
            cosine, sine = phase[which, 0], sign * phase[which, 1]
            field[item, :, :width] = (real * cosine - imag * sine).astype(BF16)
            field[item, :, width:] = (real * sine + imag * cosine).astype(BF16)
        for item in range(2):
            product = jnp.dot(field[item], two_ref[...], preferred_element_type=F32)
            half[item, :width] = product[:, :width].astype(BF16)
            half[item, width:] = product[:, width:].astype(BF16)
        for item in range(2):
            result = jnp.dot(one_ref[...], half[item], preferred_element_type=F32)
            finish(item, result[:width], result[width:])

    def put(item, real, imag):
        field[item, :, :width] = real.astype(BF16)
        field[item, :, width:] = imag.astype(BF16)

    def one_pair(turn_index, _):
        entries = []
        for item in range(2):
            entry = plan.item(kind, core, item)
            if places > 2:
                late = plan.item(kind, core, 2)
                entry = tuple(jnp.where(turn_index > 0, b, a) for a, b in zip(entry, late))
            entries.append(entry)
        at = [jnp.minimum(2 * turn_index + item, places - 1) for item in range(2)]
        if kind == "A":
            copies = []
            for item in range(2):
                copy = pltpu.make_async_copy(
                    intensity_ref.at[0, entries[item][1]], levels.at[item], level_sems.at[item]
                )
                copy.start()
                copies.append(copy)
        for item in range(2):
            col = entries[item][3]
            mask = foreign_mask(col, item == 0)
            for source, part_ref, page_ref in ((core, self_ref, straight_ref), (other, swap_ref, cross_ref)):
                for plane in range(2):
                    page = jnp.where(mask, page_ref[plane].astype(F32), 0.0)
                    if item == 0:
                        page = turn(page, width - col, width)
                    own = part_ref[at[item], plane].astype(F32)
                    patch[source, item, plane] = (page + own).astype(BF16)
        for item in range(2):
            left_re, left_im = probe_ref[0], probe_ref[1]
            right_re, right_im = patch[0, item, 0].astype(F32), patch[0, item, 1].astype(F32)
            put(item, left_re * right_re - left_im * right_im, left_re * right_im + left_im * right_re)

        def after_first(item, real, imag):
            real, imag = real.astype(BF16), imag.astype(BF16)
            wave[item, 0] = real
            wave[item, 1] = imag
            real, imag = real.astype(F32), imag.astype(F32)
            right_re, right_im = patch[1, item, 0].astype(F32), patch[1, item, 1].astype(F32)
            put(item, real * right_re - imag * right_im, real * right_im + imag * right_re)

        propagate(False, 0, after_first)
        if kind == "A":
            for copy in copies:
                copy.wait()

        def after_second(item, real, imag):
            real, imag = real.astype(BF16).astype(F32), imag.astype(BF16).astype(F32)
            if kind == "A":
                level = levels[item]
            else:
                level = straight_ref[2 + item].astype(F32)
            gain = 2.0 * (real * real + imag * imag - level)
            gain = jnp.where(entries[item][0], gain, 0.0)
            put(item, gain * real, gain * imag)

        propagate(False, 1, after_second)

        def before_second(item, real, imag):
            left_re, left_im = wave[item, 0].astype(F32), wave[item, 1].astype(F32)
            grads[1, item, 0] = (left_re * real + left_im * imag).astype(BF16)
            grads[1, item, 1] = (left_re * imag - left_im * real).astype(BF16)
            left_re, left_im = patch[1, item, 0].astype(F32), patch[1, item, 1].astype(F32)
            put(item, left_re * real + left_im * imag, left_re * imag - left_im * real)

        propagate(True, 1, before_second)

        def before_first(item, real, imag):
            left_re, left_im = probe_ref[0], probe_ref[1]
            grads[0, item, 0] = (left_re * real + left_im * imag).astype(BF16)
            grads[0, item, 1] = (left_re * imag - left_im * real).astype(BF16)

        propagate(True, 0, before_first)
        for item in range(2):
            out_self[at[item]] = grads[core, item]
            out_swap[at[item]] = grads[other, item]

        @pl.when(turn_index == 0)
        def _():
            live0, _, _, col0 = entries[0]
            live1, _, _, col1 = entries[1]
            mask0 = live0 & foreign_mask(col0, True)
            mask1 = live1 & foreign_mask(col1, False)
            for source, out_ref in ((core, back_straight), (other, back_cross)):
                for plane in range(2):
                    first = turn(grads[source, 0, plane].astype(F32), col0, width)
                    second = grads[source, 1, plane].astype(F32)
                    page = jnp.where(mask0, first, jnp.where(mask1, second, 0.0))
                    out_ref[plane] = page.astype(BF16)

        return 0

    if places > 2:
        turns = jnp.where(plan.item(kind, core, 2)[0], 2, 1)
        lax.fori_loop(0, turns, one_pair, 0)
    else:
        one_pair(jnp.int32(0), 0)


def deposit_kernel(places, sizes, *refs):
    slots, scan, width, height = sizes
    (own_ref, behind_ref, a_self, a_swap, b_self, b_swap, b_back, b_back_cross, a_back, a_back_cross,
     out_ref) = refs
    core = own_ref[2 + slots + 2 * scan]
    other = 1 - core
    own = Plan(own_ref, slots, scan, width)
    behind = Plan(behind_ref, slots, scan, width)
    lane = columns((width, width))
    out_ref[...] = jnp.zeros_like(out_ref)

    def add(entry, in_next, pieces, in_tile):
        live, _, row, col = entry

        @pl.when(live)
        def _():
            mask = lane < col if in_next else lane >= col
            for plane in range(2):
                piece = pieces(plane).astype(F32)
                if not in_tile:
                    piece = turn(piece, col, width)
                start = pl.multiple_of(jnp.minimum(row // EXTRA * EXTRA, height - width - EXTRA), EXTRA)
                rows = pl.ds(start, width + EXTRA)
                moved = rows_up(jnp.where(mask, piece, 0.0), row - start)
                out_ref[0, plane, rows, :] = out_ref[0, plane, rows, :] + moved

    for owner, ref in ((core, b_self), (other, b_swap)):
        for place in range(2):
            add(behind.item("B", owner, place), True, lambda plane: ref[place, plane], False)
    for owner, ref in ((core, a_self), (other, a_swap)):
        for place in range(places):
            add(own.item("A", owner, place), False, lambda plane: ref[place, plane], False)
    for owner, ref in ((core, b_back), (other, b_back_cross)):
        for place in range(2):
            add(own.item("B", owner, place), False, lambda plane: ref[plane], place == 0)
    for owner, ref in ((core, a_back), (other, a_back_cross)):
        for place in range(2):
            add(behind.item("A", owner, place), True, lambda plane: ref[plane], place == 0)


def on_device(
    object_slices, probe_field, slice_phase, intensity, counts, chosen, row_offset, column_offset
):
    height, breadth = object_slices.shape[2:]
    width = probe_field.shape[-1]
    assert breadth == width and object_slices.shape[0] == 1
    slots, scan = chosen.shape[1], row_offset.shape[1]
    sizes = (slots, scan, width, height)
    places = slots // 2
    span = width + EXTRA
    core = lax.axis_index("cuts")
    final = lax.axis_index("tile") == lax.axis_size("tile") - 1
    own = jnp.concatenate(
        [
            counts,
            chosen[0],
            row_offset[0],
            column_offset[0],
            jnp.stack([final.astype(jnp.int32), core.astype(jnp.int32)]),
        ]
    )
    behind = send(own, 0, 1)
    turned = jnp.stack([jnp.cos(slice_phase[0]), jnp.sin(slice_phase[0])])
    turned_other = send(turned, 1, 0)
    one, two = make_tables(width)

    smem = pl.BlockSpec(memory_space=pltpu.SMEM)
    vmem = pl.BlockSpec(memory_space=pltpu.VMEM)
    anywhere = pl.BlockSpec(memory_space=pl.ANY)
    params = pltpu.CompilerParams(vmem_limit_bytes=LIMIT)
    window = lambda count: pltpu.VMEM((count, 2, span, width), F32)
    planes = lambda *lead: jax.ShapeDtypeStruct((*lead, width, width), BF16)
    cost = lambda flops, moved: pl.CostEstimate(flops=flops, bytes_accessed=moved, transcendentals=0)

    def pages(kind, idx):
        first = 4 if kind == "B" else 2
        extra = [intensity] if kind == "B" else []
        scratch = [window(4)]
        if kind == "B":
            scratch += [pltpu.VMEM((2, width, width), F32)]
        scratch += [pltpu.SemaphoreType.DMA((4,))]
        if kind == "B":
            scratch += [pltpu.SemaphoreType.DMA((2,))]
        return pl.pallas_call(
            functools.partial(pages_kernel, kind, sizes),
            out_shape=[planes(first), planes(2)],
            in_specs=[smem, smem, anywhere] + [anywhere] * len(extra),
            out_specs=[vmem, vmem],
            scratch_shapes=scratch,
            compiler_params=params,
            cost_estimate=cost(0, 6 * 1024 * 1024),
            name="pages_" + kind.lower(),
        )(idx, own, object_slices, *extra)

    def parts(kind, idx, count):
        return pl.pallas_call(
            functools.partial(parts_kernel, kind, count, sizes),
            out_shape=[planes(count, 2), planes(count, 2)],
            in_specs=[smem, smem, anywhere],
            out_specs=[vmem, vmem],
            scratch_shapes=[window(2 * count), pltpu.SemaphoreType.DMA((2 * count,))],
            compiler_params=params,
            cost_estimate=cost(0, 6 * 1024 * 1024),
            name="parts_" + kind.lower(),
        )(idx, own, object_slices)

    def waves(kind, idx, count, straight, cross, part_self, part_swap):
        scratch = [
            pltpu.VMEM((2, 2, width, width), F32),
            pltpu.VMEM((2, 2, 2, width, width), BF16),
            pltpu.VMEM((2, 2, width, width), BF16),
            pltpu.VMEM((2, 2, 2, width, width), BF16),
            pltpu.VMEM((2, width, 2 * width), BF16),
            pltpu.VMEM((2, 2 * width, width), BF16),
            pltpu.VMEM((2, width, width), F32),
        ]
        operands = [idx, own, straight, cross, part_self, part_swap, turned, turned_other, probe_field, one, two]
        specs = [smem, smem] + [vmem] * 9
        if kind == "A":
            operands.append(intensity)
            specs.append(anywhere)
            scratch.append(pltpu.SemaphoreType.DMA((2,)))
        return pl.pallas_call(
            functools.partial(waves_kernel, kind, count, sizes),
            out_shape=[planes(2), planes(2), planes(count, 2), planes(count, 2)],
            in_specs=specs,
            out_specs=[vmem] * 4,
            scratch_shapes=scratch,
            compiler_params=params,
            cost_estimate=cost(32 * 8 * width ** 3 * 2, 8 * 1024 * 1024),
            name="waves_" + kind.lower(),
        )(*operands)

    b_straight, b_cross = pages("B", own)
    b_straight, b_cross = send(b_straight, 0, 1), send(b_cross, 1, 1)
    a_part, a_part_swap = parts("A", own, places)
    a_part_swap = send(a_part_swap, 1, 0)
    a_straight, a_cross = pages("A", behind)
    a_straight, a_cross = send(a_straight, 0, -1), send(a_cross, 1, -1)
    b_part, b_part_swap = parts("B", behind, 2)
    b_part_swap = send(b_part_swap, 1, 0)
    b_back, b_back_cross, b_self, b_swap = waves("B", behind, 2, b_straight, b_cross, b_part, b_part_swap)
    b_back, b_back_cross = send(b_back, 0, -1), send(b_back_cross, 1, -1)
    b_swap = send(b_swap, 1, 0)
    a_back, a_back_cross, a_self, a_swap = waves("A", own, places, a_straight, a_cross, a_part, a_part_swap)
    a_back, a_back_cross = send(a_back, 0, 1), send(a_back_cross, 1, 1)
    a_swap = send(a_swap, 1, 0)
    return pl.pallas_call(
        functools.partial(deposit_kernel, places, sizes),
        out_shape=jax.ShapeDtypeStruct(object_slices.shape, F32),
        in_specs=[smem, smem] + [vmem] * 8,
        out_specs=vmem,
        compiler_params=params,
        cost_estimate=cost(0, 10 * 1024 * 1024),
        name="deposit",
    )(own, behind, a_self, a_swap, b_self, b_swap, b_back, b_back_cross, a_back, a_back_cross)


def solution(mesh):
    return jax.shard_map(
        on_device,
        mesh=mesh,
        in_specs=(
            P("cuts", None, None, "tile"),
            P(),
            P("cuts", None, None),
            P("tile", None, None, None),
            P("tile"),
            P("tile", None),
            P("tile", None),
            P("tile", None),
        ),
        out_specs=P("cuts", None, None, "tile"),
        check_vma=False,
    )
```

time: 310 us -> 99.1 us (0.32)
  the two profiles are of different devices: /device:TPU:17 before, /device:TPU:13 now
where the time goes in v1:
time: 99.1 us; the launch traced here: 98.4 us
  waiting for transfers between devices  37.5 us (38%)
  starting transfers between devices  27.8 us (28%)
  Pallas kernels  26.5 us (27%)
  local copies, waits for them, and re-layouts  5.71 us (6%)
    ppermute x14, waiting for transfers between devices, send(): return lax.ppermute(value, ('cuts', 'tile'), pairs)  37.5 us
    ppermute x14, starting transfers between devices, send(): return lax.ppermute(value, ('cuts', 'tile'), pairs)  27.8 us
    pallas_call x2, Pallas kernels, waves(): pl.pallas_call(functools.partial(waves_kernel, kind, count, sizes), out_s...  14.7 us
    pallas_call x1, Pallas kernels, on_device(): pl.pallas_call(functools.partial(deposit_kernel, places, sizes), out_shap...  4.24 us
    pallas_call x2, Pallas kernels, pages(): pl.pallas_call(functools.partial(pages_kernel, kind, sizes), out_shape=[p...  3.98 us
    pallas_call x2, Pallas kernels, parts(): pl.pallas_call(functools.partial(parts_kernel, kind, count, sizes), out_s...  3.59 us
    unnamed x16, local copies, waits for them, and re-layouts  3.1 us
  transfers between devices with their start and end apart: 14, of which 5 were waited for; matrix products, arithmetic and copies ran while one was open for 2% of the time, Pallas kernels for 21%

profile of v1, /device:TPU:13, one launch (start us, length us, event | category | flops | bytes accessed | tf_op | source)
XLA Modules:
  0.0 98.4 jit_solution(10454536013220332715)
XLA Ops:
  0.7 0.8 concatenate.3.own_ref.idx_ref.refs_0_.refs_1_
  1.4 0.0 copy-start
  1.4 2.2 %copy-done = f32[1,2,2048,256]{3,2,1,0:T(8,128)S(1)} copy-done((f32[1,2,2048,256]{3,2,1,0:T(8,128)S(1)}, f32[1,2,2048,256]{3,2,1,0:T(8,128)}, u32[]{:S(2)}) %copy-start) | copy-done | bytes 4194328
  3.6 0.0 copy-start.1
  3.6 0.0 copy-start.3
  3.6 2.0 %parts_a.1 = (bf16[3,2,256,256]{3,2,1,0:T(8,128)(2,1)S(1)}, bf16[3,2,256,256]{3,2,1,0:T(8,128)(2,1)S(1)}) custom-call(s32[25]{0:T(128)S(1)} %concatenate.3.own_ref.idx_ref.refs_0_.refs_1_, s32[25]{0:T(128)S(1)} %concatenate.3.own_ref.idx_ref.refs_0_.refs_1_, f32[1,2,2048,256]{3,2,1,0:T(8,128)S(1)} %copy-done), custom_call_target="tpu_custom_call" | custom-call | bytes 6291456 | tf_op jit(solution)/shard_map/parts_a/pallas_call | solution.py:447
  5.7 0.7 collective-permute-start.3
  6.4 1.9 %fusion = (f32[1,256,256]{2,1,0:T(8,128)S(1)}, f32[1,256,256]{2,1,0:T(8,128)S(1)}) fusion(f32[1,256,256]{2,1,0:T(8,128)} %param.12), kind=kLoop, calls=%fused_computation.1 | loop fusion | bytes 786432 | tf_op jit(solution)/shard_map/cos | solution.py:414
  8.3 0.1 collective-permute-start.4
  8.4 3.1 %collective-permute-start = (s32[25]{0:T(128)S(1)}, s32[25]{0:T(128)S(1)}, u32[]{:S(2)}, u32[]{:S(2)}) collective-permute-start(s32[25]{0:T(128)S(1)} %concatenate.3.own_ref.idx_ref.refs_0_.refs_1_), channel_id=1, source_target_pairs={{0,1},{1,2},{2,3},{3,4},{4,5},{5,6},{6,7},{7,8},{8,9},{9,10},{10,1... | collective-permute-start | bytes 308 | tf_op jit(solution)/shard_map/ppermute | solution.py:26
  11.5 2.1 %collective-permute-done.idx_ref.refs_0_.refs_1_ = s32[25]{0:T(128)S(1)} collective-permute-done((s32[25]{0:T(128)S(1)}, s32[25]{0:T(128)S(1)}, u32[]{:S(2)}, u32[]{:S(2)}) %collective-permute-start) | collective-permute-done | bytes 132 | tf_op jit(solution)/shard_map/ppermute | solution.py:26
  13.6 0.0 copy-done.1
  13.6 1.3 %pages_a.1 = (bf16[2,256,256]{2,1,0:T(8,128)(2,1)S(1)}, bf16[2,256,256]{2,1,0:T(8,128)(2,1)S(1)}) custom-call(s32[25]{0:T(128)S(1)} %collective-permute-done.idx_ref.refs_0_.refs_1_, s32[25]{0:T(128)S(1)} %concatenate.3.own_ref.idx_ref.refs_0_.refs_1_, f32[1,2,2048,256]{3,2,1,0:T(8,128)S(1)} %copy-done.1), custom_call_target="tpu_custom_call" | custom-call | bytes 6291456 | tf_op jit(solution)/shard_map/pages_a/pallas_call | solution.py:435
  14.9 0.0 copy-start.2
  14.9 2.4 %collective-permute-start.1 = (bf16[2,256,256]{2,1,0:T(8,128)(2,1)S(1)}, bf16[2,256,256]{2,1,0:T(8,128)(2,1)S(1)}, u32[]{:S(2)}, u32[]{:S(2)}) collective-permute-start(bf16[2,256,256]{2,1,0:T(8,128)(2,1)S(1)} %get-tuple-element.21), channel_id=1, source_target_pairs={{1,0},{2,1},{3,2},{4,3},{5,4},{6,5},{7,6},{8,7},{9,8},{10,9},{11,1... | collective-permute-start | bytes 786440 | tf_op jit(solution)/shard_map/ppermute | solution.py:26
  17.3 0.0 copy-start.4
  17.3 0.0 copy-start.5
  17.4 0.0 copy-start.6
  17.4 5.9 %collective-permute-start.2 = (bf16[2,256,256]{2,1,0:T(8,128)(2,1)S(1)}, bf16[2,256,256]{2,1,0:T(8,128)(2,1)S(1)}, u32[]{:S(2)}, u32[]{:S(2)}) collective-permute-start(bf16[2,256,256]{2,1,0:T(8,128)(2,1)S(1)} %get-tuple-element.22), channel_id=1, source_target_pairs={{1,16},{2,17},{3,18},{4,19},{5,20},{6,21},{7,22},{8,23},{9,24},{10... | collective-permute-start | bytes 786440 | tf_op jit(solution)/shard_map/ppermute | solution.py:26
  23.3 0.0 copy-done.3
  23.3 2.7 %pages_b.1 = (bf16[4,256,256]{2,1,0:T(8,128)(2,1)S(1)}, bf16[2,256,256]{2,1,0:T(8,128)(2,1)S(1)}) custom-call(s32[25]{0:T(128)S(1)} %concatenate.3.own_ref.idx_ref.refs_0_.refs_1_, s32[25]{0:T(128)S(1)} %concatenate.3.own_ref.idx_ref.refs_0_.refs_1_, f32[1,2,2048,256]{3,2,1,0:T(8,128)} %object_ref.7, f32[1,8,256,256]{3,2,1,0:T(8,128)S(1)} %copy-done.3), custom_call_target="tpu_custom_call" | custom-call | bytes 6291456 | tf_op jit(solution)/shard_map/pages_b/pallas_call | solution.py:435
  26.0 1.9 %collective-permute-start.7 = (bf16[2,256,256]{2,1,0:T(8,128)(2,1)S(1)}, bf16[2,256,256]{2,1,0:T(8,128)(2,1)S(1)}, u32[]{:S(2)}, u32[]{:S(2)}) collective-permute-start(bf16[2,256,256]{2,1,0:T(8,128)(2,1)S(1)} %get-tuple-element.28), channel_id=1, source_target_pairs={{0,17},{1,18},{2,19},{3,20},{4,21},{5,22},{6,23},{7,24},{8,25},{9,... | collective-permute-start | bytes 786440 | tf_op jit(solution)/shard_map/ppermute | solution.py:26
  27.9 0.0 copy-done.2
  27.9 1.5 %parts_b.1 = (bf16[2,2,256,256]{3,2,1,0:T(8,128)(2,1)S(1)}, bf16[2,2,256,256]{3,2,1,0:T(8,128)(2,1)S(1)}) custom-call(s32[25]{0:T(128)S(1)} %collective-permute-done.idx_ref.refs_0_.refs_1_, s32[25]{0:T(128)S(1)} %concatenate.3.own_ref.idx_ref.refs_0_.refs_1_, f32[1,2,2048,256]{3,2,1,0:T(8,128)S(1)} %copy-done.2), custom_call_target="tpu_custom_call" | custom-call | bytes 6291456 | tf_op jit(solution)/shard_map/parts_b/pallas_call | solution.py:447
  29.5 0.0 collective-permute-done.1.refs_2_
  29.5 3.2 %collective-permute-start.6 = (bf16[4,256,256]{2,1,0:T(8,128)(2,1)S(1)}, bf16[4,256,256]{2,1,0:T(8,128)(2,1)S(1)}, u32[]{:S(2)}, u32[]{:S(2)}) collective-permute-start(bf16[4,256,256]{2,1,0:T(8,128)(2,1)S(1)} %get-tuple-element.27), channel_id=1, source_target_pairs={{0,1},{1,2},{2,3},{3,4},{4,5},{5,6},{6,7},{7,8},{8,9},{9,10},{10,1... | collective-permute-start | bytes 1572872 | tf_op jit(solution)/shard_map/ppermute | solution.py:26
  32.7 15.2 %collective-permute-done.2.refs_3_ = bf16[2,256,256]{2,1,0:T(8,128)(2,1)S(1)} collective-permute-done((bf16[2,256,256]{2,1,0:T(8,128)(2,1)S(1)}, bf16[2,256,256]{2,1,0:T(8,128)(2,1)S(1)}, u32[]{:S(2)}, u32[]{:S(2)}) %collective-permute-start.2) | collective-permute-done | bytes 262176 | tf_op jit(solution)/shard_map/ppermute | solution.py:26
  47.9 0.0 collective-permute-start.8
  47.9 0.0 collective-permute-done.4.refs_7_
  47.9 0.0 collective-permute-done.3.refs_5_
  47.9 0.0 copy-start.7
  47.9 0.9 copy-done.7
  48.7 0.0 copy-done.4
  48.8 0.0 copy-done.5
  48.8 0.0 copy-done.6
  48.8 7.8 %waves_a.1 = (bf16[2,256,256]{2,1,0:T(8,128)(2,1)S(1)}, bf16[2,256,256]{2,1,0:T(8,128)(2,1)S(1)}, bf16[3,2,256,256]{3,2,1,0:T(8,128)(2,1)S(1)}, bf16[3,2,256,256]{3,2,1,0:T(8,128)(2,1)S(1)}) custom-call(s32[25]{0:T(128)S(1)} %concatenate.3.own_ref.idx_ref.refs_0_.refs_1_, s32[25]{0:T(128)S(1)} %concatenate.3.own_ref.idx_ref.refs_0_.refs_1_, ...), custom_call_target="tpu_custom_call" | custom-call | flops 8589934592 | bytes 8388608 | tf_op jit(solution)/shard_map/waves_a/pallas_call | solution.py:474
  56.6 0.6 collective-permute-start.5
  57.1 0.0 collective-permute-done.7.refs_3_
  57.1 0.0 collective-permute-done.6.refs_2_
  57.1 0.0 collective-permute-done.8.refs_5_
  57.1 6.9 %waves_b.1 = (bf16[2,256,256]{2,1,0:T(8,128)(2,1)S(1)}, bf16[2,256,256]{2,1,0:T(8,128)(2,1)S(1)}, bf16[2,2,256,256]{3,2,1,0:T(8,128)(2,1)S(1)}, bf16[2,2,256,256]{3,2,1,0:T(8,128)(2,1)S(1)}) custom-call(s32[25]{0:T(128)S(1)} %collective-permute-done.idx_ref.refs_0_.refs_1_, s32[25]{0:T(128)S(1)} %concatenate.3.own_ref.idx_ref.refs_0_.refs_1_, ...), custom_call_target="tpu_custom_call" | custom-call | flops 8589934592 | bytes 8388608 | tf_op jit(solution)/shard_map/waves_b/pallas_call | solution.py:474
  64.0 2.1 %collective-permute-start.10 = (bf16[2,256,256]{2,1,0:T(8,128)(2,1)S(1)}, bf16[2,256,256]{2,1,0:T(8,128)(2,1)S(1)}, u32[]{:S(2)}, u32[]{:S(2)}) collective-permute-start(bf16[2,256,256]{2,1,0:T(8,128)(2,1)S(1)} %get-tuple-element.33), channel_id=1, source_target_pairs={{1,0},{2,1},{3,2},{4,3},{5,4},{6,5},{7,6},{8,7},{9,8},{10,9},{11,1... | collective-permute-start | bytes 786440 | tf_op jit(solution)/shard_map/ppermute | solution.py:26
  66.2 0.1 collective-permute-start.9
  66.3 1.9 %collective-permute-start.11 = (bf16[2,256,256]{2,1,0:T(8,128)(2,1)S(1)}, bf16[2,256,256]{2,1,0:T(8,128)(2,1)S(1)}, u32[]{:S(2)}, u32[]{:S(2)}) collective-permute-start(bf16[2,256,256]{2,1,0:T(8,128)(2,1)S(1)} %get-tuple-element.34), channel_id=1, source_target_pairs={{1,16},{2,17},{3,18},{4,19},{5,20},{6,21},{7,22},{8,23},{9,24},{10... | collective-permute-start | bytes 786440 | tf_op jit(solution)/shard_map/ppermute | solution.py:26
  68.2 3.8 %collective-permute-start.12 = (bf16[2,256,256]{2,1,0:T(8,128)(2,1)S(1)}, bf16[2,256,256]{2,1,0:T(8,128)(2,1)S(1)}, u32[]{:S(2)}, u32[]{:S(2)}) collective-permute-start(bf16[2,256,256]{2,1,0:T(8,128)(2,1)S(1)} %get-tuple-element.35), channel_id=1, source_target_pairs={{0,1},{1,2},{2,3},{3,4},{4,5},{5,6},{6,7},{7,8},{8,9},{9,10},{10,1... | collective-permute-start | bytes 786440 | tf_op jit(solution)/shard_map/ppermute | solution.py:26
  72.0 10.9 %collective-permute-done.10.refs_6_ = bf16[2,256,256]{2,1,0:T(8,128)(2,1)S(1)} collective-permute-done((bf16[2,256,256]{2,1,0:T(8,128)(2,1)S(1)}, bf16[2,256,256]{2,1,0:T(8,128)(2,1)S(1)}, u32[]{:S(2)}, u32[]{:S(2)}) %collective-permute-start.10) | collective-permute-done | bytes 262176 | tf_op jit(solution)/shard_map/ppermute | solution.py:26
  82.9 1.9 %collective-permute-start.13 = (bf16[2,256,256]{2,1,0:T(8,128)(2,1)S(1)}, bf16[2,256,256]{2,1,0:T(8,128)(2,1)S(1)}, u32[]{:S(2)}, u32[]{:S(2)}) collective-permute-start(bf16[2,256,256]{2,1,0:T(8,128)(2,1)S(1)} %get-tuple-element.36), channel_id=1, source_target_pairs={{0,17},{1,18},{2,19},{3,20},{4,21},{5,22},{6,23},{7,24},{8,25},{9,... | collective-permute-start | bytes 786440 | tf_op jit(solution)/shard_map/ppermute | solution.py:26
  84.8 3.7 %collective-permute-done.11.refs_7_ = bf16[2,256,256]{2,1,0:T(8,128)(2,1)S(1)} collective-permute-done((bf16[2,256,256]{2,1,0:T(8,128)(2,1)S(1)}, bf16[2,256,256]{2,1,0:T(8,128)(2,1)S(1)}, u32[]{:S(2)}, u32[]{:S(2)}) %collective-permute-start.11) | collective-permute-done | bytes 262176 | tf_op jit(solution)/shard_map/ppermute | solution.py:26
  88.5 0.0 collective-permute-done.12.refs_8_
  88.5 5.6 %collective-permute-done.13.refs_9_ = bf16[2,256,256]{2,1,0:T(8,128)(2,1)S(1)} collective-permute-done((bf16[2,256,256]{2,1,0:T(8,128)(2,1)S(1)}, bf16[2,256,256]{2,1,0:T(8,128)(2,1)S(1)}, u32[]{:S(2)}, u32[]{:S(2)}) %collective-permute-start.13) | collective-permute-done | bytes 262176 | tf_op jit(solution)/shard_map/ppermute | solution.py:26
  94.2 0.0 collective-permute-done.9.refs_5_
  94.2 0.0 collective-permute-done.5.refs_3_
  94.2 4.2 %deposit.1 = f32[1,2,2048,256]{3,2,1,0:T(8,128)} custom-call(s32[25]{0:T(128)S(1)} %concatenate.3.own_ref.idx_ref.refs_0_.refs_1_, s32[25]{0:T(128)S(1)} %collective-permute-done.idx_ref.refs_0_.refs_1_, bf16[3,2,256,256]{3,2,1,0:T(8,128)(2,1)S(1)} %get-tuple-element.25.refs_2_, bf16[3,2,256,256]{3,2,1,0:T(8,128)(2,1)S(1)} %collective-permute-done.5.refs_3_, ...), custom_call_target="tpu_custom_call" | custom-call | bytes 10485760 | tf_op jit(solution)/shard_map/deposit/pallas_call | solution.py:499
  (1 shorter events, 0.0 us)
Async XLA Ops:
  1.4 2.2 %copy-start = (f32[1,2,2048,256]{3,2,1,0:T(8,128)S(1)}, f32[1,2,2048,256]{3,2,1,0:T(8,128)}, u32[]{:S(2)}) copy-start(f32[1,2,2048,256]{3,2,1,0:T(8,128)} %object_ref.7) | copy-start | bytes 12582916
  3.6 10.0 %copy-start.1 = (f32[1,2,2048,256]{3,2,1,0:T(8,128)S(1)}, f32[1,2,2048,256]{3,2,1,0:T(8,128)}, u32[]{:S(2)}) copy-start(f32[1,2,2048,256]{3,2,1,0:T(8,128)} %object_ref.7) | copy-start | bytes 12582916
  3.6 19.7 %copy-start.3 = (f32[1,8,256,256]{3,2,1,0:T(8,128)S(1)}, f32[1,8,256,256]{3,2,1,0:T(8,128)}, u32[]{:S(2)}) copy-start(f32[1,8,256,256]{3,2,1,0:T(8,128)} %rest_0_.1) | copy-start | bytes 6291460
  5.7 42.2 %collective-permute-start.3 = (bf16[3,2,256,256]{3,2,1,0:T(8,128)(2,1)S(1)}, bf16[3,2,256,256]{3,2,1,0:T(8,128)(2,1)S(1)}, u32[]{:S(2)}, u32[]{:S(2)}) collective-permute-start(bf16[3,2,256,256]{3,2,1,0:T(8,128)(2,1)S(1)} %get-tuple-element.24), channel_id=1, source_target_pairs={{0,16},{1,17},{2,18},{3,19},{4,20},{5,21},{6,22},{7,23},{8,24},{9,... | collective-permute-start | bytes 2359304 | tf_op jit(solution)/shard_map/ppermute | solution.py:26
  8.3 39.6 %collective-permute-start.4 = (f32[2,256,256]{2,1,0:T(8,128)S(1)}, f32[2,256,256]{2,1,0:T(8,128)S(1)}, u32[]{:S(2)}, u32[]{:S(2)}) collective-permute-start(f32[2,256,256]{2,1,0:T(8,128)S(1)} %pad_maximum_fusion.refs_6_), channel_id=1, source_target_pairs={{0,16},{1,17},{2,18},{3,19},{4,20},{5,21},{6,22},{7,23},{8,24},{9,... | collective-permute-start | bytes 1572872 | tf_op jit(solution)/shard_map/ppermute | solution.py:26
  8.4 5.2 %collective-permute-start = (s32[25]{0:T(128)S(1)}, s32[25]{0:T(128)S(1)}, u32[]{:S(2)}, u32[]{:S(2)}) collective-permute-start(s32[25]{0:T(128)S(1)} %concatenate.3.own_ref.idx_ref.refs_0_.refs_1_), channel_id=1, source_target_pairs={{0,1},{1,2},{2,3},{3,4},{4,5},{5,6},{6,7},{7,8},{8,9},{9,10},{10,1... | collective-permute-start | bytes 308 | tf_op jit(solution)/shard_map/ppermute | solution.py:26
  14.9 13.0 %copy-start.2 = (f32[1,2,2048,256]{3,2,1,0:T(8,128)S(1)}, f32[1,2,2048,256]{3,2,1,0:T(8,128)}, u32[]{:S(2)}) copy-start(f32[1,2,2048,256]{3,2,1,0:T(8,128)} %object_ref.7) | copy-start | bytes 12582916
  14.9 14.6 %collective-permute-start.1 = (bf16[2,256,256]{2,1,0:T(8,128)(2,1)S(1)}, bf16[2,256,256]{2,1,0:T(8,128)(2,1)S(1)}, u32[]{:S(2)}, u32[]{:S(2)}) collective-permute-start(bf16[2,256,256]{2,1,0:T(8,128)(2,1)S(1)} %get-tuple-element.21), channel_id=1, source_target_pairs={{1,0},{2,1},{3,2},{4,3},{5,4},{6,5},{7,6},{8,7},{9,8},{10,9},{11,1... | collective-permute-start | bytes 786440 | tf_op jit(solution)/shard_map/ppermute | solution.py:26
  17.3 31.4 %copy-start.4 = (f32[2,256,256]{2,1,0:T(8,128)S(1)}, f32[2,256,256]{2,1,0:T(8,128)}, u32[]{:S(2)}) copy-start(f32[2,256,256]{2,1,0:T(8,128)} %refs_8_.3) | copy-start | bytes 1572868
  17.3 31.4 %copy-start.5 = (bf16[512,512]{1,0:T(8,128)(2,1)S(1)}, bf16[512,512]{1,0:T(8,128)(2,1)}, u32[]{:S(2)}) copy-start(bf16[512,512]{1,0:T(8,128)(2,1)} %constant.16.clone.refs_10_) | copy-start | bytes 1572868
  17.4 31.4 %copy-start.6 = (bf16[512,512]{1,0:T(8,128)(2,1)S(1)}, bf16[512,512]{1,0:T(8,128)(2,1)}, u32[]{:S(2)}) copy-start(bf16[512,512]{1,0:T(8,128)(2,1)} %constant.15.clone.refs_9_) | copy-start | bytes 1572868
  17.4 30.5 %collective-permute-start.2 = (bf16[2,256,256]{2,1,0:T(8,128)(2,1)S(1)}, bf16[2,256,256]{2,1,0:T(8,128)(2,1)S(1)}, u32[]{:S(2)}, u32[]{:S(2)}) collective-permute-start(bf16[2,256,256]{2,1,0:T(8,128)(2,1)S(1)} %get-tuple-element.22), channel_id=1, source_target_pairs={{1,16},{2,17},{3,18},{4,19},{5,20},{6,21},{7,22},{8,23},{9,24},{10... | collective-permute-start | bytes 786440 | tf_op jit(solution)/shard_map/ppermute | solution.py:26
  26.0 31.2 %collective-permute-start.7 = (bf16[2,256,256]{2,1,0:T(8,128)(2,1)S(1)}, bf16[2,256,256]{2,1,0:T(8,128)(2,1)S(1)}, u32[]{:S(2)}, u32[]{:S(2)}) collective-permute-start(bf16[2,256,256]{2,1,0:T(8,128)(2,1)S(1)} %get-tuple-element.28), channel_id=1, source_target_pairs={{0,17},{1,18},{2,19},{3,20},{4,21},{5,22},{6,23},{7,24},{8,25},{9,... | collective-permute-start | bytes 786440 | tf_op jit(solution)/shard_map/ppermute | solution.py:26
  29.5 27.7 %collective-permute-start.6 = (bf16[4,256,256]{2,1,0:T(8,128)(2,1)S(1)}, bf16[4,256,256]{2,1,0:T(8,128)(2,1)S(1)}, u32[]{:S(2)}, u32[]{:S(2)}) collective-permute-start(bf16[4,256,256]{2,1,0:T(8,128)(2,1)S(1)} %get-tuple-element.27), channel_id=1, source_target_pairs={{0,1},{1,2},{2,3},{3,4},{4,5},{5,6},{6,7},{7,8},{8,9},{9,10},{10,1... | collective-permute-start | bytes 1572872 | tf_op jit(solution)/shard_map/ppermute | solution.py:26
  47.9 9.3 %collective-permute-start.8 = (bf16[2,2,256,256]{3,2,1,0:T(8,128)(2,1)S(1)}, bf16[2,2,256,256]{3,2,1,0:T(8,128)(2,1)S(1)}, u32[]{:S(2)}, u32[]{:S(2)}) collective-permute-start(bf16[2,2,256,256]{3,2,1,0:T(8,128)(2,1)S(1)} %get-tuple-element.30), channel_id=1, source_target_pairs={{0,16},{1,17},{2,18},{3,19},{4,20},{5,21},{6,22},{7,23},{8,24},{9,... | collective-permute-start | bytes 1572872 | tf_op jit(solution)/shard_map/ppermute | solution.py:26
  47.9 0.9 copy-start.7
  56.6 37.6 %collective-permute-start.5 = (bf16[3,2,256,256]{3,2,1,0:T(8,128)(2,1)S(1)}, bf16[3,2,256,256]{3,2,1,0:T(8,128)(2,1)S(1)}, u32[]{:S(2)}, u32[]{:S(2)}) collective-permute-start(bf16[3,2,256,256]{3,2,1,0:T(8,128)(2,1)S(1)} %get-tuple-element.26), channel_id=1, source_target_pairs={{0,16},{1,17},{2,18},{3,19},{4,20},{5,21},{6,22},{7,23},{8,24},{9,... | collective-permute-start | bytes 2359304 | tf_op jit(solution)/shard_map/ppermute | solution.py:26
  64.0 18.9 %collective-permute-start.10 = (bf16[2,256,256]{2,1,0:T(8,128)(2,1)S(1)}, bf16[2,256,256]{2,1,0:T(8,128)(2,1)S(1)}, u32[]{:S(2)}, u32[]{:S(2)}) collective-permute-start(bf16[2,256,256]{2,1,0:T(8,128)(2,1)S(1)} %get-tuple-element.33), channel_id=1, source_target_pairs={{1,0},{2,1},{3,2},{4,3},{5,4},{6,5},{7,6},{8,7},{9,8},{10,9},{11,1... | collective-permute-start | bytes 786440 | tf_op jit(solution)/shard_map/ppermute | solution.py:26
  66.2 28.0 %collective-permute-start.9 = (bf16[2,2,256,256]{3,2,1,0:T(8,128)(2,1)S(1)}, bf16[2,2,256,256]{3,2,1,0:T(8,128)(2,1)S(1)}, u32[]{:S(2)}, u32[]{:S(2)}) collective-permute-start(bf16[2,2,256,256]{3,2,1,0:T(8,128)(2,1)S(1)} %get-tuple-element.32), channel_id=1, source_target_pairs={{0,16},{1,17},{2,18},{3,19},{4,20},{5,21},{6,22},{7,23},{8,24},{9,... | collective-permute-start | bytes 1572872 | tf_op jit(solution)/shard_map/ppermute | solution.py:26
  66.3 22.2 %collective-permute-start.11 = (bf16[2,256,256]{2,1,0:T(8,128)(2,1)S(1)}, bf16[2,256,256]{2,1,0:T(8,128)(2,1)S(1)}, u32[]{:S(2)}, u32[]{:S(2)}) collective-permute-start(bf16[2,256,256]{2,1,0:T(8,128)(2,1)S(1)} %get-tuple-element.34), channel_id=1, source_target_pairs={{1,16},{2,17},{3,18},{4,19},{5,20},{6,21},{7,22},{8,23},{9,24},{10... | collective-permute-start | bytes 786440 | tf_op jit(solution)/shard_map/ppermute | solution.py:26
  68.2 20.3 %collective-permute-start.12 = (bf16[2,256,256]{2,1,0:T(8,128)(2,1)S(1)}, bf16[2,256,256]{2,1,0:T(8,128)(2,1)S(1)}, u32[]{:S(2)}, u32[]{:S(2)}) collective-permute-start(bf16[2,256,256]{2,1,0:T(8,128)(2,1)S(1)} %get-tuple-element.35), channel_id=1, source_target_pairs={{0,1},{1,2},{2,3},{3,4},{4,5},{5,6},{6,7},{7,8},{8,9},{9,10},{10,1... | collective-permute-start | bytes 786440 | tf_op jit(solution)/shard_map/ppermute | solution.py:26
  82.9 11.3 %collective-permute-start.13 = (bf16[2,256,256]{2,1,0:T(8,128)(2,1)S(1)}, bf16[2,256,256]{2,1,0:T(8,128)(2,1)S(1)}, u32[]{:S(2)}, u32[]{:S(2)}) collective-permute-start(bf16[2,256,256]{2,1,0:T(8,128)(2,1)S(1)} %get-tuple-element.36), channel_id=1, source_target_pairs={{0,17},{1,18},{2,19},{3,20},{4,21},{5,22},{6,23},{7,24},{8,25},{9,... | collective-permute-start | bytes 786440 | tf_op jit(solution)/shard_map/ppermute | solution.py:26

commit v2 on v1

v2 whole, which is shorter than its diff:
```python
import functools

import jax
import jax.numpy as jnp
import ml_dtypes
import numpy as np
from jax import lax
from jax.experimental import pallas as pl
from jax.experimental.pallas import tpu as pltpu
from jax.sharding import PartitionSpec as P

F32 = jnp.float32
BF16 = jnp.bfloat16
EXTRA = 8
HALVES = 16
DIGIT, HALF = 256, 64
FULL = 60 * 1024 * 1024
LIMIT = 24 * 1024 * 1024


def send(value, flip, steps):
    cores, count = lax.axis_size("cuts"), lax.axis_size("tile")
    first, last = max(0, -steps), min(count, count - steps)
    pairs = [
        (core * count + tile, (core ^ flip) * count + tile + steps)
        for core in range(cores)
        for tile in range(first, last)
    ]
    return lax.ppermute(value, ("cuts", "tile"), pairs)


def make_tables(length):
    index = np.arange(length, dtype=np.int32)
    product = index[:, None] * index[None, :] % length
    angle = product.astype(np.float32) * np.float32(2.0 * np.pi / length)
    scale = np.float32(length ** (-0.5))
    cosine = (np.cos(angle) * scale).astype(ml_dtypes.bfloat16)
    sine = (-np.sin(angle) * scale).astype(ml_dtypes.bfloat16)
    one = np.concatenate(
        [np.concatenate([cosine, sine], 1), np.concatenate([-sine, cosine], 1)], 0
    )
    two = np.concatenate(
        [np.concatenate([cosine, -sine], 1), np.concatenate([sine, cosine], 1)], 0
    )
    return jnp.asarray(one), jnp.asarray(two)


class Plan:
    def __init__(self, ref, slots, scan, width):
        assert slots == 6
        self.ref, self.slots, self.scan, self.width = ref, slots, scan, width
        live = ref[0, 0]
        final = ref[0, 1 + slots + 2 * scan] > 0
        self.live = live
        cols = [ref[0, 1 + slots + scan + ref[0, 1 + slot]] for slot in range(slots)]
        here = [(2 * pair < live) for pair in range(3)]
        fits = [
            final | (2 * pair + 1 >= live) | (cols[2 * pair] + cols[2 * pair + 1] <= width)
            for pair in range(3)
        ]
        is_a = [jnp.where(here[pair] & fits[pair], 1, 0) for pair in range(3)]
        is_b = [jnp.where(here[pair] & jnp.logical_not(fits[pair]), 1, 0) for pair in range(3)]
        count_a, count_b = sum(is_a), sum(is_b)

        def chosen(flags):
            first = jnp.where(flags[0] > 0, 0, jnp.where(flags[1] > 0, 1, 2))
            second = jnp.where((flags[0] > 0) & (flags[1] > 0), 1, 2)
            return first, second

        def bins(flags, count, spill):
            first, second = chosen(flags)
            lone = jnp.where(spill, 4, -1)
            return {
                (0, 0): jnp.where(count >= 1, 2 * first, lone),
                (1, 0): jnp.where(
                    count >= 2, 2 * second, jnp.where(count == 1, 2 * first + 1, jnp.where(spill, 5, -1))
                ),
                (0, 1): jnp.where(count >= 2, 2 * first + 1, -1),
                (1, 1): jnp.where(count >= 2, 2 * second + 1, -1),
            }

        self.bins = {
            "A": bins(is_a, count_a, count_b == 3),
            "B": bins(is_b, count_b, (count_a == 3) & jnp.logical_not(final)),
        }
        third = (count_a == 3) & final
        self.bins["A"][(0, 2)] = jnp.where(third, 4, -1)
        self.bins["A"][(1, 2)] = jnp.where(third, 5, -1)

    def item(self, kind, core, place):
        table = self.bins[kind]
        slot = jnp.where(core == 0, table[(0, place)], table[(1, place)])
        valid = (slot >= 0) & (slot < self.live)
        position = self.ref[0, 1 + jnp.where(valid, slot, 0)]
        row = self.ref[0, 1 + self.slots + position]
        col = self.ref[0, 1 + self.slots + self.scan + position]
        return valid, position, row, col


def turn(value, amount, width):
    return pltpu.roll(value, lax.rem(amount, width), 1)


def rows_down(value, shift):
    span, width = value.shape
    tiles = value.reshape(span // EXTRA, EXTRA, width)
    rolled = pltpu.roll(tiles, lax.rem(EXTRA - shift, EXTRA), 1)
    row = lax.broadcasted_iota(jnp.int32, (span // EXTRA - 1, EXTRA, width), 1)
    moved = jnp.where(row < EXTRA - shift, rolled[:-1], rolled[1:])
    return moved.reshape(span - EXTRA, width)


def rows_up(value, shift):
    height, width = value.shape
    tiles = value.reshape(height // EXTRA, EXTRA, width)
    rolled = pltpu.roll(tiles, lax.rem(shift, EXTRA), 1)
    blank = jnp.zeros((1, EXTRA, width), value.dtype)
    row = lax.broadcasted_iota(jnp.int32, (height // EXTRA + 1, EXTRA, width), 1)
    moved = jnp.where(
        row >= shift, jnp.concatenate([rolled, blank], 0), jnp.concatenate([blank, rolled], 0)
    )
    return moved.reshape(height + EXTRA, width)


def columns(shape):
    return lax.broadcasted_iota(jnp.int32, shape, 1)


def patch_rows(ref, at, plane, row, height, width):
    step = EXTRA if ref.dtype == F32 else HALVES
    start = pl.multiple_of(jnp.minimum(row // step * step, height - width - step), step)
    value = ref[(*at, plane, pl.ds(start, width + step), slice(None))].astype(F32)
    shift = row - start
    if step > EXTRA:
        late = shift >= EXTRA
        value = jnp.where(late, value[EXTRA:], value[: value.shape[0] - EXTRA])
        shift = shift - jnp.where(late, EXTRA, 0)
    return rows_down(value, shift)


def first_kernel(
    sizes, counts_ref, chosen_ref, row_ref, col_ref, object_ref, intensity_ref, own_ref, small_ref, straight_ref,
    cross_ref, whole, levels, sems, level_sems,
):
    slots, scan, width, height = sizes
    loads = [
        pltpu.make_async_copy(object_ref.at[0, plane], whole.at[plane], sems.at[plane]) for plane in range(2)
    ]
    for load in loads:
        load.start()
    core = lax.axis_index("cuts")
    own_ref[0, 0] = counts_ref[0]
    for slot in range(slots):
        own_ref[0, 1 + slot] = chosen_ref[0, slot]
    for place in range(scan):
        own_ref[0, 1 + slots + place] = row_ref[0, place]
        own_ref[0, 1 + slots + scan + place] = col_ref[0, place]
    final = lax.axis_index("tile") == lax.axis_size("tile") - 1
    own_ref[0, 1 + slots + 2 * scan] = jnp.where(final, 1, 0)
    own_ref[0, 2 + slots + 2 * scan] = core
    plan = Plan(own_ref, slots, scan, width)
    outs = (straight_ref, cross_ref)
    items = [[plan.item("B", owner, place) for place in range(2)] for owner in (core, 1 - core)]
    level_loads = [
        pltpu.make_async_copy(intensity_ref.at[0, items[group][group][1]], levels.at[group], level_sems.at[group])
        for group in range(2)
    ]
    for load in level_loads:
        load.start()
    tail = (HALVES, width)
    place = columns(tail)
    coded = jnp.zeros(tail, jnp.int32)
    for at in range(own_ref.shape[1]):
        value = own_ref[0, at]
        coded = jnp.where(place == at, value // DIGIT, jnp.where(place == at + HALF, value % DIGIT, coded))
    for group in range(2):
        outs[group][3 * width :] = coded.astype(F32).astype(BF16)
    lane = columns((width, width))
    for plane in range(2):
        loads[plane].wait()
        for group in range(2):
            (live0, _, row0, col0), (live1, _, row1, col1) = items[group]
            first = patch_rows(whole, (), plane, row0, height, width)
            second = turn(patch_rows(whole, (), plane, row1, height, width), width - col1, width)
            page = jnp.where(live0 & (lane >= col0), first, jnp.where(live1 & (lane < width - col1), second, 0.0))
            outs[group][plane * width : (plane + 1) * width] = page.astype(BF16)
        small_ref[plane] = whole[plane].astype(BF16)
    for group in range(2):
        level_loads[group].wait()
        outs[group][2 * width : 3 * width] = levels[group].astype(BF16)


def pages_kernel(sizes, own_ref, self_ref, other_ref, message_ref, _, out_ref, behind_ref, decoded, sem):
    slots, scan, width, height = sizes
    coded = message_ref[3 * width :, : 2 * HALF].astype(F32)
    value = coded * float(DIGIT) + pltpu.roll(coded, HALF, 1)
    decoded[...] = value[:EXTRA].astype(jnp.int32)
    copy = pltpu.make_async_copy(decoded, behind_ref, sem)
    copy.start()
    copy.wait()
    core = own_ref[0, 2 + slots + 2 * scan]
    plan = Plan(behind_ref, slots, scan, width)
    (live0, _, row0, col0), (live1, _, row1, col1) = [plan.item("A", core, place) for place in range(2)]
    lane = columns((width, width))
    mask0 = live0 & (lane < col0)
    mask1 = live1 & (lane >= width - col1)
    for source, ref in ((core, self_ref), (1 - core, other_ref)):
        for plane in range(2):
            first = patch_rows(ref, (), plane, row0, height, width)
            second = turn(patch_rows(ref, (), plane, row1, height, width), width - col1, width)
            out_ref[source, plane] = jnp.where(mask0, first, jnp.where(mask1, second, 0.0)).astype(BF16)


def parts_kernel(kind, sizes, behind_ref, own_ref, self_ref, other_ref, _, *rest):
    slots, scan, width, height = sizes
    core = own_ref[0, 2 + slots + 2 * scan]
    own = Plan(own_ref, slots, scan, width)
    if kind == "A":
        angle_ref, angle_other_ref, out_ref, turned_ref = rest
        items = [own.item("A", core, place) for place in range(2)]
        for source, ref in ((core, angle_ref), (1 - core, angle_other_ref)):
            turned_ref[source, 0] = jnp.cos(ref[0])
            turned_ref[source, 1] = jnp.sin(ref[0])
    else:
        (out_ref,) = rest
        plan = Plan(behind_ref, slots, scan, width)
        items = [plan.item("B", core, place) for place in range(2)] + [own.item("A", core, 2)]
    lane = columns((width, width))
    for place, (_, _, row, col) in enumerate(items):
        mask = lane >= width - col if kind == "B" and place < 2 else lane < width - col
        for source, ref in ((core, self_ref), (1 - core, other_ref)):
            for plane in range(2):
                rolled = turn(patch_rows(ref, (), plane, row, height, width), width - col, width)
                out_ref[place, source, plane] = jnp.where(mask, rolled, 0.0).astype(BF16)


def waves_kernel(kind, places, sizes, *refs):
    slots, scan, width, height = sizes
    behind_ref, own_ref = refs[:2]
    if kind == "A":
        page_ref, part_ref, phase, probe_ref, one_ref, two_ref, intensity_ref, _ = refs[2:10]
        rest = refs[10:]
    else:
        straight_ref, cross_ref, part_ref, phase, probe_ref, one_ref, two_ref, intensity_ref = refs[2:10]
        rest = refs[10:]
    back_straight, back_cross, out_self = rest[:3]
    out_swap, rest = rest[3], rest[4:]
    patch, wave, grads, field, half, levels, level_sems = rest
    core = own_ref[0, 2 + slots + 2 * scan]
    other = 1 - core
    plan = Plan(own_ref if kind == "A" else behind_ref, slots, scan, width)
    late = Plan(own_ref, slots, scan, width).item("A", core, 2)
    lane = columns((width, width))

    def foreign_mask(col, in_tile):
        if kind == "A":
            return lane < col if in_tile else lane >= width - col
        return lane >= col if in_tile else lane < width - col

    def propagate(adjoint, which, finish):
        sign = -1.0 if adjoint else 1.0
        for item in range(2):
            product = jnp.dot(field[item], one_ref[...], preferred_element_type=F32)
            half[item, :width] = product[:, :width].astype(BF16)
            half[item, width:] = product[:, width:].astype(BF16)
        for item in range(2):
            spectrum = jnp.dot(two_ref[...], half[item], preferred_element_type=F32)
            real, imag = spectrum[:width], spectrum[width:]
            cosine, sine = phase[which, 0], sign * phase[which, 1]
            field[item, :, :width] = (real * cosine - imag * sine).astype(BF16)
            field[item, :, width:] = (real * sine + imag * cosine).astype(BF16)
        for item in range(2):
            product = jnp.dot(field[item], two_ref[...], preferred_element_type=F32)
            half[item, :width] = product[:, :width].astype(BF16)
            half[item, width:] = product[:, width:].astype(BF16)
        for item in range(2):
            result = jnp.dot(one_ref[...], half[item], preferred_element_type=F32)
            finish(item, result[:width], result[width:])

    def put(item, real, imag):
        field[item, :, :width] = real.astype(BF16)
        field[item, :, width:] = imag.astype(BF16)

    def one_pair(turn_index, _):
        entries = []
        for item in range(2):
            entry = plan.item(kind, core, item)
            if places > 2:
                entry = tuple(jnp.where(turn_index > 0, b, a) for a, b in zip(entry, late))
            entries.append(entry)
        at = [jnp.minimum(2 * turn_index + item, places - 1) for item in range(2)]

        def levels_of(item):
            return pltpu.make_async_copy(
                intensity_ref.at[0, entries[item][1]], levels.at[item], level_sems.at[item]
            )

        if kind == "A":
            for item in range(2):
                levels_of(item).start()
        else:

            @pl.when(turn_index > 0)
            def _():
                for item in range(2):
                    levels_of(item).start()
                for item in range(2):
                    levels_of(item).wait()

            @pl.when(turn_index == 0)
            def _():
                levels[0] = straight_ref[2 * width : 3 * width].astype(F32)
                levels[1] = cross_ref[2 * width : 3 * width].astype(F32)

        for item in range(2):
            live, _, _, col = entries[item]
            mask = foreign_mask(col, item == 0)
            if kind == "B":
                mask = mask & (turn_index == 0)
            for at_source, source in enumerate((core, other)):
                for plane in range(2):
                    if kind == "A":
                        page = page_ref[source, plane]
                    else:
                        page = (straight_ref, cross_ref)[at_source][plane * width : (plane + 1) * width]
                    page = jnp.where(mask, page.astype(F32), 0.0)
                    if item == 0:
                        page = turn(page, width - col, width)
                    own = part_ref[at[item], source, plane].astype(F32)
                    patch[source, item, plane] = (page + own).astype(BF16)
        for item in range(2):
            left_re, left_im = probe_ref[0], probe_ref[1]
            right_re, right_im = patch[0, item, 0].astype(F32), patch[0, item, 1].astype(F32)
            put(item, left_re * right_re - left_im * right_im, left_re * right_im + left_im * right_re)

        def after_first(item, real, imag):
            real, imag = real.astype(BF16), imag.astype(BF16)
            wave[item, 0] = real
            wave[item, 1] = imag
            real, imag = real.astype(F32), imag.astype(F32)
            right_re, right_im = patch[1, item, 0].astype(F32), patch[1, item, 1].astype(F32)
            put(item, real * right_re - imag * right_im, real * right_im + imag * right_re)

        propagate(False, 0, after_first)
        if kind == "A":
            for item in range(2):
                levels_of(item).wait()

        def after_second(item, real, imag):
            real, imag = real.astype(BF16).astype(F32), imag.astype(BF16).astype(F32)
            gain = 2.0 * (real * real + imag * imag - levels[item])
            gain = jnp.where(entries[item][0], gain, 0.0)
            put(item, gain * real, gain * imag)

        propagate(False, 1, after_second)

        def before_second(item, real, imag):
            left_re, left_im = wave[item, 0].astype(F32), wave[item, 1].astype(F32)
            grads[1, item, 0] = (left_re * real + left_im * imag).astype(BF16)
            grads[1, item, 1] = (left_re * imag - left_im * real).astype(BF16)
            left_re, left_im = patch[1, item, 0].astype(F32), patch[1, item, 1].astype(F32)
            put(item, left_re * real + left_im * imag, left_re * imag - left_im * real)

        propagate(True, 1, before_second)

        def before_first(item, real, imag):
            left_re, left_im = probe_ref[0], probe_ref[1]
            grads[0, item, 0] = (left_re * real + left_im * imag).astype(BF16)
            grads[0, item, 1] = (left_re * imag - left_im * real).astype(BF16)

        propagate(True, 0, before_first)
        for item in range(2):
            out_self[at[item]] = grads[core, item]
            out_swap[at[item]] = grads[other, item]

        @pl.when(turn_index == 0)
        def _():
            live0, _, _, col0 = entries[0]
            live1, _, _, col1 = entries[1]
            mask0 = live0 & foreign_mask(col0, True)
            mask1 = live1 & foreign_mask(col1, False)
            for source, out_ref in ((core, back_straight), (other, back_cross)):
                for plane in range(2):
                    first = turn(grads[source, 0, plane].astype(F32), col0, width)
                    second = grads[source, 1, plane].astype(F32)
                    page = jnp.where(mask0, first, jnp.where(mask1, second, 0.0))
                    out_ref[plane] = page.astype(BF16)

        return 0

    if places > 2:
        turns = jnp.where(late[0], 2, 1)
        lax.fori_loop(0, turns, one_pair, 0)
    else:
        one_pair(jnp.int32(0), 0)


def add_piece(total, plane, entry, in_next, piece_ref, in_tile):
    live, _, row, col = entry
    height, width = total.shape[1:]

    @pl.when(live)
    def _():
        lane = columns((width, width))
        mask = lane < col if in_next else lane >= col
        start = pl.multiple_of(jnp.minimum(row // EXTRA * EXTRA, height - width - EXTRA), EXTRA)
        rows = pl.ds(start, width + EXTRA)
        piece = piece_ref[plane].astype(F32)
        if not in_tile:
            piece = turn(piece, col, width)
        moved = rows_up(jnp.where(mask, piece, 0.0), row - start)
        total[plane, rows, :] = total[plane, rows, :] + moved


def gather_kernel(sizes, own_ref, behind_ref, b_self, b_swap, b_back, b_back_cross, a_self, out_ref):
    slots, scan, width, height = sizes
    core = own_ref[0, 2 + slots + 2 * scan]
    other = 1 - core
    own = Plan(own_ref, slots, scan, width)
    behind = Plan(behind_ref, slots, scan, width)
    total = out_ref.at[0]
    out_ref[...] = jnp.zeros_like(out_ref)
    for plane in range(2):
        for owner, ref in ((core, b_self), (other, b_swap)):
            for place in range(2):
                add_piece(total, plane, behind.item("B", owner, place), True, ref.at[place], False)
            add_piece(total, plane, own.item("A", owner, 2), False, ref.at[2], False)
        for owner, ref in ((core, b_back), (other, b_back_cross)):
            for place in range(2):
                add_piece(total, plane, own.item("B", owner, place), False, ref, place == 0)
        for place in range(2):
            add_piece(total, plane, own.item("A", core, place), False, a_self.at[place], False)


def finish_kernel(
    sizes, own_ref, behind_ref, canvas_ref, a_swap, a_back, a_back_cross, out_ref, total, sems
):
    slots, scan, width, height = sizes
    core = own_ref[0, 2 + slots + 2 * scan]
    other = 1 - core
    own = Plan(own_ref, slots, scan, width)
    behind = Plan(behind_ref, slots, scan, width)
    copies = []
    for plane in range(2):
        total[plane] = canvas_ref[0, plane]
        for place in range(2):
            add_piece(total, plane, own.item("A", other, place), False, a_swap.at[place], False)
        for owner, ref in ((core, a_back), (other, a_back_cross)):
            for place in range(2):
                add_piece(total, plane, behind.item("A", owner, place), True, ref, place == 0)
        copy = pltpu.make_async_copy(total.at[plane], out_ref.at[0, plane], sems.at[plane])
        copy.start()
        copies.append(copy)
    for copy in copies:
        copy.wait()


def on_device(
    object_slices, probe_field, slice_phase, intensity, counts, chosen, row_offset, column_offset
):
    height, breadth = object_slices.shape[2:]
    width = probe_field.shape[-1]
    assert breadth == width and object_slices.shape[0] == 1
    slots, scan = chosen.shape[1], row_offset.shape[1]
    sizes = (slots, scan, width, height)
    one, two = make_tables(width)

    smem = pl.BlockSpec(memory_space=pltpu.SMEM)
    vmem = pl.BlockSpec(memory_space=pltpu.VMEM)
    anywhere = pl.BlockSpec(memory_space=pl.ANY)
    hbm = pl.BlockSpec(memory_space=pltpu.HBM)
    params = pltpu.CompilerParams(vmem_limit_bytes=LIMIT)
    planes = lambda *lead: jax.ShapeDtypeStruct((*lead, width, width), BF16)
    dma = lambda *shape: pltpu.SemaphoreType.DMA(shape)

    def call(kernel, name, operands, out_shape, scratch, cost=0, limit=LIMIT, out_specs=None):
        return pl.pallas_call(
            kernel,
            out_shape=out_shape,
            in_specs=[spec for spec, _ in operands],
            out_specs=out_specs or jax.tree.map(lambda _: vmem, out_shape),
            scratch_shapes=scratch,
            compiler_params=pltpu.CompilerParams(vmem_limit_bytes=limit),
            cost_estimate=pl.CostEstimate(flops=cost * 10**9, bytes_accessed=cost * 3 * 10**6, transcendentals=0),
            name=name,
        )(*[value for _, value in operands])

    def parts(kind, idx, after):
        count = 2 if kind == "A" else 3
        operands = [(smem, idx), (smem, own)]
        operands += [(vmem, small), (vmem, small_other), (anywhere, after)]
        shapes = [planes(count, 2, 2)]
        if kind == "A":
            operands += [(vmem, slice_phase), (vmem, phase_other)]
            shapes.append(jax.ShapeDtypeStruct((2, 2, width, width), F32))
        return call(functools.partial(parts_kernel, kind, sizes), "parts_" + kind.lower(), operands, shapes, [])

    def waves(kind, pages, part, *after):
        count = 2 if kind == "A" else 3
        operands = [(smem, behind), (smem, own)]
        operands += [(vmem, value) for value in (*pages, part, turned, probe_field, one, two)]
        operands += [(hbm, intensity)] + [(anywhere, value) for value in after]
        scratch = [
            pltpu.VMEM((2, 2, 2, width, width), BF16),
            pltpu.VMEM((2, 2, width, width), BF16),
            pltpu.VMEM((2, 2, 2, width, width), BF16),
            pltpu.VMEM((2, width, 2 * width), BF16),
            pltpu.VMEM((2, 2 * width, width), BF16),
            pltpu.VMEM((2, width, width), F32),
            dma(2),
        ]
        shapes = [planes(2), planes(2), planes(count, 2), planes(count, 2)]
        return call(
            functools.partial(waves_kernel, kind, count, sizes), "waves_" + kind.lower(), operands, shapes, scratch, 7
        )

    phase_other = send(slice_phase, 1, 0)
    message = jax.ShapeDtypeStruct((3 * width + HALVES, width), BF16)
    own, small, b_straight, b_cross = call(
        functools.partial(first_kernel, sizes),
        "first",
        [(smem, value) for value in (counts, chosen, row_offset, column_offset)]
        + [(hbm, object_slices), (hbm, intensity)],
        [
            jax.ShapeDtypeStruct((1, 3 + slots + 2 * scan), jnp.int32),
            jax.ShapeDtypeStruct(object_slices.shape[1:], BF16),
            message,
            message,
        ],
        [pltpu.VMEM((2, height, width), F32), pltpu.VMEM((2, width, width), F32), dma(2), dma(2)],
        limit=FULL,
        out_specs=[smem, vmem, vmem, vmem],
    )
    small_other = send(small, 1, 0)
    b_first = b_cross
    b_straight, b_cross = send(b_straight, 0, 1), send(b_cross, 1, 1)
    a_part, turned = parts("A", own, b_first)
    page, behind = call(
        functools.partial(pages_kernel, sizes),
        "pages",
        [(smem, own), (vmem, small), (vmem, small_other), (vmem, b_straight), (anywhere, a_part)],
        [planes(2, 2), jax.ShapeDtypeStruct((EXTRA, 2 * HALF), jnp.int32)],
        [pltpu.VMEM((EXTRA, 2 * HALF), jnp.int32), pltpu.SemaphoreType.DMA(())],
        out_specs=[vmem, smem],
    )
    b_part, = parts("B", behind, page)
    page = send(page, 0, -1)
    b_back, b_back_cross, b_self, b_swap = waves("B", (b_straight, b_cross), b_part)
    b_swap = send(b_swap, 1, 0)
    b_back, b_back_cross = send(b_back, 0, -1), send(b_back_cross, 1, -1)
    a_back, a_back_cross, a_self, a_swap = waves("A", (page,), a_part, b_self)
    a_back, a_back_cross = send(a_back, 0, 1), send(a_back_cross, 1, 1)
    a_swap = send(a_swap, 1, 0)
    whole = jax.ShapeDtypeStruct(object_slices.shape, F32)
    pieces = [(smem, own), (smem, behind)]
    canvas = call(
        functools.partial(gather_kernel, sizes),
        "gather",
        pieces + [(vmem, value) for value in (b_self, b_swap, b_back, b_back_cross, a_self)],
        whole,
        [],
        cost=10,
    )
    return call(
        functools.partial(finish_kernel, sizes),
        "finish",
        pieces + [(vmem, value) for value in (canvas, a_swap, a_back, a_back_cross)],
        whole,
        [pltpu.VMEM((2, height, width), F32), dma(2)],
        out_specs=hbm,
    )


def solution(mesh):
    return jax.shard_map(
        on_device,
        mesh=mesh,
        in_specs=(
            P("cuts", None, None, "tile"),
            P(),
            P("cuts", None, None),
            P("tile", None, None, None),
            P("tile"),
            P("tile", None),
            P("tile", None),
            P("tile", None),
        ),
        out_specs=P("cuts", None, None, "tile"),
        check_vma=False,
    )
```

time: 99.1 us -> 72.1 us (0.73)
  the two profiles are of different devices: /device:TPU:13 before, /device:TPU:17 now
where the time goes in v2:
time: 72.1 us; the launch traced here: 71.3 us
  Pallas kernels  32 us (44%)
  starting transfers between devices  24.4 us (34%)
  waiting for transfers between devices  10.4 us (14%)
  local copies, waits for them, and re-layouts  3.51 us (5%)
  between operations  1.04 us (1%)
    pallas_call x8, Pallas kernels, call(): pl.pallas_call(kernel, out_shape=out_shape, in_specs=[spec for spec, _ in...  32 us
    ppermute x11, starting transfers between devices, send(): return lax.ppermute(value, ('cuts', 'tile'), pairs)  24.4 us
    ppermute x11, waiting for transfers between devices, send(): return lax.ppermute(value, ('cuts', 'tile'), pairs)  10.4 us
    unnamed x16, local copies, waits for them, and re-layouts  3.51 us
  transfers between devices with their start and end apart: 11, of which 3 were waited for; matrix products, arithmetic and copies ran while one was open for 0% of the time, Pallas kernels for 34%

profile of v2, /device:TPU:17, one launch (start us, length us, event | category | flops | bytes accessed | tf_op | source)
XLA Modules:
  0.0 71.3 jit_solution(17425941363275673845)
XLA Ops:
  0.7 0.0 copy-start.3
  0.7 5.0 %first.1 = (s32[1,25]{1,0:T(1,128)}, bf16[2,2048,256]{2,1,0:T(8,128)(2,1)}, bf16[784,256]{1,0:T(8,128)(2,1)}, bf16[784,256]{1,0:T(8,128)(2,1)}) custom-call(s32[1]{0:T(128)S(6)} %copy.11.counts_ref, s32[1,6]{1,0:T(1,128)} %chosen_ref.1, s32[1,8]{1,0:T(1,128)} %row_ref.1, s32[1,8]{1,0:T(1,128)} %col_ref.1, f32[1,2,2048,256]{3,2,1,0:T(8,128)} %object_ref.1, ...), custom_call_target="tpu_custom_call" | custom-call | tf_op jit(solution)/shard_map/first/pallas_call | solution.py:477
  5.7 0.7 %collective-permute-start = (bf16[2,2048,256]{2,1,0:T(8,128)(2,1)}, bf16[2,2048,256]{2,1,0:T(8,128)(2,1)S(1)}, u32[]{:S(2)}, u32[]{:S(2)}) collective-permute-start(bf16[2,2048,256]{2,1,0:T(8,128)(2,1)} %get-tuple-element.22.self_ref), channel_id=1, source_target_pairs={{0,16},{1,17},{2,18},{3,19},{4,20},{5,21},{6,22},{7,23},{8,24},{9,... | collective-permute-start | bytes 6291464 | tf_op jit(solution)/shard_map/ppermute | solution.py:29
  6.4 3.1 %collective-permute-start.1 = (bf16[784,256]{1,0:T(8,128)(2,1)}, bf16[784,256]{1,0:T(8,128)(2,1)S(1)}, u32[]{:S(2)}, u32[]{:S(2)}) collective-permute-start(bf16[784,256]{1,0:T(8,128)(2,1)} %get-tuple-element.23), channel_id=1, source_target_pairs={{0,1},{1,2},{2,3},{3,4},{4,5},{5,6},{6,7},{7,8},{8,9},{9,10},{10,1... | collective-permute-start | bytes 1204232 | tf_op jit(solution)/shard_map/ppermute | solution.py:29
  9.5 3.3 %collective-permute-start.3 = (bf16[784,256]{1,0:T(8,128)(2,1)}, bf16[784,256]{1,0:T(8,128)(2,1)S(1)}, u32[]{:S(2)}, u32[]{:S(2)}) collective-permute-start(bf16[784,256]{1,0:T(8,128)(2,1)} %get-tuple-element.24._), channel_id=1, source_target_pairs={{0,17},{1,18},{2,19},{3,20},{4,21},{5,22},{6,23},{7,24},{8,25},{9,... | collective-permute-start | bytes 1204232 | tf_op jit(solution)/shard_map/ppermute | solution.py:29
  12.8 0.0 copy-done.3
  12.8 0.3 collective-permute-start.2
  13.1 1.3 %collective-permute-done.2.rest_1_ = f32[1,256,256]{2,1,0:T(8,128)S(1)} collective-permute-done((f32[1,256,256]{2,1,0:T(8,128)S(1)}, f32[1,256,256]{2,1,0:T(8,128)S(1)}, u32[]{:S(2)}, u32[]{:S(2)}) %collective-permute-start.2) | collective-permute-done | bytes 262176 | tf_op jit(solution)/shard_map/ppermute | solution.py:29
  14.4 0.0 collective-permute-done.other_ref
  14.4 0.0 copy-start
  14.4 1.6 %copy-done = bf16[2,2048,256]{2,1,0:T(8,128)(2,1)S(1)} copy-done((bf16[2,2048,256]{2,1,0:T(8,128)(2,1)S(1)}, bf16[2,2048,256]{2,1,0:T(8,128)(2,1)}, u32[]{:S(2)}) %copy-start) | copy-done | bytes 2097176
  16.0 0.0 copy-start.2
  16.0 1.0 %copy-done.2 = bf16[784,256]{1,0:T(8,128)(2,1)S(1)} copy-done((bf16[784,256]{1,0:T(8,128)(2,1)S(1)}, bf16[784,256]{1,0:T(8,128)(2,1)}, u32[]{:S(2)}) %copy-start.2) | copy-done | bytes 401432
  17.0 0.0 copy-start.4
  17.0 0.6 copy-done.4
  17.7 4.5 %parts_a.1 = (bf16[2,2,2,256,256]{4,3,2,1,0:T(8,128)(2,1)S(1)}, f32[2,2,256,256]{3,2,1,0:T(8,128)S(1)}) custom-call(s32[1,25]{1,0:T(1,128)S(1)} %copy-done.4, s32[1,25]{1,0:T(1,128)S(1)} %copy-done.4, bf16[2,2048,256]{2,1,0:T(8,128)(2,1)S(1)} %copy-done, bf16[2,2048,256]{2,1,0:T(8,128)(2,1)S(1)} %collective-permute-done.other_ref, ...), custom_call_target="tpu_custom_call" | custom-call | tf_op jit(solution)/shard_map/parts_a/pallas_call | solution.py:477
  22.2 0.0 collective-permute-done.1.message_ref.refs_2_
  22.2 1.9 %pages.1 = (bf16[2,2,256,256]{3,2,1,0:T(8,128)(2,1)S(1)}, s32[8,128]{1,0:T(8,128)S(1)}) custom-call(s32[1,25]{1,0:T(1,128)S(1)} %copy-done.4, bf16[2,2048,256]{2,1,0:T(8,128)(2,1)S(1)} %copy-done, bf16[2,2048,256]{2,1,0:T(8,128)(2,1)S(1)} %collective-permute-done.other_ref, bf16[784,256]{1,0:T(8,128)(2,1)S(1)} %collective-permute-done.1.message_ref.refs_2_, ...), custom_call_target="tpu_custom_call" | custom-call | tf_op jit(solution)/shard_map/pages/pallas_call | solution.py:477
  24.1 4.1 %collective-permute-start.7 = (bf16[2,2,256,256]{3,2,1,0:T(8,128)(2,1)S(1)}, bf16[2,2,256,256]{3,2,1,0:T(8,128)(2,1)S(1)}, u32[]{:S(2)}, u32[]{:S(2)}) collective-permute-start(bf16[2,2,256,256]{3,2,1,0:T(8,128)(2,1)S(1)} %get-tuple-element.27._), channel_id=1, source_target_pairs={{1,0},{2,1},{3,2},{4,3},{5,4},{6,5},{7,6},{8,7},{9,8},{10,9},{11,1... | collective-permute-start | bytes 1572872 | tf_op jit(solution)/shard_map/ppermute | solution.py:29
  28.3 0.0 copy-start.1
  28.3 0.0 copy-start.5
  28.3 0.0 copy-start.6
  28.3 0.0 copy-start.7
  28.3 1.6 %parts_b.1.refs_4_ = bf16[3,2,2,256,256]{4,3,2,1,0:T(8,128)(2,1)S(1)} custom-call(s32[8,128]{1,0:T(8,128)S(1)} %get-tuple-element.26.behind_ref.refs_0_, s32[1,25]{1,0:T(1,128)S(1)} %copy-done.4, bf16[2,2048,256]{2,1,0:T(8,128)(2,1)S(1)} %copy-done, bf16[2,2048,256]{2,1,0:T(8,128)(2,1)S(1)} %collective-permute-done.other_ref, ...), custom_call_target="tpu_custom_call" | custom-call | tf_op jit(solution)/shard_map/parts_b/pallas_call | solution.py:477
  30.0 0.0 collective-permute-done.3.refs_3_
  30.0 0.0 copy-done.1
  30.0 0.0 copy-done.5
  30.0 0.1 copy-done.6
  30.1 0.2 copy-done.7
  30.3 7.0 %waves_b.1 = (bf16[2,256,256]{2,1,0:T(8,128)(2,1)S(1)}, bf16[2,256,256]{2,1,0:T(8,128)(2,1)S(1)}, bf16[3,2,256,256]{3,2,1,0:T(8,128)(2,1)S(1)}, bf16[3,2,256,256]{3,2,1,0:T(8,128)(2,1)S(1)}) custom-call(s32[8,128]{1,0:T(8,128)S(1)} %get-tuple-element.26.behind_ref.refs_0_, s32[1,25]{1,0:T(1,128)S(1)} %copy-done.4, ...), custom_call_target="tpu_custom_call" | custom-call | flops 7000000000 | bytes 21000000 | tf_op jit(solution)/shard_map/waves_b/pallas_call | solution.py:477
  37.3 0.5 collective-permute-start.4
  37.9 2.2 %collective-permute-start.5 = (bf16[2,256,256]{2,1,0:T(8,128)(2,1)S(1)}, bf16[2,256,256]{2,1,0:T(8,128)(2,1)S(1)}, u32[]{:S(2)}, u32[]{:S(2)}) collective-permute-start(bf16[2,256,256]{2,1,0:T(8,128)(2,1)S(1)} %get-tuple-element.31), channel_id=1, source_target_pairs={{1,0},{2,1},{3,2},{4,3},{5,4},{6,5},{7,6},{8,7},{9,8},{10,9},{11,1... | collective-permute-start | bytes 786440 | tf_op jit(solution)/shard_map/ppermute | solution.py:29
  40.0 3.5 %collective-permute-start.6 = (bf16[2,256,256]{2,1,0:T(8,128)(2,1)S(1)}, bf16[2,256,256]{2,1,0:T(8,128)(2,1)S(1)}, u32[]{:S(2)}, u32[]{:S(2)}) collective-permute-start(bf16[2,256,256]{2,1,0:T(8,128)(2,1)S(1)} %get-tuple-element.32), channel_id=1, source_target_pairs={{1,16},{2,17},{3,18},{4,19},{5,20},{6,21},{7,22},{8,23},{9,24},{10... | collective-permute-start | bytes 786440 | tf_op jit(solution)/shard_map/ppermute | solution.py:29
  43.6 0.0 collective-permute-done.7.refs_2_
  43.6 7.2 %waves_a.1 = (bf16[2,256,256]{2,1,0:T(8,128)(2,1)S(1)}, bf16[2,256,256]{2,1,0:T(8,128)(2,1)S(1)}, bf16[2,2,256,256]{3,2,1,0:T(8,128)(2,1)S(1)}, bf16[2,2,256,256]{3,2,1,0:T(8,128)(2,1)S(1)}) custom-call(s32[8,128]{1,0:T(8,128)S(1)} %get-tuple-element.26.behind_ref.refs_0_, s32[1,25]{1,0:T(1,128)S(1)} %copy-done.4, ...), custom_call_target="tpu_custom_call" | custom-call | flops 7000000000 | bytes 21000000 | tf_op jit(solution)/shard_map/waves_a/pallas_call | solution.py:477
  50.8 2.2 %collective-permute-start.9 = (bf16[2,256,256]{2,1,0:T(8,128)(2,1)S(1)}, bf16[2,256,256]{2,1,0:T(8,128)(2,1)S(1)}, u32[]{:S(2)}, u32[]{:S(2)}) collective-permute-start(bf16[2,256,256]{2,1,0:T(8,128)(2,1)S(1)} %get-tuple-element.35), channel_id=1, source_target_pairs={{0,1},{1,2},{2,3},{3,4},{4,5},{5,6},{6,7},{7,8},{8,9},{9,10},{10,1... | collective-permute-start | bytes 786440 | tf_op jit(solution)/shard_map/ppermute | solution.py:29
  52.9 4.4 %collective-permute-start.10 = (bf16[2,256,256]{2,1,0:T(8,128)(2,1)S(1)}, bf16[2,256,256]{2,1,0:T(8,128)(2,1)S(1)}, u32[]{:S(2)}, u32[]{:S(2)}) collective-permute-start(bf16[2,256,256]{2,1,0:T(8,128)(2,1)S(1)} %get-tuple-element.36), channel_id=1, source_target_pairs={{0,17},{1,18},{2,19},{3,20},{4,21},{5,22},{6,23},{7,24},{8,25},{9,... | collective-permute-start | bytes 786440 | tf_op jit(solution)/shard_map/ppermute | solution.py:29
  57.3 0.0 collective-permute-done.5.b_back
  57.3 0.1 collective-permute-start.8
  57.4 0.0 collective-permute-done.6.b_back_cross
  57.4 0.0 collective-permute-done.4.b_swap
  57.4 1.6 %gather.1.canvas_ref = f32[1,2,2048,256]{3,2,1,0:T(8,128)S(1)} custom-call(s32[1,25]{1,0:T(1,128)S(1)} %copy-done.4, s32[8,128]{1,0:T(8,128)S(1)} %get-tuple-element.26.behind_ref.refs_0_, bf16[3,2,256,256]{3,2,1,0:T(8,128)(2,1)S(1)} %get-tuple-element.29.refs_9_.b_self, bf16[3,2,256,256]{3,2,1,0:T(8,128)(2,1)S(1)} %collective-permute-done.4.b_swap, ...), custom_call_target="tpu_custom_call" | custom-call | flops 10000000000 | bytes 30000000 | tf_op jit(solution)/shard_map/gather/pallas_call | solution.py:477
  59.1 3.1 %collective-permute-done.9.a_back = bf16[2,256,256]{2,1,0:T(8,128)(2,1)S(1)} collective-permute-done((bf16[2,256,256]{2,1,0:T(8,128)(2,1)S(1)}, bf16[2,256,256]{2,1,0:T(8,128)(2,1)S(1)}, u32[]{:S(2)}, u32[]{:S(2)}) %collective-permute-start.9) | collective-permute-done | bytes 262176 | tf_op jit(solution)/shard_map/ppermute | solution.py:29
  62.2 5.9 %collective-permute-done.10.a_back_cross = bf16[2,256,256]{2,1,0:T(8,128)(2,1)S(1)} collective-permute-done((bf16[2,256,256]{2,1,0:T(8,128)(2,1)S(1)}, bf16[2,256,256]{2,1,0:T(8,128)(2,1)S(1)}, u32[]{:S(2)}, u32[]{:S(2)}) %collective-permute-start.10) | collective-permute-done | bytes 262176 | tf_op jit(solution)/shard_map/ppermute | solution.py:29
  68.1 0.0 collective-permute-done.8.a_swap
  68.1 3.0 %finish.1 = f32[1,2,2048,256]{3,2,1,0:T(8,128)} custom-call(s32[1,25]{1,0:T(1,128)S(1)} %copy-done.4, s32[8,128]{1,0:T(8,128)S(1)} %get-tuple-element.26.behind_ref.refs_0_, f32[1,2,2048,256]{3,2,1,0:T(8,128)S(1)} %gather.1.canvas_ref, bf16[2,2,256,256]{3,2,1,0:T(8,128)(2,1)S(1)} %collective-permute-done.8.a_swap, ...), custom_call_target="tpu_custom_call" | custom-call | tf_op jit(solution)/shard_map/finish/pallas_call | solution.py:477
Async XLA Ops:
  0.7 12.2 %copy-start.3 = (f32[1,256,256]{2,1,0:T(8,128)S(1)}, f32[1,256,256]{2,1,0:T(8,128)}, u32[]{:S(2)}) copy-start(f32[1,256,256]{2,1,0:T(8,128)} %rest_0_.1) | copy-start | bytes 786436
  5.7 8.8 %collective-permute-start = (bf16[2,2048,256]{2,1,0:T(8,128)(2,1)}, bf16[2,2048,256]{2,1,0:T(8,128)(2,1)S(1)}, u32[]{:S(2)}, u32[]{:S(2)}) collective-permute-start(bf16[2,2048,256]{2,1,0:T(8,128)(2,1)} %get-tuple-element.22.self_ref), channel_id=1, source_target_pairs={{0,16},{1,17},{2,18},{3,19},{4,20},{5,21},{6,22},{7,23},{8,24},{9,... | collective-permute-start | bytes 6291464 | tf_op jit(solution)/shard_map/ppermute | solution.py:29
  6.4 15.8 %collective-permute-start.1 = (bf16[784,256]{1,0:T(8,128)(2,1)}, bf16[784,256]{1,0:T(8,128)(2,1)S(1)}, u32[]{:S(2)}, u32[]{:S(2)}) collective-permute-start(bf16[784,256]{1,0:T(8,128)(2,1)} %get-tuple-element.23), channel_id=1, source_target_pairs={{0,1},{1,2},{2,3},{3,4},{4,5},{5,6},{6,7},{7,8},{8,9},{9,10},{10,1... | collective-permute-start | bytes 1204232 | tf_op jit(solution)/shard_map/ppermute | solution.py:29
  9.5 20.5 %collective-permute-start.3 = (bf16[784,256]{1,0:T(8,128)(2,1)}, bf16[784,256]{1,0:T(8,128)(2,1)S(1)}, u32[]{:S(2)}, u32[]{:S(2)}) collective-permute-start(bf16[784,256]{1,0:T(8,128)(2,1)} %get-tuple-element.24._), channel_id=1, source_target_pairs={{0,17},{1,18},{2,19},{3,20},{4,21},{5,22},{6,23},{7,24},{8,25},{9,... | collective-permute-start | bytes 1204232 | tf_op jit(solution)/shard_map/ppermute | solution.py:29
  12.8 1.6 %collective-permute-start.2 = (f32[1,256,256]{2,1,0:T(8,128)S(1)}, f32[1,256,256]{2,1,0:T(8,128)S(1)}, u32[]{:S(2)}, u32[]{:S(2)}) collective-permute-start(f32[1,256,256]{2,1,0:T(8,128)S(1)} %copy-done.3), channel_id=1, source_target_pairs={{0,16},{1,17},{2,18},{3,19},{4,20},{5,21},{6,22},{7,23},{8,24},{9,... | collective-permute-start | bytes 786440 | tf_op jit(solution)/shard_map/ppermute | solution.py:29
  14.4 1.6 %copy-start = (bf16[2,2048,256]{2,1,0:T(8,128)(2,1)S(1)}, bf16[2,2048,256]{2,1,0:T(8,128)(2,1)}, u32[]{:S(2)}) copy-start(bf16[2,2048,256]{2,1,0:T(8,128)(2,1)} %get-tuple-element.22.self_ref) | copy-start | bytes 6291460
  16.0 1.0 %copy-start.2 = (bf16[784,256]{1,0:T(8,128)(2,1)S(1)}, bf16[784,256]{1,0:T(8,128)(2,1)}, u32[]{:S(2)}) copy-start(bf16[784,256]{1,0:T(8,128)(2,1)} %get-tuple-element.24._) | copy-start | bytes 1204228
  17.0 0.6 copy-start.4
  24.1 19.4 %collective-permute-start.7 = (bf16[2,2,256,256]{3,2,1,0:T(8,128)(2,1)S(1)}, bf16[2,2,256,256]{3,2,1,0:T(8,128)(2,1)S(1)}, u32[]{:S(2)}, u32[]{:S(2)}) collective-permute-start(bf16[2,2,256,256]{3,2,1,0:T(8,128)(2,1)S(1)} %get-tuple-element.27._), channel_id=1, source_target_pairs={{1,0},{2,1},{3,2},{4,3},{5,4},{6,5},{7,6},{8,7},{9,8},{10,9},{11,1... | collective-permute-start | bytes 1572872 | tf_op jit(solution)/shard_map/ppermute | solution.py:29
  28.3 1.7 %copy-start.1 = (f32[1,8,256,256]{3,2,1,0:T(8,128)S(1)}, f32[1,8,256,256]{3,2,1,0:T(8,128)}, u32[]{:S(2)}) copy-start(f32[1,8,256,256]{3,2,1,0:T(8,128)} %refs_8_.2) | copy-start | bytes 6291460
  28.3 1.7 %copy-start.5 = (f32[2,256,256]{2,1,0:T(8,128)S(1)}, f32[2,256,256]{2,1,0:T(8,128)}, u32[]{:S(2)}) copy-start(f32[2,256,256]{2,1,0:T(8,128)} %refs_5_.1) | copy-start | bytes 1572868
  28.3 1.8 %copy-start.6 = (bf16[512,512]{1,0:T(8,128)(2,1)S(1)}, bf16[512,512]{1,0:T(8,128)(2,1)}, u32[]{:S(2)}) copy-start(bf16[512,512]{1,0:T(8,128)(2,1)} %constant.5.clone.refs_8_.refs_7_) | copy-start | bytes 1572868
  28.3 2.0 %copy-start.7 = (bf16[512,512]{1,0:T(8,128)(2,1)S(1)}, bf16[512,512]{1,0:T(8,128)(2,1)}, u32[]{:S(2)}) copy-start(bf16[512,512]{1,0:T(8,128)(2,1)} %constant.4.clone.refs_7_.refs_6_) | copy-start | bytes 1572868
  37.3 20.1 %collective-permute-start.4 = (bf16[3,2,256,256]{3,2,1,0:T(8,128)(2,1)S(1)}, bf16[3,2,256,256]{3,2,1,0:T(8,128)(2,1)S(1)}, u32[]{:S(2)}, u32[]{:S(2)}) collective-permute-start(bf16[3,2,256,256]{3,2,1,0:T(8,128)(2,1)S(1)} %get-tuple-element.30), channel_id=1, source_target_pairs={{0,16},{1,17},{2,18},{3,19},{4,20},{5,21},{6,22},{7,23},{8,24},{9,... | collective-permute-start | bytes 2359304 | tf_op jit(solution)/shard_map/ppermute | solution.py:29
  37.9 19.4 %collective-permute-start.5 = (bf16[2,256,256]{2,1,0:T(8,128)(2,1)S(1)}, bf16[2,256,256]{2,1,0:T(8,128)(2,1)S(1)}, u32[]{:S(2)}, u32[]{:S(2)}) collective-permute-start(bf16[2,256,256]{2,1,0:T(8,128)(2,1)S(1)} %get-tuple-element.31), channel_id=1, source_target_pairs={{1,0},{2,1},{3,2},{4,3},{5,4},{6,5},{7,6},{8,7},{9,8},{10,9},{11,1... | collective-permute-start | bytes 786440 | tf_op jit(solution)/shard_map/ppermute | solution.py:29
  40.0 17.4 %collective-permute-start.6 = (bf16[2,256,256]{2,1,0:T(8,128)(2,1)S(1)}, bf16[2,256,256]{2,1,0:T(8,128)(2,1)S(1)}, u32[]{:S(2)}, u32[]{:S(2)}) collective-permute-start(bf16[2,256,256]{2,1,0:T(8,128)(2,1)S(1)} %get-tuple-element.32), channel_id=1, source_target_pairs={{1,16},{2,17},{3,18},{4,19},{5,20},{6,21},{7,22},{8,23},{9,24},{10... | collective-permute-start | bytes 786440 | tf_op jit(solution)/shard_map/ppermute | solution.py:29
  50.8 11.5 %collective-permute-start.9 = (bf16[2,256,256]{2,1,0:T(8,128)(2,1)S(1)}, bf16[2,256,256]{2,1,0:T(8,128)(2,1)S(1)}, u32[]{:S(2)}, u32[]{:S(2)}) collective-permute-start(bf16[2,256,256]{2,1,0:T(8,128)(2,1)S(1)} %get-tuple-element.35), channel_id=1, source_target_pairs={{0,1},{1,2},{2,3},{3,4},{4,5},{5,6},{6,7},{7,8},{8,9},{9,10},{10,1... | collective-permute-start | bytes 786440 | tf_op jit(solution)/shard_map/ppermute | solution.py:29
  52.9 15.2 %collective-permute-start.10 = (bf16[2,256,256]{2,1,0:T(8,128)(2,1)S(1)}, bf16[2,256,256]{2,1,0:T(8,128)(2,1)S(1)}, u32[]{:S(2)}, u32[]{:S(2)}) collective-permute-start(bf16[2,256,256]{2,1,0:T(8,128)(2,1)S(1)} %get-tuple-element.36), channel_id=1, source_target_pairs={{0,17},{1,18},{2,19},{3,20},{4,21},{5,22},{6,23},{7,24},{8,25},{9,... | collective-permute-start | bytes 786440 | tf_op jit(solution)/shard_map/ppermute | solution.py:29
  57.3 10.8 %collective-permute-start.8 = (bf16[2,2,256,256]{3,2,1,0:T(8,128)(2,1)S(1)}, bf16[2,2,256,256]{3,2,1,0:T(8,128)(2,1)S(1)}, u32[]{:S(2)}, u32[]{:S(2)}) collective-permute-start(bf16[2,2,256,256]{3,2,1,0:T(8,128)(2,1)S(1)} %get-tuple-element.34), channel_id=1, source_target_pairs={{0,16},{1,17},{2,18},{3,19},{4,20},{5,21},{6,22},{7,23},{8,24},{9,... | collective-permute-start | bytes 1572872 | tf_op jit(solution)/shard_map/ppermute | solution.py:29

commit v3 on v2

v3 whole, which is shorter than its diff:
```python
import functools
import math

import jax
import jax.numpy as jnp
import ml_dtypes
import numpy as np
from jax import lax
from jax.experimental import pallas as pl
from jax.experimental.pallas import tpu as pltpu
from jax.sharding import PartitionSpec as P

F32 = jnp.float32
BF16 = jnp.bfloat16
EXTRA = 8
HALVES = 16
DIGIT, HALF, LANES = 256, 64, 128
REACH = 256
LIMIT = 24 * 1024 * 1024


def send(value, flip, steps):
    cores, count = lax.axis_size("cuts"), lax.axis_size("tile")
    first, last = max(0, -steps), min(count, count - steps)
    pairs = [
        (core * count + tile, (core ^ flip) * count + tile + steps)
        for core in range(cores)
        for tile in range(first, last)
    ]
    return lax.ppermute(value, ("cuts", "tile"), pairs)


def make_tables(length):
    index = np.arange(length, dtype=np.int32)
    product = index[:, None] * index[None, :] % length
    angle = product.astype(np.float32) * np.float32(2.0 * np.pi / length)
    scale = np.float32(length ** (-0.5))
    cosine = (np.cos(angle) * scale).astype(ml_dtypes.bfloat16)
    sine = (-np.sin(angle) * scale).astype(ml_dtypes.bfloat16)
    one = np.concatenate(
        [np.concatenate([cosine, sine], 1), np.concatenate([-sine, cosine], 1)], 0
    )
    two = np.concatenate(
        [np.concatenate([cosine, -sine], 1), np.concatenate([sine, cosine], 1)], 0
    )
    return jnp.asarray(one), jnp.asarray(two)


ENTRY, FIELDS = 8, 4


class Table:
    def __init__(self, ref):
        self.ref = ref

    def item(self, kind, core, place):
        index = 3 * core + place if kind == "A" else 6 + 2 * core + place
        at = ENTRY + FIELDS * index
        return self.ref[0, at] > 0, self.ref[0, at + 1], self.ref[0, at + 2], self.ref[0, at + 3]


def fill_table(table, counts_ref, chosen_ref, row_ref, col_ref, width, core, final):
    slots = chosen_ref.shape[1]
    assert slots == 6
    count = counts_ref[0]
    cols = [col_ref[0, chosen_ref[0, slot]] for slot in range(slots)]
    live = [slot < count for slot in range(slots)]
    ranks = []
    for slot in range(slots):
        rank = 0
        for other in range(slots):
            if other != slot:
                ahead = cols[other] <= cols[slot] if other < slot else cols[other] < cols[slot]
                rank = rank + jnp.where(live[other] & ahead, 1, 0)
        ranks.append(rank)

    def pick(values, place, backwards):
        total = 0
        for slot in range(slots):
            rank = count - 1 - ranks[slot] if backwards else ranks[slot]
            total = total + jnp.where(live[slot] & (rank == place), values[slot], 0)
        return total

    def widths(strips):
        return [
            0,
            strips[0],
            strips[1],
            jnp.maximum(strips[0] + strips[1], strips[2]),
            jnp.maximum(strips[0] + strips[3], strips[1] + strips[2]),
        ]

    wide_a = widths([pick(cols, place, False) for place in range(4)])
    wide_b = widths([width - pick(cols, place, True) for place in range(4)])
    best, lead = 4 * width, 0
    for number in range(5):
        other = count - number
        rest = 0
        for value in range(1, 5):
            rest = jnp.where(other == value, wide_b[value], rest)
        worst = jnp.where((other >= 0) & (other <= 4), jnp.maximum(wide_a[number], rest), 4 * width)
        lead = jnp.where(worst < best, number, lead)
        best = jnp.minimum(worst, best)

    def bins(number, backwards):
        at = [pick([1 + slot for slot in range(slots)], place, backwards) - 1 for place in range(4)]
        return {
            (0, 0): jnp.where(number >= 1, at[0], -1),
            (1, 0): jnp.where(number == 3, at[2], jnp.where(number >= 2, at[1], -1)),
            (0, 1): jnp.where(number == 4, at[3], jnp.where(number == 3, at[1], -1)),
            (1, 1): jnp.where(number == 4, at[2], -1),
        }

    bins_a = bins(jnp.where(final, 0, lead), False)
    bins_b = bins(jnp.where(final, 0, count - lead), True)
    for owner in range(2):
        for place in range(3):
            slot = 2 * place + owner
            whole = jnp.where(final & (slot < count), slot, -1)
            bins_a[owner, place] = jnp.where(final, whole, bins_a.get((owner, place), -1))
    for kind, places, table_of in (("A", 3, bins_a), ("B", 2, bins_b)):
        for owner in range(2):
            for place in range(places):
                slot = table_of[owner, place]
                position = chosen_ref[0, jnp.maximum(slot, 0)]
                index = 3 * owner + place if kind == "A" else 6 + 2 * owner + place
                at = ENTRY + FIELDS * index
                table[0, at] = jnp.where(slot >= 0, 1, 0)
                table[0, at + 1] = position
                table[0, at + 2] = row_ref[0, position]
                table[0, at + 3] = col_ref[0, position]
    for at in range(ENTRY):
        table[0, at] = 0
    table[0, 0] = core
    table[0, 1] = jnp.where(final, 0, best)
    for at in range(ENTRY + 10 * FIELDS, table.shape[1]):
        table[0, at] = 0


def pieces_of(reach):
    left, offset, found = reach - LANES, 0, []
    size = LANES
    while left:
        if left >= size:
            found.append((offset, size))
            offset, left = offset + size, left - size
        size //= 2
    return found


def fold(page, reach):
    rows = page.shape[0]
    main, extra = page[:, :LANES], page[:, LANES:]
    lane = columns((rows, LANES))
    parts = [main]
    for offset, size in pieces_of(reach):
        groups = LANES // size
        high = rows // groups
        total = None
        for group in range(groups):
            part = extra[group * high : (group + 1) * high]
            amount = (group * size - offset) % LANES
            part = pltpu.roll(part, amount, 1) if amount else part
            inside = lane[:high] >= group * size
            total = part if total is None else jnp.where(inside, part, total)
        parts.append(total)
    return jnp.concatenate(parts, 0)


def unfold(value, rows, reach):
    main, start = value[:rows], rows
    lane = columns((rows, LANES))
    extra = None
    for offset, size in pieces_of(reach):
        groups = LANES // size
        high = rows // groups
        part = value[start : start + high]
        start += high
        turned = []
        for group in range(groups):
            amount = (offset - group * size) % LANES
            turned.append(pltpu.roll(part, amount, 1) if amount else part)
        turned = jnp.concatenate(turned, 0)
        extra = turned if extra is None else jnp.where(lane >= offset, turned, extra)
    return jnp.concatenate([main, extra], 1)


def turn(value, amount, width):
    return pltpu.roll(value, lax.rem(amount, width), 1)


def rows_down(value, shift):
    span, width = value.shape
    tiles = value.reshape(span // EXTRA, EXTRA, width)
    rolled = pltpu.roll(tiles, lax.rem(EXTRA - shift, EXTRA), 1)
    row = lax.broadcasted_iota(jnp.int32, (span // EXTRA - 1, EXTRA, width), 1)
    moved = jnp.where(row < EXTRA - shift, rolled[:-1], rolled[1:])
    return moved.reshape(span - EXTRA, width)


def rows_up(value, shift):
    height, width = value.shape
    tiles = value.reshape(height // EXTRA, EXTRA, width)
    rolled = pltpu.roll(tiles, lax.rem(shift, EXTRA), 1)
    blank = jnp.zeros((1, EXTRA, width), value.dtype)
    row = lax.broadcasted_iota(jnp.int32, (height // EXTRA + 1, EXTRA, width), 1)
    moved = jnp.where(
        row >= shift, jnp.concatenate([rolled, blank], 0), jnp.concatenate([blank, rolled], 0)
    )
    return moved.reshape(height + EXTRA, width)


def columns(shape):
    return lax.broadcasted_iota(jnp.int32, shape, 1)


def patch_rows(ref, at, plane, row, height, width):
    step = EXTRA if ref.dtype == F32 else HALVES
    start = pl.multiple_of(jnp.minimum(row // step * step, height - width - step), step)
    value = ref[(*at, plane, pl.ds(start, width + step), slice(None))].astype(F32)
    shift = row - start
    if step > EXTRA:
        late = shift >= EXTRA
        value = jnp.where(late, value[EXTRA:], value[: value.shape[0] - EXTRA])
        shift = shift - jnp.where(late, EXTRA, 0)
    return rows_down(value, shift)


def place_pair(kind, reach, pair, first, second, width):
    (live0, _, _, col0), (live1, _, _, col1) = pair
    lane = columns((width, width))
    if kind == "A":
        mask0 = lane < col0
        mask1 = (lane >= reach - col1) & (lane < reach)
        second = turn(second, width + reach - col1, width)
    else:
        mask0 = (lane >= reach - width + col0) & (lane < reach)
        mask1 = lane < width - col1
        first = turn(first, reach, width) if reach < width else first
        second = turn(second, width - col1, width)
    return jnp.where(live0 & mask0, first, jnp.where(live1 & mask1, second, 0.0))


def first_kernel(
    reach, counts_ref, chosen_hbm, row_hbm, col_hbm, object_ref, own_ref, small_ref, straight_ref, cross_ref,
    chosen_ref, row_ref, col_ref, whole, sems, table_sems,
):
    height, width = object_ref.shape[2:]
    loads = [
        pltpu.make_async_copy(object_ref.at[0, plane], whole.at[plane], sems.at[plane]) for plane in range(2)
    ]
    scalars = zip((chosen_hbm, row_hbm, col_hbm), (chosen_ref, row_ref, col_ref))
    scalars = [
        pltpu.make_async_copy(source, target, table_sems.at[at]) for at, (source, target) in enumerate(scalars)
    ]
    for load in scalars + loads:
        load.start()
    for load in scalars:
        load.wait()
    core = lax.axis_index("cuts")
    final = lax.axis_index("tile") == lax.axis_size("tile") - 1
    fill_table(own_ref, counts_ref, chosen_ref, row_ref, col_ref, width, core, final)
    own = Table(own_ref)
    outs = (straight_ref, cross_ref)
    items = [[own.item("B", owner, place) for place in range(2)] for owner in (core, 1 - core)]
    tail = (HALVES, LANES)
    place = columns(tail)
    coded = jnp.zeros(tail, jnp.int32)
    for at in range(HALF):
        value = own_ref[0, at]
        coded = jnp.where(place == at, value // DIGIT, jnp.where(place == at + HALF, value % DIGIT, coded))
    for group in range(2):
        outs[group][4 * reach :] = coded.astype(F32).astype(BF16)
    for plane in range(2):
        loads[plane].wait()
        for group in range(2):
            first, second = [
                patch_rows(whole, (), plane, items[group][place][2], height, width) for place in range(2)
            ]
            page = place_pair("B", reach, items[group], first, second, width)
            outs[group][plane * 2 * reach : (plane + 1) * 2 * reach] = fold(page, reach).astype(BF16)
        small_ref[plane] = whole[plane].astype(BF16)


def levels_kernel(own_ref, intensity_ref, _, out_ref, levels, sems):
    own = Table(own_ref)
    copies = []
    for place in range(2):
        position = own.item("B", own_ref[0, 0], place)[1]
        copies.append(pltpu.make_async_copy(intensity_ref.at[0, position], levels.at[place], sems.at[place]))
        copies[place].start()
    for place in range(2):
        copies[place].wait()
        out_ref[place] = levels[place].astype(BF16)


def cos_sin(angle):
    half = 0.5 * angle
    square = half * half
    sine, cosine = 0.0, 0.0
    for power in range(13, -1, -1):
        factor = (-1.0) ** (power // 2) / math.factorial(power)
        if power % 2:
            sine = sine * square + factor
        else:
            cosine = cosine * square + factor
    sine = sine * half
    return 1.0 - 2.0 * sine * sine, 2.0 * sine * cosine


def angles_kernel(own_ref, self_ref, other_ref, _, out_ref):
    core = own_ref[0, 0]
    for source, ref in ((core, self_ref), (1 - core, other_ref)):
        out_ref[source, 0], out_ref[source, 1] = cos_sin(ref[0])


def pages_kernel(reach, own_ref, self_ref, other_ref, message_ref, _, out_ref, behind_ref, decoded, sem):
    height, width = self_ref.shape[1:]
    coded = message_ref[4 * reach :].astype(F32)
    value = coded * float(DIGIT) + pltpu.roll(coded, HALF, 1)
    decoded[...] = value[:EXTRA].astype(jnp.int32)
    copy = pltpu.make_async_copy(decoded, behind_ref, sem)
    copy.start()
    copy.wait()
    core = own_ref[0, 0]
    pair = [Table(behind_ref).item("A", core, place) for place in range(2)]
    for source, ref in ((core, self_ref), (1 - core, other_ref)):
        for plane in range(2):
            first, second = [patch_rows(ref, (), plane, pair[place][2], height, width) for place in range(2)]
            page = place_pair("A", reach, pair, first, second, width)
            out_ref[source, plane] = fold(page, reach).astype(BF16)


def parts_kernel(kind, behind_ref, own_ref, self_ref, other_ref, _, out_ref):
    height, width = self_ref.shape[1:]
    core = own_ref[0, 0]
    own = Table(own_ref)
    if kind == "A":
        items = [own.item("A", core, place) for place in range(2)]
    else:
        behind = Table(behind_ref)
        items = [behind.item("B", core, place) for place in range(2)] + [own.item("A", core, 2)]
    lane = columns((width, width))

    def write(place):
        _, _, row, col = items[place]
        mask = lane >= width - col if kind == "B" and place < 2 else lane < width - col
        for source, ref in ((core, self_ref), (1 - core, other_ref)):
            for plane in range(2):
                rolled = turn(patch_rows(ref, (), plane, row, height, width), width - col, width)
                out_ref[place, source, plane] = jnp.where(mask, rolled, 0.0).astype(BF16)

    write(0)
    write(1)
    if kind == "B":
        pl.when(items[2][0])(lambda: write(2))


def waves_kernel(kind, places, reach, *refs):
    behind_ref, own_ref = refs[:2]
    if kind == "A":
        page_ref, part_ref, phase, probe_ref, one_ref, two_ref, intensity_ref, _ = refs[2:10]
        rest = refs[10:]
    else:
        straight_ref, cross_ref, level_ref, part_ref, phase, probe_ref, one_ref, two_ref, intensity_ref = refs[2:11]
        rest = refs[11:]
    back_straight, back_cross, out_self, out_swap = rest[:4]
    patch, wave, grads, field, half, levels, level_sems = rest[4:]
    width = probe_ref.shape[-1]
    core = own_ref[0, 0]
    other = 1 - core
    table = Table(own_ref if kind == "A" else behind_ref)
    late = Table(own_ref).item("A", core, 2)
    lane = columns((width, width))

    def propagate(adjoint, which, finish):
        sign = -1.0 if adjoint else 1.0
        for item in range(2):
            product = jnp.dot(field[item], one_ref[...], preferred_element_type=F32)
            half[item, :width] = product[:, :width].astype(BF16)
            half[item, width:] = product[:, width:].astype(BF16)
        for item in range(2):
            spectrum = jnp.dot(two_ref[...], half[item], preferred_element_type=F32)
            real, imag = spectrum[:width], spectrum[width:]
            cosine, sine = phase[which, 0], sign * phase[which, 1]
            field[item, :, :width] = (real * cosine - imag * sine).astype(BF16)
            field[item, :, width:] = (real * sine + imag * cosine).astype(BF16)
        for item in range(2):
            product = jnp.dot(field[item], two_ref[...], preferred_element_type=F32)
            half[item, :width] = product[:, :width].astype(BF16)
            half[item, width:] = product[:, width:].astype(BF16)
        for item in range(2):
            result = jnp.dot(one_ref[...], half[item], preferred_element_type=F32)
            finish(item, result[:width], result[width:])

    def put(item, real, imag):
        field[item, :, :width] = real.astype(BF16)
        field[item, :, width:] = imag.astype(BF16)

    def one_pair(turn_index, _):
        entries = []
        for item in range(2):
            entry = table.item(kind, core, item)
            if places > 2:
                entry = tuple(jnp.where(turn_index > 0, b, a) for a, b in zip(entry, late))
            entries.append(entry)
        at = [jnp.minimum(2 * turn_index + item, places - 1) for item in range(2)]

        def levels_of(item):
            return pltpu.make_async_copy(
                intensity_ref.at[0, entries[item][1]], levels.at[item], level_sems.at[item]
            )

        if kind == "A":
            for item in range(2):
                levels_of(item).start()
        else:

            @pl.when(turn_index > 0)
            def _():
                for item in range(2):
                    levels_of(item).start()
                for item in range(2):
                    levels_of(item).wait()

            @pl.when(turn_index == 0)
            def _():
                for item in range(2):
                    levels[item] = level_ref[item].astype(F32)

        masks = []
        for item in range(2):
            col = entries[item][3]
            mask = lane >= width - col if kind == "A" else lane < width - col
            masks.append(mask & (turn_index == 0) if kind == "B" else mask)
        for at_source, source in enumerate((core, other)):
            for plane in range(2):
                if kind == "A":
                    page = page_ref[source, plane]
                else:
                    page = (straight_ref, cross_ref)[at_source][plane * 2 * reach : (plane + 1) * 2 * reach]
                page = unfold(page.astype(F32), width, reach)
                for item in range(2):
                    col = entries[item][3]
                    if item == 0:
                        foreign = turn(page, width - col if kind == "A" else 2 * width - reach - col, width)
                    elif kind == "A" and reach < width:
                        foreign = turn(page, width - reach, width)
                    else:
                        foreign = page
                    own = part_ref[at[item], source, plane].astype(F32)
                    patch[source, item, plane] = jnp.where(masks[item], foreign, own).astype(BF16)
        for item in range(2):
            left_re, left_im = probe_ref[0], probe_ref[1]
            right_re, right_im = patch[0, item, 0].astype(F32), patch[0, item, 1].astype(F32)
            put(item, left_re * right_re - left_im * right_im, left_re * right_im + left_im * right_re)

        def after_first(item, real, imag):
            real, imag = real.astype(BF16), imag.astype(BF16)
            wave[item, 0] = real
            wave[item, 1] = imag
            real, imag = real.astype(F32), imag.astype(F32)
            right_re, right_im = patch[1, item, 0].astype(F32), patch[1, item, 1].astype(F32)
            put(item, real * right_re - imag * right_im, real * right_im + imag * right_re)

        propagate(False, 0, after_first)
        if kind == "A":
            for item in range(2):
                levels_of(item).wait()

        def after_second(item, real, imag):
            real, imag = real.astype(BF16).astype(F32), imag.astype(BF16).astype(F32)
            gain = 2.0 * (real * real + imag * imag - levels[item])
            gain = jnp.where(entries[item][0], gain, 0.0)
            put(item, gain * real, gain * imag)

        propagate(False, 1, after_second)

        def before_second(item, real, imag):
            left_re, left_im = wave[item, 0].astype(F32), wave[item, 1].astype(F32)
            grads[1, item, 0] = (left_re * real + left_im * imag).astype(BF16)
            grads[1, item, 1] = (left_re * imag - left_im * real).astype(BF16)
            left_re, left_im = patch[1, item, 0].astype(F32), patch[1, item, 1].astype(F32)
            put(item, left_re * real + left_im * imag, left_re * imag - left_im * real)

        propagate(True, 1, before_second)

        def before_first(item, real, imag):
            left_re, left_im = probe_ref[0], probe_ref[1]
            grads[0, item, 0] = (left_re * real + left_im * imag).astype(BF16)
            grads[0, item, 1] = (left_re * imag - left_im * real).astype(BF16)

        propagate(True, 0, before_first)
        for item in range(2):
            out_self[at[item]] = grads[core, item]
            out_swap[at[item]] = grads[other, item]

        @pl.when(turn_index == 0)
        def _():
            (live0, _, _, col0), (live1, _, _, col1) = entries
            if kind == "A":
                mask0 = lane < col0
                mask1 = (lane >= reach - col1) & (lane < reach)
            else:
                mask0 = (lane >= reach - width + col0) & (lane < reach)
                mask1 = lane < width - col1
            for source, out_ref in ((core, back_straight), (other, back_cross)):
                for plane in range(2):
                    first = grads[source, 0, plane].astype(F32)
                    first = turn(first, col0 if kind == "A" else col0 + reach, width)
                    second = grads[source, 1, plane].astype(F32)
                    if kind == "A" and reach < width:
                        second = turn(second, reach, width)
                    page = jnp.where(live0 & mask0, first, jnp.where(live1 & mask1, second, 0.0))
                    out_ref[plane] = fold(page, reach).astype(BF16)

        return 0

    if places > 2:
        turns = jnp.where(late[0], 2, 1)
        lax.fori_loop(0, turns, one_pair, 0)
    else:
        one_pair(jnp.int32(0), 0)


def add_piece(total, plane, entry, in_next, piece, amount):
    live, _, row, col = entry
    height, width = total.shape[1:]

    @pl.when(live)
    def _():
        lane = columns((width, width))
        mask = lane < col if in_next else lane >= col
        start = pl.multiple_of(jnp.minimum(row // EXTRA * EXTRA, height - width - EXTRA), EXTRA)
        rows = pl.ds(start, width + EXTRA)
        value = piece()
        if amount is not None:
            value = turn(value, amount, width)
        moved = rows_up(jnp.where(mask, value, 0.0), row - start)
        total[plane, rows, :] = total[plane, rows, :] + moved


def gather_kernel(reach, own_ref, behind_ref, b_self, b_swap, b_back, b_back_cross, a_self, out_ref):
    width = out_ref.shape[-1]
    core = own_ref[0, 0]
    other = 1 - core
    own, behind = Table(own_ref), Table(behind_ref)
    total = out_ref.at[0]
    out_ref[...] = jnp.zeros_like(out_ref)

    def add(plane, entry, in_next, ref, place):
        add_piece(total, plane, entry, in_next, lambda: ref[place, plane].astype(F32), entry[3])

    for plane in range(2):
        for owner, ref in ((core, b_self), (other, b_swap)):
            for place in range(2):
                add(plane, behind.item("B", owner, place), True, ref, place)
            add(plane, own.item("A", owner, 2), False, ref, 2)
        for place in range(2):
            add(plane, own.item("A", core, place), False, a_self, place)
        for owner, ref in ((core, b_back), (other, b_back_cross)):
            page = unfold(ref[plane].astype(F32), width, reach)
            for place in range(2):
                entry = own.item("B", owner, place)
                amount = (width - reach if reach < width else None) if place == 0 else entry[3]
                add_piece(total, plane, entry, False, lambda: page, amount)


def finish_kernel(reach, own_ref, behind_ref, canvas_ref, a_swap, a_back, a_back_cross, out_ref, total, sems):
    width = canvas_ref.shape[-1]
    core = own_ref[0, 0]
    other = 1 - core
    own, behind = Table(own_ref), Table(behind_ref)
    copies = []
    for plane in range(2):
        total[plane] = canvas_ref[0, plane]
        for place in range(2):
            entry = own.item("A", other, place)
            add_piece(total, plane, entry, False, lambda: a_swap[place, plane].astype(F32), entry[3])
        for owner, ref in ((core, a_back), (other, a_back_cross)):
            page = unfold(ref[plane].astype(F32), width, reach)
            for place in range(2):
                entry = behind.item("A", owner, place)
                amount = None if place == 0 else width - reach + entry[3]
                add_piece(total, plane, entry, True, lambda: page, amount)
        copy = pltpu.make_async_copy(total.at[plane], out_ref.at[0, plane], sems.at[plane])
        copy.start()
        copies.append(copy)
    for copy in copies:
        copy.wait()


def on_device(
    object_slices, probe_field, slice_phase, intensity, counts, chosen, row_offset, column_offset
):
    height, breadth = object_slices.shape[2:]
    width = probe_field.shape[-1]
    assert breadth == width and object_slices.shape[0] == 1
    one, two = make_tables(width)

    smem = pl.BlockSpec(memory_space=pltpu.SMEM)
    vmem = pl.BlockSpec(memory_space=pltpu.VMEM)
    anywhere = pl.BlockSpec(memory_space=pl.ANY)
    hbm = pl.BlockSpec(memory_space=pltpu.HBM)
    planes = lambda *lead: jax.ShapeDtypeStruct((*lead, width, width), BF16)
    dma = lambda *shape: pltpu.SemaphoreType.DMA(shape)
    whole = jax.ShapeDtypeStruct(object_slices.shape, F32)
    still = lambda value: pltpu.with_memory_space_constraint(value, pltpu.HBM)

    def call(kernel, name, operands, out_shape, scratch, cost=0, limit=LIMIT, out_specs=None):
        return pl.pallas_call(
            kernel,
            out_shape=out_shape,
            in_specs=[spec for spec, _ in operands],
            out_specs=out_specs or jax.tree.map(lambda _: vmem, out_shape),
            scratch_shapes=scratch,
            compiler_params=pltpu.CompilerParams(vmem_limit_bytes=limit),
            cost_estimate=pl.CostEstimate(flops=cost * 10**9, bytes_accessed=cost * 3 * 10**6, transcendentals=0),
            name=name,
        )(*[value for _, value in operands])

    def run(reach):
        folded = lambda *lead: jax.ShapeDtypeStruct((*lead, 2 * reach, LANES), BF16)
        message = jax.ShapeDtypeStruct((4 * reach + HALVES, LANES), BF16)

        def parts(kind, idx, after):
            operands = [(smem, idx), (smem, own), (vmem, small), (vmem, small_other), (anywhere, after)]
            shape = planes(2 if kind == "A" else 3, 2, 2)
            return call(functools.partial(parts_kernel, kind), "parts_" + kind.lower(), operands, shape, [])

        def waves(kind, pages, part, *after):
            count = 2 if kind == "A" else 3
            operands = [(smem, behind), (smem, own)]
            operands += [(vmem, value) for value in (*pages, part, turned, probe_field, one, two)]
            operands += [(hbm, still(intensity))] + [(anywhere, value) for value in after]
            scratch = [
                pltpu.VMEM((2, 2, 2, width, width), BF16),
                pltpu.VMEM((2, 2, width, width), BF16),
                pltpu.VMEM((2, 2, 2, width, width), BF16),
                pltpu.VMEM((2, width, 2 * width), BF16),
                pltpu.VMEM((2, 2 * width, width), BF16),
                pltpu.VMEM((2, width, width), F32),
                dma(2),
            ]
            shapes = [folded(2), folded(2), planes(count, 2), planes(count, 2)]
            kernel = functools.partial(waves_kernel, kind, count, reach)
            return call(kernel, "waves_" + kind.lower(), operands, shapes, scratch, 7)

        phase_other = send(slice_phase, 1, 0)
        scalars = (chosen, row_offset, column_offset)
        own, small, b_straight, b_cross = call(
            functools.partial(first_kernel, reach),
            "first",
            [(smem, counts)] + [(hbm, still(value)) for value in scalars]
            + [(hbm, still(object_slices))],
            [
                jax.ShapeDtypeStruct((1, HALF), jnp.int32),
                jax.ShapeDtypeStruct(object_slices.shape[1:], BF16),
                message,
                message,
            ],
            [pltpu.SMEM(value.shape, value.dtype) for value in scalars]
            + [pltpu.VMEM((2, height, width), F32), dma(2), dma(3)],
            out_specs=[smem, vmem, vmem, vmem],
        )
        small_other = send(small, 1, 0)
        level = call(
            levels_kernel,
            "levels",
            [(smem, own), (hbm, still(intensity)), (anywhere, b_cross)],
            planes(2),
            [pltpu.VMEM((2, width, width), F32), dma(2)],
        )
        turned = call(
            angles_kernel,
            "angles",
            [(smem, own), (vmem, slice_phase), (vmem, phase_other), (anywhere, level)],
            jax.ShapeDtypeStruct((2, 2, width, width), F32),
            [],
        )
        b_straight, b_cross = send(b_straight, 0, 1), send(b_cross, 1, 1)
        level = send(level, 0, 1)
        a_part = parts("A", own, turned)
        page, behind = call(
            functools.partial(pages_kernel, reach),
            "pages",
            [(smem, own), (vmem, small), (vmem, small_other), (vmem, b_straight), (anywhere, a_part)],
            [folded(2, 2), jax.ShapeDtypeStruct((EXTRA, LANES), jnp.int32)],
            [pltpu.VMEM((EXTRA, LANES), jnp.int32), pltpu.SemaphoreType.DMA(())],
            out_specs=[vmem, smem],
        )
        b_part = parts("B", behind, page)
        page = send(page, 0, -1)
        b_back, b_back_cross, b_self, b_swap = waves("B", (b_straight, b_cross, level), b_part)
        b_swap = send(b_swap, 1, 0)
        b_back, b_back_cross = send(b_back, 0, -1), send(b_back_cross, 1, -1)
        a_back, a_back_cross, a_self, a_swap = waves("A", (page,), a_part, b_self)
        a_back, a_back_cross = send(a_back, 0, 1), send(a_back_cross, 1, 1)
        a_swap = send(a_swap, 1, 0)
        canvas = call(
            functools.partial(gather_kernel, reach),
            "gather",
            [(smem, own), (smem, behind)]
            + [(vmem, value) for value in (b_self, b_swap, b_back, b_back_cross, a_self)],
            whole,
            [],
            cost=10,
        )
        return own, behind, canvas, a_swap, a_back, a_back_cross

    def finish(reach, own, behind, *values):
        return call(
            functools.partial(finish_kernel, reach),
            "finish",
            [(smem, own), (smem, behind)] + [(vmem, value) for value in values],
            whole,
            [pltpu.VMEM((2, height, width), F32), dma(2)],
            out_specs=hbm,
        )

    reach = REACH
    narrow = run(reach)
    return finish(reach, *narrow)


def solution(mesh):
    return jax.shard_map(
        on_device,
        mesh=mesh,
        in_specs=(
            P("cuts", None, None, "tile"),
            P(),
            P("cuts", None, None),
            P("tile", None, None, None),
            P("tile"),
            P("tile", None),
            P("tile", None),
            P("tile", None),
        ),
        out_specs=P("cuts", None, None, "tile"),
        check_vma=False,
    )
```

time: 72.1 us -> 68.9 us (0.956)
  local copies, waits for them, and re-layouts: 3.51 us -> 0.02 us
  Pallas kernels: 32 us -> 28.6 us
  starting transfers between devices: 24.4 us -> 27.7 us
    unnamed x16 -> x8, local copies, waits for them, and re-layouts: 3.51 us -> 0.02 us
    pallas_call x8 -> x10, Pallas kernels: 32 us -> 28.6 us  [call(): pl.pallas_call(kernel, out_shape=out_shape, in_specs=[spec for spec, _ in...]
    ppermute x11 -> x12, starting transfers between devices: 24.4 us -> 27.7 us  [send(): return lax.ppermute(value, ('cuts', 'tile'), pairs)]
    ppermute x11 -> x12, waiting for transfers between devices: 10.4 us -> 10.9 us  [send(): return lax.ppermute(value, ('cuts', 'tile'), pairs)]
  transfers between devices with their start and end apart: 11 -> 12, of which waited for: 3 -> 3; matrix products, arithmetic and copies ran while one was open for 0% -> 0% of each run, Pallas kernels for 34% -> 33%
where the time goes in v3:
time: 68.9 us; the launch traced here: 68.3 us
  Pallas kernels  28.6 us (42%)
  starting transfers between devices  27.7 us (40%)
  waiting for transfers between devices  10.9 us (16%)
  between operations  1.05 us (2%)
    pallas_call x10, Pallas kernels, call(): pl.pallas_call(kernel, out_shape=out_shape, in_specs=[spec for spec, _ in...  28.6 us
    ppermute x12, starting transfers between devices, send(): return lax.ppermute(value, ('cuts', 'tile'), pairs)  27.7 us
    ppermute x12, waiting for transfers between devices, send(): return lax.ppermute(value, ('cuts', 'tile'), pairs)  10.9 us
  transfers between devices with their start and end apart: 12, of which 3 were waited for; matrix products, arithmetic and copies ran while one was open for 0% of the time, Pallas kernels for 33%

profile of v3, /device:TPU:17, one launch (start us, length us, event | category | flops | bytes accessed | tf_op | source)
XLA Modules:
  0.0 68.3 jit_solution(4987275262792109194)
XLA Ops:
  0.7 0.0 copy-start
  0.7 2.9 %first.1 = (s32[1,64]{1,0:T(1,128)S(1)}, bf16[2,2048,256]{2,1,0:T(8,128)(2,1)S(1)}, bf16[1040,128]{1,0:T(8,128)(2,1)S(1)}, bf16[1040,128]{1,0:T(8,128)(2,1)S(1)}) custom-call(s32[1]{0:T(128)S(6)} %copy.11.counts_ref, s32[1,6]{1,0:T(1,128)} %chosen_hbm.1, s32[1,8]{1,0:T(1,128)} %row_hbm.1, s32[1,8]{1,0:T(1,128)} %col_hbm.1, f32[1,2,2048,256]{3,2,1,0:T(8,128)} %object_ref.1), custom_call_target="tpu_custom_call" | custom-call | tf_op jit(solution)/shard_map/first/pallas_call | solution.py:611
  3.6 0.7 %collective-permute-start = (bf16[2,2048,256]{2,1,0:T(8,128)(2,1)S(1)}, bf16[2,2048,256]{2,1,0:T(8,128)(2,1)S(1)}, u32[]{:S(2)}, u32[]{:S(2)}) collective-permute-start(bf16[2,2048,256]{2,1,0:T(8,128)(2,1)S(1)} %get-tuple-element.20.self_ref), channel_id=1, source_target_pairs={{0,16},{1,17},{2,18},{3,19},{4,20},{5,21},{6,22},{7,23},{8,24},{9,... | collective-permute-start | bytes 6291464 | tf_op jit(solution)/shard_map/ppermute | solution.py:30
  4.3 3.1 %collective-permute-start.1 = (bf16[1040,128]{1,0:T(8,128)(2,1)S(1)}, bf16[1040,128]{1,0:T(8,128)(2,1)S(1)}, u32[]{:S(2)}, u32[]{:S(2)}) collective-permute-start(bf16[1040,128]{1,0:T(8,128)(2,1)S(1)} %get-tuple-element.21), channel_id=1, source_target_pairs={{0,1},{1,2},{2,3},{3,4},{4,5},{5,6},{6,7},{7,8},{8,9},{9,10},{10,1... | collective-permute-start | bytes 798728 | tf_op jit(solution)/shard_map/ppermute | solution.py:30
  7.4 3.3 %collective-permute-start.3 = (bf16[1040,128]{1,0:T(8,128)(2,1)S(1)}, bf16[1040,128]{1,0:T(8,128)(2,1)S(1)}, u32[]{:S(2)}, u32[]{:S(2)}) collective-permute-start(bf16[1040,128]{1,0:T(8,128)(2,1)S(1)} %get-tuple-element.22._), channel_id=1, source_target_pairs={{0,17},{1,18},{2,19},{3,20},{4,21},{5,22},{6,23},{7,24},{8,25},{9,... | collective-permute-start | bytes 798728 | tf_op jit(solution)/shard_map/ppermute | solution.py:30
  10.8 0.0 copy-done
  10.8 0.3 collective-permute-start.2
  11.0 1.6 %levels.1._ = bf16[2,256,256]{2,1,0:T(8,128)(2,1)S(1)} custom-call(s32[1,64]{1,0:T(1,128)S(1)} %get-tuple-element.19.own_ref.behind_ref.refs_1_, f32[1,8,256,256]{3,2,1,0:T(8,128)} %refs_8_.2, bf16[1040,128]{1,0:T(8,128)(2,1)S(1)} %get-tuple-element.22._), custom_call_target="tpu_custom_call" | custom-call | tf_op jit(solution)/shard_map/levels/pallas_call | solution.py:611
  12.6 3.1 %collective-permute-start.4 = (bf16[2,256,256]{2,1,0:T(8,128)(2,1)S(1)}, bf16[2,256,256]{2,1,0:T(8,128)(2,1)S(1)}, u32[]{:S(2)}, u32[]{:S(2)}) collective-permute-start(bf16[2,256,256]{2,1,0:T(8,128)(2,1)S(1)} %levels.1._), channel_id=1, source_target_pairs={{0,1},{1,2},{2,3},{3,4},{4,5},{5,6},{6,7},{7,8},{8,9},{9,10},{10,1... | collective-permute-start | bytes 786440 | tf_op jit(solution)/shard_map/ppermute | solution.py:30
  15.8 0.0 collective-permute-done.2.other_ref
  15.8 1.2 %angles.1._.refs_6_.refs_4_ = f32[2,2,256,256]{3,2,1,0:T(8,128)S(1)} custom-call(s32[1,64]{1,0:T(1,128)S(1)} %get-tuple-element.19.own_ref.behind_ref.refs_1_, f32[1,256,256]{2,1,0:T(8,128)S(1)} %copy-done, f32[1,256,256]{2,1,0:T(8,128)S(1)} %collective-permute-done.2.other_ref, bf16[2,256,256]{2,1,0:T(8,128)(2,1)S(1)} %levels.1._), custom_call_target="tpu_custom_call" | custom-call | tf_op jit(solution)/shard_map/angles/pallas_call | solution.py:611
  17.0 0.0 collective-permute-done.other_ref
  17.0 1.2 %parts_a.1._.refs_3_ = bf16[2,2,2,256,256]{4,3,2,1,0:T(8,128)(2,1)S(1)} custom-call(s32[1,64]{1,0:T(1,128)S(1)} %get-tuple-element.19.own_ref.behind_ref.refs_1_, s32[1,64]{1,0:T(1,128)S(1)} %get-tuple-element.19.own_ref.behind_ref.refs_1_, bf16[2,2048,256]{2,1,0:T(8,128)(2,1)S(1)} %get-tuple-element.20.self_ref, ...), custom_call_target="tpu_custom_call" | custom-call | tf_op jit(solution)/shard_map/parts_a/pallas_call | solution.py:611
  18.2 0.0 collective-permute-done.1.message_ref.refs_2_
  18.2 2.0 %pages.1 = (bf16[2,2,512,128]{3,2,1,0:T(8,128)(2,1)S(1)}, s32[8,128]{1,0:T(8,128)S(1)}) custom-call(s32[1,64]{1,0:T(1,128)S(1)} %get-tuple-element.19.own_ref.behind_ref.refs_1_, bf16[2,2048,256]{2,1,0:T(8,128)(2,1)S(1)} %get-tuple-element.20.self_ref, bf16[2,2048,256]{2,1,0:T(8,128)(2,1)S(1)} %collective-permute-done.other_ref, ...), custom_call_target="tpu_custom_call" | custom-call | tf_op jit(solution)/shard_map/pages/pallas_call | solution.py:611
  20.2 4.0 %collective-permute-start.8 = (bf16[2,2,512,128]{3,2,1,0:T(8,128)(2,1)S(1)}, bf16[2,2,512,128]{3,2,1,0:T(8,128)(2,1)S(1)}, u32[]{:S(2)}, u32[]{:S(2)}) collective-permute-start(bf16[2,2,512,128]{3,2,1,0:T(8,128)(2,1)S(1)} %get-tuple-element.24._), channel_id=1, source_target_pairs={{1,0},{2,1},{3,2},{4,3},{5,4},{6,5},{7,6},{8,7},{9,8},{10,9},{11,1... | collective-permute-start | bytes 1572872 | tf_op jit(solution)/shard_map/ppermute | solution.py:30
  24.2 0.0 copy-start.1
  24.2 0.0 copy-start.2
  24.2 0.0 copy-start.3
  24.2 1.3 %parts_b.1.refs_5_ = bf16[3,2,2,256,256]{4,3,2,1,0:T(8,128)(2,1)S(1)} custom-call(s32[8,128]{1,0:T(8,128)S(1)} %get-tuple-element.23.behind_ref.refs_0_, s32[1,64]{1,0:T(1,128)S(1)} %get-tuple-element.19.own_ref.behind_ref.refs_1_, bf16[2,2048,256]{2,1,0:T(8,128)(2,1)S(1)} %get-tuple-element.20.self_ref, ...), custom_call_target="tpu_custom_call" | custom-call | tf_op jit(solution)/shard_map/parts_b/pallas_call | solution.py:611
  25.5 1.9 %collective-permute-done.4.refs_4_ = bf16[2,256,256]{2,1,0:T(8,128)(2,1)S(1)} collective-permute-done((bf16[2,256,256]{2,1,0:T(8,128)(2,1)S(1)}, bf16[2,256,256]{2,1,0:T(8,128)(2,1)S(1)}, u32[]{:S(2)}, u32[]{:S(2)}) %collective-permute-start.4) | collective-permute-done | bytes 262176 | tf_op jit(solution)/shard_map/ppermute | solution.py:30
  27.3 0.0 collective-permute-done.3.refs_3_
  27.3 0.0 copy-done.1
  27.3 0.0 copy-done.2
  27.3 0.0 copy-done.3
  27.4 6.8 %waves_b.1 = (bf16[2,512,128]{2,1,0:T(8,128)(2,1)S(1)}, bf16[2,512,128]{2,1,0:T(8,128)(2,1)S(1)}, bf16[3,2,256,256]{3,2,1,0:T(8,128)(2,1)S(1)}, bf16[3,2,256,256]{3,2,1,0:T(8,128)(2,1)S(1)}) custom-call(s32[8,128]{1,0:T(8,128)S(1)} %get-tuple-element.23.behind_ref.refs_0_, s32[1,64]{1,0:T(1,128)S(1)} %get-tuple-element.19.own_ref.behind_ref.refs_1_, ...), custom_call_target="tpu_custom_call" | custom-call | flops 7000000000 | bytes 21000000 | tf_op jit(solution)/shard_map/waves_b/pallas_call | solution.py:611
  34.2 1.0 %collective-permute-start.5 = (bf16[3,2,256,256]{3,2,1,0:T(8,128)(2,1)S(1)}, bf16[3,2,256,256]{3,2,1,0:T(8,128)(2,1)S(1)}, u32[]{:S(2)}, u32[]{:S(2)}) collective-permute-start(bf16[3,2,256,256]{3,2,1,0:T(8,128)(2,1)S(1)} %get-tuple-element.26), channel_id=1, source_target_pairs={{0,16},{1,17},{2,18},{3,19},{4,20},{5,21},{6,22},{7,23},{8,24},{9,... | collective-permute-start | bytes 2359304 | tf_op jit(solution)/shard_map/ppermute | solution.py:30
  35.2 2.5 %collective-permute-start.6 = (bf16[2,512,128]{2,1,0:T(8,128)(2,1)S(1)}, bf16[2,512,128]{2,1,0:T(8,128)(2,1)S(1)}, u32[]{:S(2)}, u32[]{:S(2)}) collective-permute-start(bf16[2,512,128]{2,1,0:T(8,128)(2,1)S(1)} %get-tuple-element.27), channel_id=1, source_target_pairs={{1,0},{2,1},{3,2},{4,3},{5,4},{6,5},{7,6},{8,7},{9,8},{10,9},{11,1... | collective-permute-start | bytes 786440 | tf_op jit(solution)/shard_map/ppermute | solution.py:30
  37.6 3.4 %collective-permute-start.7 = (bf16[2,512,128]{2,1,0:T(8,128)(2,1)S(1)}, bf16[2,512,128]{2,1,0:T(8,128)(2,1)S(1)}, u32[]{:S(2)}, u32[]{:S(2)}) collective-permute-start(bf16[2,512,128]{2,1,0:T(8,128)(2,1)S(1)} %get-tuple-element.28), channel_id=1, source_target_pairs={{1,16},{2,17},{3,18},{4,19},{5,20},{6,21},{7,22},{8,23},{9,24},{10... | collective-permute-start | bytes 786440 | tf_op jit(solution)/shard_map/ppermute | solution.py:30
  41.1 0.0 collective-permute-done.8.refs_2_
  41.1 6.9 %waves_a.1 = (bf16[2,512,128]{2,1,0:T(8,128)(2,1)S(1)}, bf16[2,512,128]{2,1,0:T(8,128)(2,1)S(1)}, bf16[2,2,256,256]{3,2,1,0:T(8,128)(2,1)S(1)}, bf16[2,2,256,256]{3,2,1,0:T(8,128)(2,1)S(1)}) custom-call(s32[8,128]{1,0:T(8,128)S(1)} %get-tuple-element.23.behind_ref.refs_0_, s32[1,64]{1,0:T(1,128)S(1)} %get-tuple-element.19.own_ref.behind_ref.refs_1_, ...), custom_call_target="tpu_custom_call" | custom-call | flops 7000000000 | bytes 21000000 | tf_op jit(solution)/shard_map/waves_a/pallas_call | solution.py:611
  48.0 2.2 %collective-permute-start.10 = (bf16[2,512,128]{2,1,0:T(8,128)(2,1)S(1)}, bf16[2,512,128]{2,1,0:T(8,128)(2,1)S(1)}, u32[]{:S(2)}, u32[]{:S(2)}) collective-permute-start(bf16[2,512,128]{2,1,0:T(8,128)(2,1)S(1)} %get-tuple-element.31), channel_id=1, source_target_pairs={{0,1},{1,2},{2,3},{3,4},{4,5},{5,6},{6,7},{7,8},{8,9},{9,10},{10,1... | collective-permute-start | bytes 786440 | tf_op jit(solution)/shard_map/ppermute | solution.py:30
  50.2 4.1 %collective-permute-start.11 = (bf16[2,512,128]{2,1,0:T(8,128)(2,1)S(1)}, bf16[2,512,128]{2,1,0:T(8,128)(2,1)S(1)}, u32[]{:S(2)}, u32[]{:S(2)}) collective-permute-start(bf16[2,512,128]{2,1,0:T(8,128)(2,1)S(1)} %get-tuple-element.32), channel_id=1, source_target_pairs={{0,17},{1,18},{2,19},{3,20},{4,21},{5,22},{6,23},{7,24},{8,25},{9,... | collective-permute-start | bytes 786440 | tf_op jit(solution)/shard_map/ppermute | solution.py:30
  54.3 0.0 collective-permute-done.6.b_back
  54.3 0.1 collective-permute-start.9
  54.4 0.0 collective-permute-done.7.b_back_cross
  54.4 0.0 collective-permute-done.5.b_swap
  54.4 1.9 %gather.1.canvas_ref = f32[1,2,2048,256]{3,2,1,0:T(8,128)S(1)} custom-call(s32[1,64]{1,0:T(1,128)S(1)} %get-tuple-element.19.own_ref.behind_ref.refs_1_, s32[8,128]{1,0:T(8,128)S(1)} %get-tuple-element.23.behind_ref.refs_0_, bf16[3,2,256,256]{3,2,1,0:T(8,128)(2,1)S(1)} %get-tuple-element.25.refs_9_.b_self, ...), custom_call_target="tpu_custom_call" | custom-call | flops 10000000000 | bytes 30000000 | tf_op jit(solution)/shard_map/gather/pallas_call | solution.py:611
  56.3 3.1 %collective-permute-done.10.a_back = bf16[2,512,128]{2,1,0:T(8,128)(2,1)S(1)} collective-permute-done((bf16[2,512,128]{2,1,0:T(8,128)(2,1)S(1)}, bf16[2,512,128]{2,1,0:T(8,128)(2,1)S(1)}, u32[]{:S(2)}, u32[]{:S(2)}) %collective-permute-start.10) | collective-permute-done | bytes 262176 | tf_op jit(solution)/shard_map/ppermute | solution.py:30
  59.4 5.9 %collective-permute-done.11.a_back_cross = bf16[2,512,128]{2,1,0:T(8,128)(2,1)S(1)} collective-permute-done((bf16[2,512,128]{2,1,0:T(8,128)(2,1)S(1)}, bf16[2,512,128]{2,1,0:T(8,128)(2,1)S(1)}, u32[]{:S(2)}, u32[]{:S(2)}) %collective-permute-start.11) | collective-permute-done | bytes 262176 | tf_op jit(solution)/shard_map/ppermute | solution.py:30
  65.3 0.0 collective-permute-done.9.a_swap
  65.3 2.8 %finish.1 = f32[1,2,2048,256]{3,2,1,0:T(8,128)} custom-call(s32[1,64]{1,0:T(1,128)S(1)} %get-tuple-element.19.own_ref.behind_ref.refs_1_, s32[8,128]{1,0:T(8,128)S(1)} %get-tuple-element.23.behind_ref.refs_0_, f32[1,2,2048,256]{3,2,1,0:T(8,128)S(1)} %gather.1.canvas_ref, bf16[2,2,256,256]{3,2,1,0:T(8,128)(2,1)S(1)} %collective-permute-done.9.a_swap, ...), custom_call_target="tpu_custom_call" | custom-call | tf_op jit(solution)/shard_map/finish/pallas_call | solution.py:611
Async XLA Ops:
  0.7 10.1 %copy-start = (f32[1,256,256]{2,1,0:T(8,128)S(1)}, f32[1,256,256]{2,1,0:T(8,128)}, u32[]{:S(2)}) copy-start(f32[1,256,256]{2,1,0:T(8,128)} %self_ref.1) | copy-start | bytes 786436
  3.6 13.4 %collective-permute-start = (bf16[2,2048,256]{2,1,0:T(8,128)(2,1)S(1)}, bf16[2,2048,256]{2,1,0:T(8,128)(2,1)S(1)}, u32[]{:S(2)}, u32[]{:S(2)}) collective-permute-start(bf16[2,2048,256]{2,1,0:T(8,128)(2,1)S(1)} %get-tuple-element.20.self_ref), channel_id=1, source_target_pairs={{0,16},{1,17},{2,18},{3,19},{4,20},{5,21},{6,22},{7,23},{8,24},{9,... | collective-permute-start | bytes 6291464 | tf_op jit(solution)/shard_map/ppermute | solution.py:30
  4.3 13.9 %collective-permute-start.1 = (bf16[1040,128]{1,0:T(8,128)(2,1)S(1)}, bf16[1040,128]{1,0:T(8,128)(2,1)S(1)}, u32[]{:S(2)}, u32[]{:S(2)}) collective-permute-start(bf16[1040,128]{1,0:T(8,128)(2,1)S(1)} %get-tuple-element.21), channel_id=1, source_target_pairs={{0,1},{1,2},{2,3},{3,4},{4,5},{5,6},{6,7},{7,8},{8,9},{9,10},{10,1... | collective-permute-start | bytes 798728 | tf_op jit(solution)/shard_map/ppermute | solution.py:30
  7.4 19.9 %collective-permute-start.3 = (bf16[1040,128]{1,0:T(8,128)(2,1)S(1)}, bf16[1040,128]{1,0:T(8,128)(2,1)S(1)}, u32[]{:S(2)}, u32[]{:S(2)}) collective-permute-start(bf16[1040,128]{1,0:T(8,128)(2,1)S(1)} %get-tuple-element.22._), channel_id=1, source_target_pairs={{0,17},{1,18},{2,19},{3,20},{4,21},{5,22},{6,23},{7,24},{8,25},{9,... | collective-permute-start | bytes 798728 | tf_op jit(solution)/shard_map/ppermute | solution.py:30
  10.8 5.0 %collective-permute-start.2 = (f32[1,256,256]{2,1,0:T(8,128)S(1)}, f32[1,256,256]{2,1,0:T(8,128)S(1)}, u32[]{:S(2)}, u32[]{:S(2)}) collective-permute-start(f32[1,256,256]{2,1,0:T(8,128)S(1)} %copy-done), channel_id=1, source_target_pairs={{0,16},{1,17},{2,18},{3,19},{4,20},{5,21},{6,22},{7,23},{8,24},{9,... | collective-permute-start | bytes 786440 | tf_op jit(solution)/shard_map/ppermute | solution.py:30
  12.6 14.7 %collective-permute-start.4 = (bf16[2,256,256]{2,1,0:T(8,128)(2,1)S(1)}, bf16[2,256,256]{2,1,0:T(8,128)(2,1)S(1)}, u32[]{:S(2)}, u32[]{:S(2)}) collective-permute-start(bf16[2,256,256]{2,1,0:T(8,128)(2,1)S(1)} %levels.1._), channel_id=1, source_target_pairs={{0,1},{1,2},{2,3},{3,4},{4,5},{5,6},{6,7},{7,8},{8,9},{9,10},{10,1... | collective-permute-start | bytes 786440 | tf_op jit(solution)/shard_map/ppermute | solution.py:30
  20.2 20.9 %collective-permute-start.8 = (bf16[2,2,512,128]{3,2,1,0:T(8,128)(2,1)S(1)}, bf16[2,2,512,128]{3,2,1,0:T(8,128)(2,1)S(1)}, u32[]{:S(2)}, u32[]{:S(2)}) collective-permute-start(bf16[2,2,512,128]{3,2,1,0:T(8,128)(2,1)S(1)} %get-tuple-element.24._), channel_id=1, source_target_pairs={{1,0},{2,1},{3,2},{4,3},{5,4},{6,5},{7,6},{8,7},{9,8},{10,9},{11,1... | collective-permute-start | bytes 1572872 | tf_op jit(solution)/shard_map/ppermute | solution.py:30
  24.2 3.2 %copy-start.1 = (f32[2,256,256]{2,1,0:T(8,128)S(1)}, f32[2,256,256]{2,1,0:T(8,128)}, u32[]{:S(2)}) copy-start(f32[2,256,256]{2,1,0:T(8,128)} %refs_5_.1) | copy-start | bytes 1572868
  24.2 3.2 %copy-start.2 = (bf16[512,512]{1,0:T(8,128)(2,1)S(1)}, bf16[512,512]{1,0:T(8,128)(2,1)}, u32[]{:S(2)}) copy-start(bf16[512,512]{1,0:T(8,128)(2,1)} %constant.5.clone.refs_9_.refs_7_) | copy-start | bytes 1572868
  24.2 3.2 %copy-start.3 = (bf16[512,512]{1,0:T(8,128)(2,1)S(1)}, bf16[512,512]{1,0:T(8,128)(2,1)}, u32[]{:S(2)}) copy-start(bf16[512,512]{1,0:T(8,128)(2,1)} %constant.4.clone.refs_8_.refs_6_) | copy-start | bytes 1572868
  34.2 20.2 %collective-permute-start.5 = (bf16[3,2,256,256]{3,2,1,0:T(8,128)(2,1)S(1)}, bf16[3,2,256,256]{3,2,1,0:T(8,128)(2,1)S(1)}, u32[]{:S(2)}, u32[]{:S(2)}) collective-permute-start(bf16[3,2,256,256]{3,2,1,0:T(8,128)(2,1)S(1)} %get-tuple-element.26), channel_id=1, source_target_pairs={{0,16},{1,17},{2,18},{3,19},{4,20},{5,21},{6,22},{7,23},{8,24},{9,... | collective-permute-start | bytes 2359304 | tf_op jit(solution)/shard_map/ppermute | solution.py:30
  35.2 19.2 %collective-permute-start.6 = (bf16[2,512,128]{2,1,0:T(8,128)(2,1)S(1)}, bf16[2,512,128]{2,1,0:T(8,128)(2,1)S(1)}, u32[]{:S(2)}, u32[]{:S(2)}) collective-permute-start(bf16[2,512,128]{2,1,0:T(8,128)(2,1)S(1)} %get-tuple-element.27), channel_id=1, source_target_pairs={{1,0},{2,1},{3,2},{4,3},{5,4},{6,5},{7,6},{8,7},{9,8},{10,9},{11,1... | collective-permute-start | bytes 786440 | tf_op jit(solution)/shard_map/ppermute | solution.py:30
  37.6 16.8 %collective-permute-start.7 = (bf16[2,512,128]{2,1,0:T(8,128)(2,1)S(1)}, bf16[2,512,128]{2,1,0:T(8,128)(2,1)S(1)}, u32[]{:S(2)}, u32[]{:S(2)}) collective-permute-start(bf16[2,512,128]{2,1,0:T(8,128)(2,1)S(1)} %get-tuple-element.28), channel_id=1, source_target_pairs={{1,16},{2,17},{3,18},{4,19},{5,20},{6,21},{7,22},{8,23},{9,24},{10... | collective-permute-start | bytes 786440 | tf_op jit(solution)/shard_map/ppermute | solution.py:30
  48.0 11.4 %collective-permute-start.10 = (bf16[2,512,128]{2,1,0:T(8,128)(2,1)S(1)}, bf16[2,512,128]{2,1,0:T(8,128)(2,1)S(1)}, u32[]{:S(2)}, u32[]{:S(2)}) collective-permute-start(bf16[2,512,128]{2,1,0:T(8,128)(2,1)S(1)} %get-tuple-element.31), channel_id=1, source_target_pairs={{0,1},{1,2},{2,3},{3,4},{4,5},{5,6},{6,7},{7,8},{8,9},{9,10},{10,1... | collective-permute-start | bytes 786440 | tf_op jit(solution)/shard_map/ppermute | solution.py:30
  50.2 15.1 %collective-permute-start.11 = (bf16[2,512,128]{2,1,0:T(8,128)(2,1)S(1)}, bf16[2,512,128]{2,1,0:T(8,128)(2,1)S(1)}, u32[]{:S(2)}, u32[]{:S(2)}) collective-permute-start(bf16[2,512,128]{2,1,0:T(8,128)(2,1)S(1)} %get-tuple-element.32), channel_id=1, source_target_pairs={{0,17},{1,18},{2,19},{3,20},{4,21},{5,22},{6,23},{7,24},{8,25},{9,... | collective-permute-start | bytes 786440 | tf_op jit(solution)/shard_map/ppermute | solution.py:30
  54.3 11.0 %collective-permute-start.9 = (bf16[2,2,256,256]{3,2,1,0:T(8,128)(2,1)S(1)}, bf16[2,2,256,256]{3,2,1,0:T(8,128)(2,1)S(1)}, u32[]{:S(2)}, u32[]{:S(2)}) collective-permute-start(bf16[2,2,256,256]{3,2,1,0:T(8,128)(2,1)S(1)} %get-tuple-element.30), channel_id=1, source_target_pairs={{0,16},{1,17},{2,18},{3,19},{4,20},{5,21},{6,22},{7,23},{8,24},{9,... | collective-permute-start | bytes 1572872 | tf_op jit(solution)/shard_map/ppermute | solution.py:30

commit v4 on v3

--- a/solution.py
+++ b/solution.py
@@ -14,7 +14,8 @@
 BF16 = jnp.bfloat16
 EXTRA = 8
 HALVES = 16
-DIGIT, HALF, LANES = 256, 64, 128
+BITS, HALF, LANES = 8, 64, 128
+DIGIT = 1 << BITS
 REACH = 256
 LIMIT = 24 * 1024 * 1024
 
@@ -216,7 +217,7 @@
 
 def patch_rows(ref, at, plane, row, height, width):
     step = EXTRA if ref.dtype == F32 else HALVES
-    start = pl.multiple_of(jnp.minimum(row // step * step, height - width - step), step)
+    start = pl.multiple_of(jnp.minimum(row - (row & (step - 1)), height - width - step), step)
     value = ref[(*at, plane, pl.ds(start, width + step), slice(None))].astype(F32)
     shift = row - start
     if step > EXTRA:
@@ -266,9 +267,10 @@
     tail = (HALVES, LANES)
     place = columns(tail)
     coded = jnp.zeros(tail, jnp.int32)
-    for at in range(HALF):
+    for at in range(ENTRY, ENTRY + 10 * FIELDS):
         value = own_ref[0, at]
-        coded = jnp.where(place == at, value // DIGIT, jnp.where(place == at + HALF, value % DIGIT, coded))
+        high, low = value >> BITS, value & (DIGIT - 1)
+        coded = jnp.where(place == at, high, jnp.where(place == at + HALF, low, coded))
     for group in range(2):
         outs[group][4 * reach :] = coded.astype(F32).astype(BF16)
     for plane in range(2):
@@ -356,6 +358,164 @@
         pl.when(items[2][0])(lambda: write(2))
 
 
+def propagate(field, half, phase, one_ref, two_ref, adjoint, which, finish):
+    width = one_ref.shape[0] // 2
+    sign = -1.0 if adjoint else 1.0
+    for item in range(2):
+        for side in range(2):
+            part = slice(side * width, (side + 1) * width)
+            product = jnp.dot(field[item], one_ref[:, part], preferred_element_type=F32)
+            half[item, part] = product.astype(BF16)
+    for item in range(2):
+        real = jnp.dot(two_ref[:width], half[item], preferred_element_type=F32)
+        imag = jnp.dot(two_ref[width:], half[item], preferred_element_type=F32)
+        cosine, sine = phase[which, 0], sign * phase[which, 1]
+        field[item, :, :width] = (real * cosine - imag * sine).astype(BF16)
+        field[item, :, width:] = (real * sine + imag * cosine).astype(BF16)
+    for item in range(2):
+        for side in range(2):
+            part = slice(side * width, (side + 1) * width)
+            product = jnp.dot(field[item], two_ref[:, part], preferred_element_type=F32)
+            half[item, part] = product.astype(BF16)
+    for item in range(2):
+        real = jnp.dot(one_ref[:width], half[item], preferred_element_type=F32)
+        imag = jnp.dot(one_ref[width:], half[item], preferred_element_type=F32)
+        finish(item, real, imag)
+
+
+def pair_of(turn_index, table, late, lone, core):
+    entries, spare = [], []
+    for item in range(2):
+        taken = (turn_index > 0) | lone if item else turn_index > 0
+        entry = table.item("B", core, item)
+        entries.append(tuple(jnp.where(taken, b, a) for a, b in zip(entry, late)))
+        spare.append(taken)
+    return entries, spare
+
+
+def store(field, item, real, imag):
+    width = field.shape[1]
+    field[item, :, :width] = real.astype(BF16)
+    field[item, :, width:] = imag.astype(BF16)
+
+
+def turns_of(behind_ref, own_ref):
+    core = own_ref[0, 0]
+    table = Table(behind_ref)
+    late = Table(own_ref).item("A", core, 2)
+    lone = late[0] & jnp.logical_not(table.item("B", core, 1)[0])
+    return core, table, late, lone, jnp.where(late[0] & jnp.logical_not(lone), 2, 1)
+
+
+def forward_kernel(
+    reach, behind_ref, own_ref, straight_ref, cross_ref, part_ref, phase, probe_ref, one_ref, two_ref,
+    patch, wave, leave, field, half,
+):
+    width = probe_ref.shape[-1]
+    core, table, late, lone, turns = turns_of(behind_ref, own_ref)
+    lane = columns((width, width))
+    spread = functools.partial(propagate, field, half, phase, one_ref, two_ref)
+
+    def one_pair(step, _):
+        entries, spare = pair_of(step, table, late, lone, core)
+        masks = [(lane < width - entries[item][3]) & jnp.logical_not(spare[item]) for item in range(2)]
+        for source, ref in ((core, straight_ref), (1 - core, cross_ref)):
+            for plane in range(2):
+                page = unfold(ref[plane * 2 * reach : (plane + 1) * 2 * reach].astype(F32), width, reach)
+                for item in range(2):
+                    foreign = page if item else turn(page, 2 * width - reach - entries[item][3], width)
+                    own = part_ref[jnp.where(spare[item], 2, item), source, plane].astype(F32)
+                    patch[step, source, item, plane] = jnp.where(masks[item], foreign, own).astype(BF16)
+        for item in range(2):
+            left_re, left_im = probe_ref[0], probe_ref[1]
+            right_re, right_im = [patch[step, 0, item, plane].astype(F32) for plane in range(2)]
+            store(field, item, left_re * right_re - left_im * right_im, left_re * right_im + left_im * right_re)
+
+        def after_first(item, real, imag):
+            real, imag = real.astype(BF16), imag.astype(BF16)
+            wave[step, item, 0], wave[step, item, 1] = real, imag
+            real, imag = real.astype(F32), imag.astype(F32)
+            right_re, right_im = [patch[step, 1, item, plane].astype(F32) for plane in range(2)]
+            store(field, item, real * right_re - imag * right_im, real * right_im + imag * right_re)
+
+        def after_second(item, real, imag):
+            leave[step, item, 0], leave[step, item, 1] = real.astype(BF16), imag.astype(BF16)
+
+        spread(False, 0, after_first)
+        spread(False, 1, after_second)
+        return 0
+
+    lax.fori_loop(0, turns, one_pair, 0)
+
+
+def backward_kernel(
+    reach, behind_ref, own_ref, level_ref, patch, wave, leave, phase, probe_ref, one_ref, two_ref, intensity_ref,
+    back_straight, back_cross, out_self, out_swap, grads, field, half, levels, level_sems,
+):
+    width = probe_ref.shape[-1]
+    core, table, late, lone, turns = turns_of(behind_ref, own_ref)
+    lane = columns((width, width))
+    spread = functools.partial(propagate, field, half, phase, one_ref, two_ref)
+
+    def one_pair(step, _):
+        entries, spare = pair_of(step, table, late, lone, core)
+        for item in range(2):
+
+            @pl.when(spare[item])
+            def _():
+                load = pltpu.make_async_copy(
+                    intensity_ref.at[0, entries[item][1]], levels.at[item], level_sems.at[item]
+                )
+                load.start()
+                load.wait()
+
+            @pl.when(jnp.logical_not(spare[item]))
+            def _():
+                levels[item] = level_ref[item].astype(F32)
+
+        for item in range(2):
+            real, imag = leave[step, item, 0].astype(F32), leave[step, item, 1].astype(F32)
+            gain = 2.0 * (real * real + imag * imag - levels[item])
+            gain = jnp.where(entries[item][0], gain, 0.0)
+            store(field, item, gain * real, gain * imag)
+
+        def before_second(item, real, imag):
+            left_re, left_im = [wave[step, item, plane].astype(F32) for plane in range(2)]
+            grads[1, item, 0] = (left_re * real + left_im * imag).astype(BF16)
+            grads[1, item, 1] = (left_re * imag - left_im * real).astype(BF16)
+            left_re, left_im = [patch[step, 1, item, plane].astype(F32) for plane in range(2)]
+            store(field, item, left_re * real + left_im * imag, left_re * imag - left_im * real)
+
+        def before_first(item, real, imag):
+            left_re, left_im = probe_ref[0], probe_ref[1]
+            grads[0, item, 0] = (left_re * real + left_im * imag).astype(BF16)
+            grads[0, item, 1] = (left_re * imag - left_im * real).astype(BF16)
+
+        spread(True, 1, before_second)
+        spread(True, 0, before_first)
+        for item in range(2):
+            at = jnp.where(spare[item], 2, item)
+            out_self[at] = grads[core, item]
+            out_swap[at] = grads[1 - core, item]
+
+        @pl.when(step == 0)
+        def _():
+            (live0, _, _, col0), (live1, _, _, col1) = entries
+            live1 = live1 & jnp.logical_not(lone)
+            mask0 = live0 & (lane >= reach - width + col0) & (lane < reach)
+            mask1 = live1 & (lane < width - col1)
+            for source, out_ref in ((core, back_straight), (1 - core, back_cross)):
+                for plane in range(2):
+                    first = turn(grads[source, 0, plane].astype(F32), col0 + reach, width)
+                    second = grads[source, 1, plane].astype(F32)
+                    page = jnp.where(mask0, first, jnp.where(mask1, second, 0.0))
+                    out_ref[plane] = fold(page, reach).astype(BF16)
+
+        return 0
+
+    lax.fori_loop(0, turns, one_pair, 0)
+
+
 def waves_kernel(kind, places, reach, *refs):
     behind_ref, own_ref = refs[:2]
     if kind == "A":
@@ -371,40 +531,25 @@
     other = 1 - core
     table = Table(own_ref if kind == "A" else behind_ref)
     late = Table(own_ref).item("A", core, 2)
+    lone = late[0] & jnp.logical_not(table.item(kind, core, 1)[0])
     lane = columns((width, width))
 
-    def propagate(adjoint, which, finish):
-        sign = -1.0 if adjoint else 1.0
-        for item in range(2):
-            product = jnp.dot(field[item], one_ref[...], preferred_element_type=F32)
-            half[item, :width] = product[:, :width].astype(BF16)
-            half[item, width:] = product[:, width:].astype(BF16)
-        for item in range(2):
-            spectrum = jnp.dot(two_ref[...], half[item], preferred_element_type=F32)
-            real, imag = spectrum[:width], spectrum[width:]
-            cosine, sine = phase[which, 0], sign * phase[which, 1]
-            field[item, :, :width] = (real * cosine - imag * sine).astype(BF16)
-            field[item, :, width:] = (real * sine + imag * cosine).astype(BF16)
-        for item in range(2):
-            product = jnp.dot(field[item], two_ref[...], preferred_element_type=F32)
-            half[item, :width] = product[:, :width].astype(BF16)
-            half[item, width:] = product[:, width:].astype(BF16)
-        for item in range(2):
-            result = jnp.dot(one_ref[...], half[item], preferred_element_type=F32)
-            finish(item, result[:width], result[width:])
+    spread = functools.partial(propagate, field, half, phase, one_ref, two_ref)
 
     def put(item, real, imag):
         field[item, :, :width] = real.astype(BF16)
         field[item, :, width:] = imag.astype(BF16)
 
     def one_pair(turn_index, _):
-        entries = []
+        entries, spare = [], []
         for item in range(2):
             entry = table.item(kind, core, item)
             if places > 2:
-                entry = tuple(jnp.where(turn_index > 0, b, a) for a, b in zip(entry, late))
+                taken = (turn_index > 0) | lone if item else turn_index > 0
+                entry = tuple(jnp.where(taken, b, a) for a, b in zip(entry, late))
+                spare.append(taken)
             entries.append(entry)
-        at = [jnp.minimum(2 * turn_index + item, places - 1) for item in range(2)]
+        at = [jnp.where(spare[item], 2, item) for item in range(2)] if places > 2 else [0, 1]
 
         def levels_of(item):
             return pltpu.make_async_copy(
@@ -416,23 +561,22 @@
                 levels_of(item).start()
         else:
 
-            @pl.when(turn_index > 0)
-            def _():
-                for item in range(2):
+            for item in range(2):
+
+                @pl.when(spare[item])
+                def _():
                     levels_of(item).start()
-                for item in range(2):
                     levels_of(item).wait()
 
-            @pl.when(turn_index == 0)
-            def _():
-                for item in range(2):
+                @pl.when(jnp.logical_not(spare[item]))
+                def _():
                     levels[item] = level_ref[item].astype(F32)
 
         masks = []
         for item in range(2):
             col = entries[item][3]
             mask = lane >= width - col if kind == "A" else lane < width - col
-            masks.append(mask & (turn_index == 0) if kind == "B" else mask)
+            masks.append(mask & jnp.logical_not(spare[item]) if kind == "B" else mask)
         for at_source, source in enumerate((core, other)):
             for plane in range(2):
                 if kind == "A":
@@ -463,7 +607,7 @@
             right_re, right_im = patch[1, item, 0].astype(F32), patch[1, item, 1].astype(F32)
             put(item, real * right_re - imag * right_im, real * right_im + imag * right_re)
 
-        propagate(False, 0, after_first)
+        spread(False, 0, after_first)
         if kind == "A":
             for item in range(2):
                 levels_of(item).wait()
@@ -474,7 +618,7 @@
             gain = jnp.where(entries[item][0], gain, 0.0)
             put(item, gain * real, gain * imag)
 
-        propagate(False, 1, after_second)
+        spread(False, 1, after_second)
 
         def before_second(item, real, imag):
             left_re, left_im = wave[item, 0].astype(F32), wave[item, 1].astype(F32)
@@ -483,14 +627,14 @@
             left_re, left_im = patch[1, item, 0].astype(F32), patch[1, item, 1].astype(F32)
             put(item, left_re * real + left_im * imag, left_re * imag - left_im * real)
 
-        propagate(True, 1, before_second)
+        spread(True, 1, before_second)
 
         def before_first(item, real, imag):
             left_re, left_im = probe_ref[0], probe_ref[1]
             grads[0, item, 0] = (left_re * real + left_im * imag).astype(BF16)
             grads[0, item, 1] = (left_re * imag - left_im * real).astype(BF16)
 
-        propagate(True, 0, before_first)
+        spread(True, 0, before_first)
         for item in range(2):
             out_self[at[item]] = grads[core, item]
             out_swap[at[item]] = grads[other, item]
@@ -498,6 +642,8 @@
         @pl.when(turn_index == 0)
         def _():
             (live0, _, _, col0), (live1, _, _, col1) = entries
+            if places > 2:
+                live1 = live1 & jnp.logical_not(lone)
             if kind == "A":
                 mask0 = lane < col0
                 mask1 = (lane >= reach - col1) & (lane < reach)
@@ -517,7 +663,7 @@
         return 0
 
     if places > 2:
-        turns = jnp.where(late[0], 2, 1)
+        turns = jnp.where(late[0] & jnp.logical_not(lone), 2, 1)
         lax.fori_loop(0, turns, one_pair, 0)
     else:
         one_pair(jnp.int32(0), 0)
@@ -531,7 +677,7 @@
     def _():
         lane = columns((width, width))
         mask = lane < col if in_next else lane >= col
-        start = pl.multiple_of(jnp.minimum(row // EXTRA * EXTRA, height - width - EXTRA), EXTRA)
+        start = pl.multiple_of(jnp.minimum(row - (row & (EXTRA - 1)), height - width - EXTRA), EXTRA)
         rows = pl.ds(start, width + EXTRA)
         value = piece()
         if amount is not None:
@@ -566,28 +712,42 @@
                 add_piece(total, plane, entry, False, lambda: page, amount)
 
 
-def finish_kernel(reach, own_ref, behind_ref, canvas_ref, a_swap, a_back, a_back_cross, out_ref, total, sems):
-    width = canvas_ref.shape[-1]
+def merge_kernel(own_ref, _, a_swap, canvas_ref, out_ref, sem):
+    other = 1 - own_ref[0, 0]
+    own = Table(own_ref)
+    for plane in range(2):
+        for place in range(2):
+            entry = own.item("A", other, place)
+            piece = lambda: a_swap[place, plane].astype(F32)
+            add_piece(canvas_ref.at[0], plane, entry, False, piece, entry[3])
+    copy = pltpu.make_async_copy(canvas_ref, out_ref, sem)
+    copy.start()
+    copy.wait()
+
+
+def finish_kernel(reach, own_ref, behind_ref, _, __, a_back, a_back_cross, canvas_ref, out_ref, sems):
+    height, width = canvas_ref.shape[2:]
     core = own_ref[0, 0]
-    other = 1 - core
-    own, behind = Table(own_ref), Table(behind_ref)
+    behind = Table(behind_ref)
+    backs = ((core, a_back), (1 - core, a_back_cross))
+    pairs = [[behind.item("A", owner, place) for place in range(2)] for owner, _ in backs]
     copies = []
     for plane in range(2):
-        total[plane] = canvas_ref[0, plane]
-        for place in range(2):
-            entry = own.item("A", other, place)
-            add_piece(total, plane, entry, False, lambda: a_swap[place, plane].astype(F32), entry[3])
-        for owner, ref in ((core, a_back), (other, a_back_cross)):
+        for (_, ref), pair in zip(backs, pairs):
             page = unfold(ref[plane].astype(F32), width, reach)
             for place in range(2):
-                entry = behind.item("A", owner, place)
-                amount = None if place == 0 else width - reach + entry[3]
-                add_piece(total, plane, entry, True, lambda: page, amount)
-        copy = pltpu.make_async_copy(total.at[plane], out_ref.at[0, plane], sems.at[plane])
-        copy.start()
-        copies.append(copy)
-    for copy in copies:
-        copy.wait()
+                amount = None if place == 0 else width - reach + pair[place][3]
+                add_piece(canvas_ref.at[0], plane, pair[place], True, lambda: page, amount)
+        for at, (live, _, row, _) in enumerate(pairs[0] + pairs[1]):
+            start = pl.multiple_of(jnp.minimum(row - (row & (EXTRA - 1)), height - width - EXTRA), EXTRA)
+            rows = pl.ds(start, width + EXTRA)
+            copy = pltpu.make_async_copy(
+                canvas_ref.at[0, plane, rows, :], out_ref.at[0, plane, rows, :], sems.at[plane, at]
+            )
+            pl.when(live)(copy.start)
+            copies.append((live, copy))
+    for live, copy in copies:
+        pl.when(live)(copy.wait)
 
 
 def on_device(
@@ -605,9 +765,10 @@
     planes = lambda *lead: jax.ShapeDtypeStruct((*lead, width, width), BF16)
     dma = lambda *shape: pltpu.SemaphoreType.DMA(shape)
     whole = jax.ShapeDtypeStruct(object_slices.shape, F32)
+    inner = pltpu.VMEM(object_slices.shape, F32)
     still = lambda value: pltpu.with_memory_space_constraint(value, pltpu.HBM)
 
-    def call(kernel, name, operands, out_shape, scratch, cost=0, limit=LIMIT, out_specs=None):
+    def call(kernel, name, operands, out_shape, scratch, cost=0, limit=LIMIT, out_specs=None, aliases=None):
         return pl.pallas_call(
             kernel,
             out_shape=out_shape,
@@ -617,6 +778,7 @@
             compiler_params=pltpu.CompilerParams(vmem_limit_bytes=limit),
             cost_estimate=pl.CostEstimate(flops=cost * 10**9, bytes_accessed=cost * 3 * 10**6, transcendentals=0),
             name=name,
+            input_output_aliases=aliases or {},
         )(*[value for _, value in operands])
 
     def run(reach):
@@ -691,7 +853,25 @@
         )
         b_part = parts("B", behind, page)
         page = send(page, 0, -1)
-        b_back, b_back_cross, b_self, b_swap = waves("B", (b_straight, b_cross, level), b_part)
+        table = [(smem, behind), (smem, own)]
+        optics = [(vmem, value) for value in (turned, probe_field, one, two)]
+        fields = [pltpu.VMEM((2, width, 2 * width), BF16), pltpu.VMEM((2, 2 * width, width), BF16)]
+        states = call(
+            functools.partial(forward_kernel, reach),
+            "waves_forward",
+            table + [(vmem, value) for value in (b_straight, b_cross, b_part)] + optics,
+            [planes(2, 2, 2, 2), planes(2, 2, 2), planes(2, 2, 2)],
+            fields,
+            3,
+        )
+        b_back, b_back_cross, b_self, b_swap = call(
+            functools.partial(backward_kernel, reach),
+            "waves_back",
+            table + [(vmem, value) for value in (level, *states)] + optics + [(hbm, still(intensity))],
+            [folded(2), folded(2), planes(3, 2), planes(3, 2)],
+            [pltpu.VMEM((2, 2, 2, width, width), BF16)] + fields + [pltpu.VMEM((2, width, width), F32), dma(2)],
+            4,
+        )
         b_swap = send(b_swap, 1, 0)
         b_back, b_back_cross = send(b_back, 0, -1), send(b_back_cross, 1, -1)
         a_back, a_back_cross, a_self, a_swap = waves("A", (page,), a_part, b_self)
@@ -702,21 +882,32 @@
             "gather",
             [(smem, own), (smem, behind)]
             + [(vmem, value) for value in (b_self, b_swap, b_back, b_back_cross, a_self)],
-            whole,
+            inner,
             [],
             cost=10,
         )
-        return own, behind, canvas, a_swap, a_back, a_back_cross
-
-    def finish(reach, own, behind, *values):
-        return call(
+        canvas, out = call(
+            merge_kernel,
+            "merge",
+            [(smem, own), (vmem, canvas), (vmem, a_swap)],
+            [inner, whole],
+            [dma()],
+            out_specs=[vmem, hbm],
+            aliases={1: 0},
+        )
+        return own, behind, canvas, out, a_back, a_back_cross
+
+    def finish(reach, own, behind, canvas, out, a_back, a_back_cross):
+        _, out = call(
             functools.partial(finish_kernel, reach),
             "finish",
-            [(smem, own), (smem, behind)] + [(vmem, value) for value in values],
-            whole,
-            [pltpu.VMEM((2, height, width), F32), dma(2)],
-            out_specs=hbm,
+            [(smem, own), (smem, behind), (vmem, canvas), (hbm, out), (vmem, a_back), (vmem, a_back_cross)],
+            [inner, whole],
+            [dma(2, 4)],
+            out_specs=[vmem, hbm],
+            aliases={2: 0, 3: 1},
         )
+        return out
 
     reach = REACH
     narrow = run(reach)

time: 68.9 us -> 64.9 us (0.942)
  waiting for transfers between devices: 10.9 us -> 6.84 us
    ppermute x12, waiting for transfers between devices: 10.9 us -> 6.84 us  [send(): return lax.ppermute(value, ('cuts', 'tile'), pairs)]
    pallas_call x10 -> x12, Pallas kernels: 28.6 us -> 28.8 us  [call(): pl.pallas_call(kernel, out_shape=out_shape, in_specs=[spec for spec, _ in...]
  transfers between devices with their start and end apart: 12 -> 12, of which waited for: 3 -> 3; matrix products, arithmetic and copies ran while one was open for 0% -> 0% of each run, Pallas kernels for 33% -> 37%
where the time goes in v4:
time: 64.9 us; the launch traced here: 64.6 us
  Pallas kernels  28.8 us (44%)
  starting transfers between devices  27.9 us (43%)
  waiting for transfers between devices  6.84 us (11%)
  between operations  1.12 us (2%)
    pallas_call x12, Pallas kernels, call(): pl.pallas_call(kernel, out_shape=out_shape, in_specs=[spec for spec, _ in...  28.8 us
    ppermute x12, starting transfers between devices, send(): return lax.ppermute(value, ('cuts', 'tile'), pairs)  27.9 us
    ppermute x12, waiting for transfers between devices, send(): return lax.ppermute(value, ('cuts', 'tile'), pairs)  6.84 us
  transfers between devices with their start and end apart: 12, of which 3 were waited for; matrix products, arithmetic and copies ran while one was open for 0% of the time, Pallas kernels for 37%

profile of v4, /device:TPU:17, one launch (start us, length us, event | category | flops | bytes accessed | tf_op | source)
XLA Modules:
  0.0 64.6 jit_solution(17808930656621805822)
XLA Ops:
  0.0 0.0 copy-start
  0.7 2.9 %first.1 = (s32[1,64]{1,0:T(1,128)S(1)}, bf16[2,2048,256]{2,1,0:T(8,128)(2,1)S(1)}, bf16[1040,128]{1,0:T(8,128)(2,1)S(1)}, bf16[1040,128]{1,0:T(8,128)(2,1)S(1)}) custom-call(s32[1]{0:T(128)S(6)} %copy.17.counts_ref, s32[1,6]{1,0:T(1,128)} %chosen_hbm.1, s32[1,8]{1,0:T(1,128)} %row_hbm.1, s32[1,8]{1,0:T(1,128)} %col_hbm.1, f32[1,2,2048,256]{3,2,1,0:T(8,128)} %object_ref.1), custom_call_target="tpu_custom_call" | custom-call | tf_op jit(solution)/shard_map/first/pallas_call | solution.py:772
  3.6 0.7 %collective-permute-start = (bf16[2,2048,256]{2,1,0:T(8,128)(2,1)S(1)}, bf16[2,2048,256]{2,1,0:T(8,128)(2,1)S(1)}, u32[]{:S(2)}, u32[]{:S(2)}) collective-permute-start(bf16[2,2048,256]{2,1,0:T(8,128)(2,1)S(1)} %get-tuple-element.26.self_ref), channel_id=1, source_target_pairs={{0,16},{1,17},{2,18},{3,19},{4,20},{5,21},{6,22},{7,23},{8,24},{9,... | collective-permute-start | bytes 6291464 | tf_op jit(solution)/shard_map/ppermute | solution.py:31
  4.3 3.1 %collective-permute-start.1 = (bf16[1040,128]{1,0:T(8,128)(2,1)S(1)}, bf16[1040,128]{1,0:T(8,128)(2,1)S(1)}, u32[]{:S(2)}, u32[]{:S(2)}) collective-permute-start(bf16[1040,128]{1,0:T(8,128)(2,1)S(1)} %get-tuple-element.27), channel_id=1, source_target_pairs={{0,1},{1,2},{2,3},{3,4},{4,5},{5,6},{6,7},{7,8},{8,9},{9,10},{10,1... | collective-permute-start | bytes 798728 | tf_op jit(solution)/shard_map/ppermute | solution.py:31
  7.4 3.3 %collective-permute-start.4 = (bf16[1040,128]{1,0:T(8,128)(2,1)S(1)}, bf16[1040,128]{1,0:T(8,128)(2,1)S(1)}, u32[]{:S(2)}, u32[]{:S(2)}) collective-permute-start(bf16[1040,128]{1,0:T(8,128)(2,1)S(1)} %get-tuple-element.28._), channel_id=1, source_target_pairs={{0,17},{1,18},{2,19},{3,20},{4,21},{5,22},{6,23},{7,24},{8,25},{9,... | collective-permute-start | bytes 798728 | tf_op jit(solution)/shard_map/ppermute | solution.py:31
  10.7 0.0 copy-done
  10.8 0.3 collective-permute-start.2
  11.0 1.6 %levels.1._ = bf16[2,256,256]{2,1,0:T(8,128)(2,1)S(1)} custom-call(s32[1,64]{1,0:T(1,128)S(1)} %get-tuple-element.25.own_ref.behind_ref.refs_1_, f32[1,8,256,256]{3,2,1,0:T(8,128)} %refs_8_.1, bf16[1040,128]{1,0:T(8,128)(2,1)S(1)} %get-tuple-element.28._), custom_call_target="tpu_custom_call" | custom-call | tf_op jit(solution)/shard_map/levels/pallas_call | solution.py:772
  12.6 3.1 %collective-permute-start.3 = (bf16[2,256,256]{2,1,0:T(8,128)(2,1)S(1)}, bf16[2,256,256]{2,1,0:T(8,128)(2,1)S(1)}, u32[]{:S(2)}, u32[]{:S(2)}) collective-permute-start(bf16[2,256,256]{2,1,0:T(8,128)(2,1)S(1)} %levels.1._), channel_id=1, source_target_pairs={{0,1},{1,2},{2,3},{3,4},{4,5},{5,6},{6,7},{7,8},{8,9},{9,10},{10,1... | collective-permute-start | bytes 786440 | tf_op jit(solution)/shard_map/ppermute | solution.py:31
  15.8 0.0 collective-permute-done.2.other_ref
  15.8 1.2 %angles.1._.phase.refs_4_ = f32[2,2,256,256]{3,2,1,0:T(8,128)S(1)} custom-call(s32[1,64]{1,0:T(1,128)S(1)} %get-tuple-element.25.own_ref.behind_ref.refs_1_, f32[1,256,256]{2,1,0:T(8,128)S(1)} %copy-done, f32[1,256,256]{2,1,0:T(8,128)S(1)} %collective-permute-done.2.other_ref, bf16[2,256,256]{2,1,0:T(8,128)(2,1)S(1)} %levels.1._), custom_call_target="tpu_custom_call" | custom-call | tf_op jit(solution)/shard_map/angles/pallas_call | solution.py:772
  17.0 0.0 collective-permute-done.other_ref
  17.0 1.2 %parts_a.1._.refs_3_ = bf16[2,2,2,256,256]{4,3,2,1,0:T(8,128)(2,1)S(1)} custom-call(s32[1,64]{1,0:T(1,128)S(1)} %get-tuple-element.25.own_ref.behind_ref.refs_1_, s32[1,64]{1,0:T(1,128)S(1)} %get-tuple-element.25.own_ref.behind_ref.refs_1_, bf16[2,2048,256]{2,1,0:T(8,128)(2,1)S(1)} %get-tuple-element.26.self_ref, ...), custom_call_target="tpu_custom_call" | custom-call | tf_op jit(solution)/shard_map/parts_a/pallas_call | solution.py:772
  18.2 0.0 collective-permute-done.1.message_ref.straight_ref
  18.2 1.9 %pages.1 = (bf16[2,2,512,128]{3,2,1,0:T(8,128)(2,1)S(1)}, s32[8,128]{1,0:T(8,128)S(1)}) custom-call(s32[1,64]{1,0:T(1,128)S(1)} %get-tuple-element.25.own_ref.behind_ref.refs_1_, bf16[2,2048,256]{2,1,0:T(8,128)(2,1)S(1)} %get-tuple-element.26.self_ref, bf16[2,2048,256]{2,1,0:T(8,128)(2,1)S(1)} %collective-permute-done.other_ref, ...), custom_call_target="tpu_custom_call" | custom-call | tf_op jit(solution)/shard_map/pages/pallas_call | solution.py:772
  20.1 0.0 copy-start.1
  20.1 0.0 copy-start.2
  20.1 0.0 copy-start.3
  20.2 4.1 %collective-permute-start.8 = (bf16[2,2,512,128]{3,2,1,0:T(8,128)(2,1)S(1)}, bf16[2,2,512,128]{3,2,1,0:T(8,128)(2,1)S(1)}, u32[]{:S(2)}, u32[]{:S(2)}) collective-permute-start(bf16[2,2,512,128]{3,2,1,0:T(8,128)(2,1)S(1)} %get-tuple-element.30._), channel_id=1, source_target_pairs={{1,0},{2,1},{3,2},{4,3},{5,4},{6,5},{7,6},{8,7},{9,8},{10,9},{11,1... | collective-permute-start | bytes 1572872 | tf_op jit(solution)/shard_map/ppermute | solution.py:31
  24.3 1.3 %parts_b.1.part_ref = bf16[3,2,2,256,256]{4,3,2,1,0:T(8,128)(2,1)S(1)} custom-call(s32[8,128]{1,0:T(8,128)S(1)} %get-tuple-element.29.behind_ref.refs_0_, s32[1,64]{1,0:T(1,128)S(1)} %get-tuple-element.25.own_ref.behind_ref.refs_1_, bf16[2,2048,256]{2,1,0:T(8,128)(2,1)S(1)} %get-tuple-element.26.self_ref, ...), custom_call_target="tpu_custom_call" | custom-call | tf_op jit(solution)/shard_map/parts_b/pallas_call | solution.py:772
  25.5 0.0 collective-permute-done.4.cross_ref
  25.6 0.0 copy-done.1
  25.6 0.0 copy-done.2
  25.6 0.0 copy-done.3
  25.6 3.4 %waves_forward.1 = (bf16[2,2,2,2,256,256]{5,4,3,2,1,0:T(8,128)(2,1)S(1)}, bf16[2,2,2,256,256]{4,3,2,1,0:T(8,128)(2,1)S(1)}, bf16[2,2,2,256,256]{4,3,2,1,0:T(8,128)(2,1)S(1)}) custom-call(s32[8,128]{1,0:T(8,128)S(1)} %get-tuple-element.29.behind_ref.refs_0_, s32[1,64]{1,0:T(1,128)S(1)} %get-tuple-element.25.own_ref.behind_ref.refs_1_, ...), custom_call_target="tpu_custom_call" | custom-call | flops 3000000000 | bytes 9000000 | tf_op jit(solution)/shard_map/waves_forward/pallas_call | solution.py:772
  29.0 0.0 collective-permute-done.3.level_ref
  29.0 3.6 %waves_back.1 = (bf16[2,512,128]{2,1,0:T(8,128)(2,1)S(1)}, bf16[2,512,128]{2,1,0:T(8,128)(2,1)S(1)}, bf16[3,2,256,256]{3,2,1,0:T(8,128)(2,1)S(1)}, bf16[3,2,256,256]{3,2,1,0:T(8,128)(2,1)S(1)}) custom-call(s32[8,128]{1,0:T(8,128)S(1)} %get-tuple-element.29.behind_ref.refs_0_, s32[1,64]{1,0:T(1,128)S(1)} %get-tuple-element.25.own_ref.behind_ref.refs_1_, ...), custom_call_target="tpu_custom_call" | custom-call | flops 4000000000 | bytes 12000000 | tf_op jit(solution)/shard_map/waves_back/pallas_call | solution.py:772
  32.6 0.9 %collective-permute-start.5 = (bf16[3,2,256,256]{3,2,1,0:T(8,128)(2,1)S(1)}, bf16[3,2,256,256]{3,2,1,0:T(8,128)(2,1)S(1)}, u32[]{:S(2)}, u32[]{:S(2)}) collective-permute-start(bf16[3,2,256,256]{3,2,1,0:T(8,128)(2,1)S(1)} %get-tuple-element.35), channel_id=1, source_target_pairs={{0,16},{1,17},{2,18},{3,19},{4,20},{5,21},{6,22},{7,23},{8,24},{9,... | collective-permute-start | bytes 2359304 | tf_op jit(solution)/shard_map/ppermute | solution.py:31
  33.5 2.2 %collective-permute-start.6 = (bf16[2,512,128]{2,1,0:T(8,128)(2,1)S(1)}, bf16[2,512,128]{2,1,0:T(8,128)(2,1)S(1)}, u32[]{:S(2)}, u32[]{:S(2)}) collective-permute-start(bf16[2,512,128]{2,1,0:T(8,128)(2,1)S(1)} %get-tuple-element.36), channel_id=1, source_target_pairs={{1,0},{2,1},{3,2},{4,3},{5,4},{6,5},{7,6},{8,7},{9,8},{10,9},{11,1... | collective-permute-start | bytes 786440 | tf_op jit(solution)/shard_map/ppermute | solution.py:31
  35.7 3.4 %collective-permute-start.7 = (bf16[2,512,128]{2,1,0:T(8,128)(2,1)S(1)}, bf16[2,512,128]{2,1,0:T(8,128)(2,1)S(1)}, u32[]{:S(2)}, u32[]{:S(2)}) collective-permute-start(bf16[2,512,128]{2,1,0:T(8,128)(2,1)S(1)} %get-tuple-element.37), channel_id=1, source_target_pairs={{1,16},{2,17},{3,18},{4,19},{5,20},{6,21},{7,22},{8,23},{9,24},{10... | collective-permute-start | bytes 786440 | tf_op jit(solution)/shard_map/ppermute | solution.py:31
  39.1 0.0 collective-permute-done.8.refs_2_
  39.1 6.2 %waves_a.1 = (bf16[2,512,128]{2,1,0:T(8,128)(2,1)S(1)}, bf16[2,512,128]{2,1,0:T(8,128)(2,1)S(1)}, bf16[2,2,256,256]{3,2,1,0:T(8,128)(2,1)S(1)}, bf16[2,2,256,256]{3,2,1,0:T(8,128)(2,1)S(1)}) custom-call(s32[8,128]{1,0:T(8,128)S(1)} %get-tuple-element.29.behind_ref.refs_0_, s32[1,64]{1,0:T(1,128)S(1)} %get-tuple-element.25.own_ref.behind_ref.refs_1_, ...), custom_call_target="tpu_custom_call" | custom-call | flops 7000000000 | bytes 21000000 | tf_op jit(solution)/shard_map/waves_a/pallas_call | solution.py:772
  45.3 2.2 %collective-permute-start.10 = (bf16[2,512,128]{2,1,0:T(8,128)(2,1)S(1)}, bf16[2,512,128]{2,1,0:T(8,128)(2,1)S(1)}, u32[]{:S(2)}, u32[]{:S(2)}) collective-permute-start(bf16[2,512,128]{2,1,0:T(8,128)(2,1)S(1)} %get-tuple-element.42), channel_id=1, source_target_pairs={{0,1},{1,2},{2,3},{3,4},{4,5},{5,6},{6,7},{7,8},{8,9},{9,10},{10,1... | collective-permute-start | bytes 786440 | tf_op jit(solution)/shard_map/ppermute | solution.py:31
  47.6 4.4 %collective-permute-start.11 = (bf16[2,512,128]{2,1,0:T(8,128)(2,1)S(1)}, bf16[2,512,128]{2,1,0:T(8,128)(2,1)S(1)}, u32[]{:S(2)}, u32[]{:S(2)}) collective-permute-start(bf16[2,512,128]{2,1,0:T(8,128)(2,1)S(1)} %get-tuple-element.43), channel_id=1, source_target_pairs={{0,17},{1,18},{2,19},{3,20},{4,21},{5,22},{6,23},{7,24},{8,25},{9,... | collective-permute-start | bytes 786440 | tf_op jit(solution)/shard_map/ppermute | solution.py:31
  52.0 0.0 collective-permute-done.6.b_back
  52.0 0.1 collective-permute-start.9
  52.1 0.0 collective-permute-done.7.b_back_cross
  52.1 0.0 collective-permute-done.5.b_swap
  52.1 1.2 %gather.1._ = f32[1,2,2048,256]{3,2,1,0:T(8,128)S(1)} custom-call(s32[1,64]{1,0:T(1,128)S(1)} %get-tuple-element.25.own_ref.behind_ref.refs_1_, s32[8,128]{1,0:T(8,128)S(1)} %get-tuple-element.29.behind_ref.refs_0_, bf16[3,2,256,256]{3,2,1,0:T(8,128)(2,1)S(1)} %get-tuple-element.34.refs_9_.b_self, ...), custom_call_target="tpu_custom_call" | custom-call | flops 10000000000 | bytes 30000000 | tf_op jit(solution)/shard_map/gather/pallas_call | solution.py:772
  53.3 0.7 %collective-permute-done.9.a_swap = bf16[2,2,256,256]{3,2,1,0:T(8,128)(2,1)S(1)} collective-permute-done((bf16[2,2,256,256]{3,2,1,0:T(8,128)(2,1)S(1)}, bf16[2,2,256,256]{3,2,1,0:T(8,128)(2,1)S(1)}, u32[]{:S(2)}, u32[]{:S(2)}) %collective-permute-start.9) | collective-permute-done | bytes 524320 | tf_op jit(solution)/shard_map/ppermute | solution.py:31
  53.9 2.6 %merge.1 = (f32[1,2,2048,256]{3,2,1,0:T(8,128)S(1)}, f32[1,2,2048,256]{3,2,1,0:T(8,128)}) custom-call(s32[1,64]{1,0:T(1,128)S(1)} %get-tuple-element.25.own_ref.behind_ref.refs_1_, f32[1,2,2048,256]{3,2,1,0:T(8,128)S(1)} %gather.1._, bf16[2,2,256,256]{3,2,1,0:T(8,128)(2,1)S(1)} %collective-permute-done.9.a_swap), custom_call_target="tpu_custom_call", output_to_operand_aliasing={{0}: (1, {})} | custom-call | tf_op jit(solution)/shard_map/merge/pallas_call | solution.py:772
  56.6 0.2 collective-permute-done.10.a_back
  56.7 5.9 %collective-permute-done.11.a_back_cross = bf16[2,512,128]{2,1,0:T(8,128)(2,1)S(1)} collective-permute-done((bf16[2,512,128]{2,1,0:T(8,128)(2,1)S(1)}, bf16[2,512,128]{2,1,0:T(8,128)(2,1)S(1)}, u32[]{:S(2)}, u32[]{:S(2)}) %collective-permute-start.11) | collective-permute-done | bytes 262176 | tf_op jit(solution)/shard_map/ppermute | solution.py:31
  62.7 1.8 %finish.1 = (f32[1,2,2048,256]{3,2,1,0:T(8,128)S(1)}, f32[1,2,2048,256]{3,2,1,0:T(8,128)}) custom-call(s32[1,64]{1,0:T(1,128)S(1)} %get-tuple-element.25.own_ref.behind_ref.refs_1_, s32[8,128]{1,0:T(8,128)S(1)} %get-tuple-element.29.behind_ref.refs_0_, f32[1,2,2048,256]{3,2,1,0:T(8,128)S(1)} %get-tuple-element.40._, ...), custom_call_target="tpu_custom_call", output_to_operand_aliasing={{0}: (2, {}), {1}: (3, {})} | custom-call | tf_op jit(solution)/shard_map/finish/pallas_call | solution.py:772
Async XLA Ops:
  0.0 10.7 %copy-start = (f32[1,256,256]{2,1,0:T(8,128)S(1)}, f32[1,256,256]{2,1,0:T(8,128)}, u32[]{:S(2)}) copy-start(f32[1,256,256]{2,1,0:T(8,128)} %self_ref.1) | copy-start | bytes 786436
  3.6 13.4 %collective-permute-start = (bf16[2,2048,256]{2,1,0:T(8,128)(2,1)S(1)}, bf16[2,2048,256]{2,1,0:T(8,128)(2,1)S(1)}, u32[]{:S(2)}, u32[]{:S(2)}) collective-permute-start(bf16[2,2048,256]{2,1,0:T(8,128)(2,1)S(1)} %get-tuple-element.26.self_ref), channel_id=1, source_target_pairs={{0,16},{1,17},{2,18},{3,19},{4,20},{5,21},{6,22},{7,23},{8,24},{9,... | collective-permute-start | bytes 6291464 | tf_op jit(solution)/shard_map/ppermute | solution.py:31
  4.3 13.9 %collective-permute-start.1 = (bf16[1040,128]{1,0:T(8,128)(2,1)S(1)}, bf16[1040,128]{1,0:T(8,128)(2,1)S(1)}, u32[]{:S(2)}, u32[]{:S(2)}) collective-permute-start(bf16[1040,128]{1,0:T(8,128)(2,1)S(1)} %get-tuple-element.27), channel_id=1, source_target_pairs={{0,1},{1,2},{2,3},{3,4},{4,5},{5,6},{6,7},{7,8},{8,9},{9,10},{10,1... | collective-permute-start | bytes 798728 | tf_op jit(solution)/shard_map/ppermute | solution.py:31
  7.4 18.1 %collective-permute-start.4 = (bf16[1040,128]{1,0:T(8,128)(2,1)S(1)}, bf16[1040,128]{1,0:T(8,128)(2,1)S(1)}, u32[]{:S(2)}, u32[]{:S(2)}) collective-permute-start(bf16[1040,128]{1,0:T(8,128)(2,1)S(1)} %get-tuple-element.28._), channel_id=1, source_target_pairs={{0,17},{1,18},{2,19},{3,20},{4,21},{5,22},{6,23},{7,24},{8,25},{9,... | collective-permute-start | bytes 798728 | tf_op jit(solution)/shard_map/ppermute | solution.py:31
  10.8 5.0 %collective-permute-start.2 = (f32[1,256,256]{2,1,0:T(8,128)S(1)}, f32[1,256,256]{2,1,0:T(8,128)S(1)}, u32[]{:S(2)}, u32[]{:S(2)}) collective-permute-start(f32[1,256,256]{2,1,0:T(8,128)S(1)} %copy-done), channel_id=1, source_target_pairs={{0,16},{1,17},{2,18},{3,19},{4,20},{5,21},{6,22},{7,23},{8,24},{9,... | collective-permute-start | bytes 786440 | tf_op jit(solution)/shard_map/ppermute | solution.py:31
  12.6 16.3 %collective-permute-start.3 = (bf16[2,256,256]{2,1,0:T(8,128)(2,1)S(1)}, bf16[2,256,256]{2,1,0:T(8,128)(2,1)S(1)}, u32[]{:S(2)}, u32[]{:S(2)}) collective-permute-start(bf16[2,256,256]{2,1,0:T(8,128)(2,1)S(1)} %levels.1._), channel_id=1, source_target_pairs={{0,1},{1,2},{2,3},{3,4},{4,5},{5,6},{6,7},{7,8},{8,9},{9,10},{10,1... | collective-permute-start | bytes 786440 | tf_op jit(solution)/shard_map/ppermute | solution.py:31
  20.1 5.4 %copy-start.1 = (f32[2,256,256]{2,1,0:T(8,128)S(1)}, f32[2,256,256]{2,1,0:T(8,128)}, u32[]{:S(2)}) copy-start(f32[2,256,256]{2,1,0:T(8,128)} %refs_5_.1) | copy-start | bytes 1572868
  20.1 5.4 %copy-start.2 = (bf16[512,512]{1,0:T(8,128)(2,1)S(1)}, bf16[512,512]{1,0:T(8,128)(2,1)}, u32[]{:S(2)}) copy-start(bf16[512,512]{1,0:T(8,128)(2,1)} %constant.5.clone.two_ref.refs_7_) | copy-start | bytes 1572868
  20.1 5.4 %copy-start.3 = (bf16[512,512]{1,0:T(8,128)(2,1)S(1)}, bf16[512,512]{1,0:T(8,128)(2,1)}, u32[]{:S(2)}) copy-start(bf16[512,512]{1,0:T(8,128)(2,1)} %constant.4.clone.one_ref.refs_6_) | copy-start | bytes 1572868
  20.2 19.0 %collective-permute-start.8 = (bf16[2,2,512,128]{3,2,1,0:T(8,128)(2,1)S(1)}, bf16[2,2,512,128]{3,2,1,0:T(8,128)(2,1)S(1)}, u32[]{:S(2)}, u32[]{:S(2)}) collective-permute-start(bf16[2,2,512,128]{3,2,1,0:T(8,128)(2,1)S(1)} %get-tuple-element.30._), channel_id=1, source_target_pairs={{1,0},{2,1},{3,2},{4,3},{5,4},{6,5},{7,6},{8,7},{9,8},{10,9},{11,1... | collective-permute-start | bytes 1572872 | tf_op jit(solution)/shard_map/ppermute | solution.py:31
  32.6 19.5 %collective-permute-start.5 = (bf16[3,2,256,256]{3,2,1,0:T(8,128)(2,1)S(1)}, bf16[3,2,256,256]{3,2,1,0:T(8,128)(2,1)S(1)}, u32[]{:S(2)}, u32[]{:S(2)}) collective-permute-start(bf16[3,2,256,256]{3,2,1,0:T(8,128)(2,1)S(1)} %get-tuple-element.35), channel_id=1, source_target_pairs={{0,16},{1,17},{2,18},{3,19},{4,20},{5,21},{6,22},{7,23},{8,24},{9,... | collective-permute-start | bytes 2359304 | tf_op jit(solution)/shard_map/ppermute | solution.py:31
  33.5 18.4 %collective-permute-start.6 = (bf16[2,512,128]{2,1,0:T(8,128)(2,1)S(1)}, bf16[2,512,128]{2,1,0:T(8,128)(2,1)S(1)}, u32[]{:S(2)}, u32[]{:S(2)}) collective-permute-start(bf16[2,512,128]{2,1,0:T(8,128)(2,1)S(1)} %get-tuple-element.36), channel_id=1, source_target_pairs={{1,0},{2,1},{3,2},{4,3},{5,4},{6,5},{7,6},{8,7},{9,8},{10,9},{11,1... | collective-permute-start | bytes 786440 | tf_op jit(solution)/shard_map/ppermute | solution.py:31
  35.7 16.4 %collective-permute-start.7 = (bf16[2,512,128]{2,1,0:T(8,128)(2,1)S(1)}, bf16[2,512,128]{2,1,0:T(8,128)(2,1)S(1)}, u32[]{:S(2)}, u32[]{:S(2)}) collective-permute-start(bf16[2,512,128]{2,1,0:T(8,128)(2,1)S(1)} %get-tuple-element.37), channel_id=1, source_target_pairs={{1,16},{2,17},{3,18},{4,19},{5,20},{6,21},{7,22},{8,23},{9,24},{10... | collective-permute-start | bytes 786440 | tf_op jit(solution)/shard_map/ppermute | solution.py:31
  45.3 11.4 %collective-permute-start.10 = (bf16[2,512,128]{2,1,0:T(8,128)(2,1)S(1)}, bf16[2,512,128]{2,1,0:T(8,128)(2,1)S(1)}, u32[]{:S(2)}, u32[]{:S(2)}) collective-permute-start(bf16[2,512,128]{2,1,0:T(8,128)(2,1)S(1)} %get-tuple-element.42), channel_id=1, source_target_pairs={{0,1},{1,2},{2,3},{3,4},{4,5},{5,6},{6,7},{7,8},{8,9},{9,10},{10,1... | collective-permute-start | bytes 786440 | tf_op jit(solution)/shard_map/ppermute | solution.py:31
  47.6 15.1 %collective-permute-start.11 = (bf16[2,512,128]{2,1,0:T(8,128)(2,1)S(1)}, bf16[2,512,128]{2,1,0:T(8,128)(2,1)S(1)}, u32[]{:S(2)}, u32[]{:S(2)}) collective-permute-start(bf16[2,512,128]{2,1,0:T(8,128)(2,1)S(1)} %get-tuple-element.43), channel_id=1, source_target_pairs={{0,17},{1,18},{2,19},{3,20},{4,21},{5,22},{6,23},{7,24},{8,25},{9,... | collective-permute-start | bytes 786440 | tf_op jit(solution)/shard_map/ppermute | solution.py:31
  52.0 2.0 %collective-permute-start.9 = (bf16[2,2,256,256]{3,2,1,0:T(8,128)(2,1)S(1)}, bf16[2,2,256,256]{3,2,1,0:T(8,128)(2,1)S(1)}, u32[]{:S(2)}, u32[]{:S(2)}) collective-permute-start(bf16[2,2,256,256]{3,2,1,0:T(8,128)(2,1)S(1)} %get-tuple-element.39), channel_id=1, source_target_pairs={{0,16},{1,17},{2,18},{3,19},{4,20},{5,21},{6,22},{7,23},{8,24},{9,... | collective-permute-start | bytes 1572872 | tf_op jit(solution)/shard_map/ppermute | solution.py:31

commit v5 on v4

--- a/solution.py
+++ b/solution.py
@@ -408,24 +408,26 @@
 
 
 def forward_kernel(
-    reach, behind_ref, own_ref, straight_ref, cross_ref, part_ref, phase, probe_ref, one_ref, two_ref,
-    patch, wave, leave, field, half,
+    reach, behind_ref, own_ref, straight_ref, cross_ref, self_ref, other_ref, phase, probe_ref, one_ref,
+    two_ref, patch, wave, leave, field, half,
 ):
-    width = probe_ref.shape[-1]
+    height, width = self_ref.shape[1:]
     core, table, late, lone, turns = turns_of(behind_ref, own_ref)
     lane = columns((width, width))
     spread = functools.partial(propagate, field, half, phase, one_ref, two_ref)
 
     def one_pair(step, _):
         entries, spare = pair_of(step, table, late, lone, core)
-        masks = [(lane < width - entries[item][3]) & jnp.logical_not(spare[item]) for item in range(2)]
-        for source, ref in ((core, straight_ref), (1 - core, cross_ref)):
+        for source, ref, near_ref in ((core, straight_ref, self_ref), (1 - core, cross_ref, other_ref)):
             for plane in range(2):
                 page = unfold(ref[plane * 2 * reach : (plane + 1) * 2 * reach].astype(F32), width, reach)
                 for item in range(2):
-                    foreign = page if item else turn(page, 2 * width - reach - entries[item][3], width)
-                    own = part_ref[jnp.where(spare[item], 2, item), source, plane].astype(F32)
-                    patch[step, source, item, plane] = jnp.where(masks[item], foreign, own).astype(BF16)
+                    _, _, row, col = entries[item]
+                    foreign = page if item else turn(page, 2 * width - reach - col, width)
+                    near = turn(patch_rows(near_ref, (), plane, row, height, width), width - col, width)
+                    head = jnp.where(spare[item], near, foreign)
+                    tail = jnp.where(spare[item], 0.0, near)
+                    patch[step, source, item, plane] = jnp.where(lane < width - col, head, tail).astype(BF16)
         for item in range(2):
             left_re, left_im = probe_ref[0], probe_ref[1]
             right_re, right_im = [patch[step, 0, item, plane].astype(F32) for plane in range(2)]
@@ -851,7 +853,6 @@
             [pltpu.VMEM((EXTRA, LANES), jnp.int32), pltpu.SemaphoreType.DMA(())],
             out_specs=[vmem, smem],
         )
-        b_part = parts("B", behind, page)
         page = send(page, 0, -1)
         table = [(smem, behind), (smem, own)]
         optics = [(vmem, value) for value in (turned, probe_field, one, two)]
@@ -859,7 +860,7 @@
         states = call(
             functools.partial(forward_kernel, reach),
             "waves_forward",
-            table + [(vmem, value) for value in (b_straight, b_cross, b_part)] + optics,
+            table + [(vmem, value) for value in (b_straight, b_cross, small, small_other)] + optics,
             [planes(2, 2, 2, 2), planes(2, 2, 2), planes(2, 2, 2)],
             fields,
             3,

time: 64.9 us -> 65.2 us (level)
  Pallas kernels: 28.8 us -> 30.1 us
  waiting for transfers between devices: 6.84 us -> 5.88 us
    pallas_call x12 -> x11, Pallas kernels: 28.8 us -> 30.1 us  [call(): pl.pallas_call(kernel, out_shape=out_shape, in_specs=[spec for spec, _ in...]
    ppermute x12, waiting for transfers between devices: 6.84 us -> 5.88 us  [send(): return lax.ppermute(value, ('cuts', 'tile'), pairs)]
  transfers between devices with their start and end apart: 12 -> 12, of which waited for: 3 -> 1; matrix products, arithmetic and copies ran while one was open for 0% -> 0% of each run, Pallas kernels for 37% -> 39%
where the time goes in v5:
time: 65.2 us; the launch traced here: 64.9 us
  Pallas kernels  30.1 us (46%)
  starting transfers between devices  27.7 us (42%)
  waiting for transfers between devices  5.88 us (9%)
  between operations  1.12 us (2%)
    pallas_call x11, Pallas kernels, call(): pl.pallas_call(kernel, out_shape=out_shape, in_specs=[spec for spec, _ in...  30.1 us
    ppermute x12, starting transfers between devices, send(): return lax.ppermute(value, ('cuts', 'tile'), pairs)  27.7 us
    ppermute x12, waiting for transfers between devices, send(): return lax.ppermute(value, ('cuts', 'tile'), pairs)  5.88 us
  transfers between devices with their start and end apart: 12, of which 1 were waited for; matrix products, arithmetic and copies ran while one was open for 0% of the time, Pallas kernels for 39%

profile of v5, /device:TPU:17, one launch (start us, length us, event | category | flops | bytes accessed | tf_op | source)
XLA Modules:
  0.0 64.9 jit_solution(9150757878416465766)
XLA Ops:
  0.0 0.0 copy-start
  0.7 2.9 %first.1 = (s32[1,64]{1,0:T(1,128)S(1)}, bf16[2,2048,256]{2,1,0:T(8,128)(2,1)S(1)}, bf16[1040,128]{1,0:T(8,128)(2,1)S(1)}, bf16[1040,128]{1,0:T(8,128)(2,1)S(1)}) custom-call(s32[1]{0:T(128)S(6)} %copy.17.counts_ref, s32[1,6]{1,0:T(1,128)} %chosen_hbm.1, s32[1,8]{1,0:T(1,128)} %row_hbm.1, s32[1,8]{1,0:T(1,128)} %col_hbm.1, f32[1,2,2048,256]{3,2,1,0:T(8,128)} %object_ref.1), custom_call_target="tpu_custom_call" | custom-call | tf_op jit(solution)/shard_map/first/pallas_call | solution.py:774
  3.6 0.7 %collective-permute-start = (bf16[2,2048,256]{2,1,0:T(8,128)(2,1)S(1)}, bf16[2,2048,256]{2,1,0:T(8,128)(2,1)S(1)}, u32[]{:S(2)}, u32[]{:S(2)}) collective-permute-start(bf16[2,2048,256]{2,1,0:T(8,128)(2,1)S(1)} %get-tuple-element.26.self_ref), channel_id=1, source_target_pairs={{0,16},{1,17},{2,18},{3,19},{4,20},{5,21},{6,22},{7,23},{8,24},{9,... | collective-permute-start | bytes 6291464 | tf_op jit(solution)/shard_map/ppermute | solution.py:31
  4.3 3.1 %collective-permute-start.1 = (bf16[1040,128]{1,0:T(8,128)(2,1)S(1)}, bf16[1040,128]{1,0:T(8,128)(2,1)S(1)}, u32[]{:S(2)}, u32[]{:S(2)}) collective-permute-start(bf16[1040,128]{1,0:T(8,128)(2,1)S(1)} %get-tuple-element.27), channel_id=1, source_target_pairs={{0,1},{1,2},{2,3},{3,4},{4,5},{5,6},{6,7},{7,8},{8,9},{9,10},{10,1... | collective-permute-start | bytes 798728 | tf_op jit(solution)/shard_map/ppermute | solution.py:31
  7.4 3.3 %collective-permute-start.4 = (bf16[1040,128]{1,0:T(8,128)(2,1)S(1)}, bf16[1040,128]{1,0:T(8,128)(2,1)S(1)}, u32[]{:S(2)}, u32[]{:S(2)}) collective-permute-start(bf16[1040,128]{1,0:T(8,128)(2,1)S(1)} %get-tuple-element.28._), channel_id=1, source_target_pairs={{0,17},{1,18},{2,19},{3,20},{4,21},{5,22},{6,23},{7,24},{8,25},{9,... | collective-permute-start | bytes 798728 | tf_op jit(solution)/shard_map/ppermute | solution.py:31
  10.7 0.0 copy-done
  10.8 0.3 collective-permute-start.2
  11.0 1.6 %levels.1._ = bf16[2,256,256]{2,1,0:T(8,128)(2,1)S(1)} custom-call(s32[1,64]{1,0:T(1,128)S(1)} %get-tuple-element.25.own_ref.behind_ref.refs_1_, f32[1,8,256,256]{3,2,1,0:T(8,128)} %refs_8_.1, bf16[1040,128]{1,0:T(8,128)(2,1)S(1)} %get-tuple-element.28._), custom_call_target="tpu_custom_call" | custom-call | tf_op jit(solution)/shard_map/levels/pallas_call | solution.py:774
  12.6 3.1 %collective-permute-start.3 = (bf16[2,256,256]{2,1,0:T(8,128)(2,1)S(1)}, bf16[2,256,256]{2,1,0:T(8,128)(2,1)S(1)}, u32[]{:S(2)}, u32[]{:S(2)}) collective-permute-start(bf16[2,256,256]{2,1,0:T(8,128)(2,1)S(1)} %levels.1._), channel_id=1, source_target_pairs={{0,1},{1,2},{2,3},{3,4},{4,5},{5,6},{6,7},{7,8},{8,9},{9,10},{10,1... | collective-permute-start | bytes 786440 | tf_op jit(solution)/shard_map/ppermute | solution.py:31
  15.8 0.0 collective-permute-done.2.other_ref
  15.8 1.2 %angles.1._.phase.refs_4_ = f32[2,2,256,256]{3,2,1,0:T(8,128)S(1)} custom-call(s32[1,64]{1,0:T(1,128)S(1)} %get-tuple-element.25.own_ref.behind_ref.refs_1_, f32[1,256,256]{2,1,0:T(8,128)S(1)} %copy-done, f32[1,256,256]{2,1,0:T(8,128)S(1)} %collective-permute-done.2.other_ref, bf16[2,256,256]{2,1,0:T(8,128)(2,1)S(1)} %levels.1._), custom_call_target="tpu_custom_call" | custom-call | tf_op jit(solution)/shard_map/angles/pallas_call | solution.py:774
  17.0 0.0 collective-permute-done.other_ref
  17.0 1.2 %parts_a.1._.refs_3_ = bf16[2,2,2,256,256]{4,3,2,1,0:T(8,128)(2,1)S(1)} custom-call(s32[1,64]{1,0:T(1,128)S(1)} %get-tuple-element.25.own_ref.behind_ref.refs_1_, s32[1,64]{1,0:T(1,128)S(1)} %get-tuple-element.25.own_ref.behind_ref.refs_1_, bf16[2,2048,256]{2,1,0:T(8,128)(2,1)S(1)} %get-tuple-element.26.self_ref, ...), custom_call_target="tpu_custom_call" | custom-call | tf_op jit(solution)/shard_map/parts_a/pallas_call | solution.py:774
  18.2 0.0 copy-start.1
  18.2 0.0 copy-start.2
  18.2 0.0 copy-start.3
  18.2 0.0 collective-permute-done.1.message_ref.straight_ref
  18.2 1.9 %pages.1 = (bf16[2,2,512,128]{3,2,1,0:T(8,128)(2,1)S(1)}, s32[8,128]{1,0:T(8,128)S(1)}) custom-call(s32[1,64]{1,0:T(1,128)S(1)} %get-tuple-element.25.own_ref.behind_ref.refs_1_, bf16[2,2048,256]{2,1,0:T(8,128)(2,1)S(1)} %get-tuple-element.26.self_ref, bf16[2,2048,256]{2,1,0:T(8,128)(2,1)S(1)} %collective-permute-done.other_ref, ...), custom_call_target="tpu_custom_call" | custom-call | tf_op jit(solution)/shard_map/pages/pallas_call | solution.py:774
  20.2 4.0 %collective-permute-start.8 = (bf16[2,2,512,128]{3,2,1,0:T(8,128)(2,1)S(1)}, bf16[2,2,512,128]{3,2,1,0:T(8,128)(2,1)S(1)}, u32[]{:S(2)}, u32[]{:S(2)}) collective-permute-start(bf16[2,2,512,128]{3,2,1,0:T(8,128)(2,1)S(1)} %get-tuple-element.37), channel_id=1, source_target_pairs={{1,0},{2,1},{3,2},{4,3},{5,4},{6,5},{7,6},{8,7},{9,8},{10,9},{11,1... | collective-permute-start | bytes 1572872 | tf_op jit(solution)/shard_map/ppermute | solution.py:31
  24.1 0.0 collective-permute-done.4.cross_ref
  24.1 0.0 copy-done.1
  24.1 0.0 copy-done.2
  24.2 0.0 copy-done.3
  24.2 4.2 %waves_forward.1 = (bf16[2,2,2,2,256,256]{5,4,3,2,1,0:T(8,128)(2,1)S(1)}, bf16[2,2,2,256,256]{4,3,2,1,0:T(8,128)(2,1)S(1)}, bf16[2,2,2,256,256]{4,3,2,1,0:T(8,128)(2,1)S(1)}) custom-call(s32[8,128]{1,0:T(8,128)S(1)} %get-tuple-element.29.behind_ref.refs_0_, s32[1,64]{1,0:T(1,128)S(1)} %get-tuple-element.25.own_ref.behind_ref.refs_1_, ...), custom_call_target="tpu_custom_call" | custom-call | flops 3000000000 | bytes 9000000 | tf_op jit(solution)/shard_map/waves_forward/pallas_call | solution.py:774
  28.4 0.0 collective-permute-done.3.level_ref
  28.4 3.8 %waves_back.1 = (bf16[2,512,128]{2,1,0:T(8,128)(2,1)S(1)}, bf16[2,512,128]{2,1,0:T(8,128)(2,1)S(1)}, bf16[3,2,256,256]{3,2,1,0:T(8,128)(2,1)S(1)}, bf16[3,2,256,256]{3,2,1,0:T(8,128)(2,1)S(1)}) custom-call(s32[8,128]{1,0:T(8,128)S(1)} %get-tuple-element.29.behind_ref.refs_0_, s32[1,64]{1,0:T(1,128)S(1)} %get-tuple-element.25.own_ref.behind_ref.refs_1_, ...), custom_call_target="tpu_custom_call" | custom-call | flops 4000000000 | bytes 12000000 | tf_op jit(solution)/shard_map/waves_back/pallas_call | solution.py:774
  32.2 0.9 %collective-permute-start.5 = (bf16[3,2,256,256]{3,2,1,0:T(8,128)(2,1)S(1)}, bf16[3,2,256,256]{3,2,1,0:T(8,128)(2,1)S(1)}, u32[]{:S(2)}, u32[]{:S(2)}) collective-permute-start(bf16[3,2,256,256]{3,2,1,0:T(8,128)(2,1)S(1)} %get-tuple-element.34), channel_id=1, source_target_pairs={{0,16},{1,17},{2,18},{3,19},{4,20},{5,21},{6,22},{7,23},{8,24},{9,... | collective-permute-start | bytes 2359304 | tf_op jit(solution)/shard_map/ppermute | solution.py:31
  33.1 2.2 %collective-permute-start.6 = (bf16[2,512,128]{2,1,0:T(8,128)(2,1)S(1)}, bf16[2,512,128]{2,1,0:T(8,128)(2,1)S(1)}, u32[]{:S(2)}, u32[]{:S(2)}) collective-permute-start(bf16[2,512,128]{2,1,0:T(8,128)(2,1)S(1)} %get-tuple-element.35), channel_id=1, source_target_pairs={{1,0},{2,1},{3,2},{4,3},{5,4},{6,5},{7,6},{8,7},{9,8},{10,9},{11,1... | collective-permute-start | bytes 786440 | tf_op jit(solution)/shard_map/ppermute | solution.py:31
  35.3 3.4 %collective-permute-start.7 = (bf16[2,512,128]{2,1,0:T(8,128)(2,1)S(1)}, bf16[2,512,128]{2,1,0:T(8,128)(2,1)S(1)}, u32[]{:S(2)}, u32[]{:S(2)}) collective-permute-start(bf16[2,512,128]{2,1,0:T(8,128)(2,1)S(1)} %get-tuple-element.36), channel_id=1, source_target_pairs={{1,16},{2,17},{3,18},{4,19},{5,20},{6,21},{7,22},{8,23},{9,24},{10... | collective-permute-start | bytes 786440 | tf_op jit(solution)/shard_map/ppermute | solution.py:31
  38.7 0.0 collective-permute-done.8.refs_2_
  38.7 6.6 %waves_a.1 = (bf16[2,512,128]{2,1,0:T(8,128)(2,1)S(1)}, bf16[2,512,128]{2,1,0:T(8,128)(2,1)S(1)}, bf16[2,2,256,256]{3,2,1,0:T(8,128)(2,1)S(1)}, bf16[2,2,256,256]{3,2,1,0:T(8,128)(2,1)S(1)}) custom-call(s32[8,128]{1,0:T(8,128)S(1)} %get-tuple-element.29.behind_ref.refs_0_, s32[1,64]{1,0:T(1,128)S(1)} %get-tuple-element.25.own_ref.behind_ref.refs_1_, ...), custom_call_target="tpu_custom_call" | custom-call | flops 7000000000 | bytes 21000000 | tf_op jit(solution)/shard_map/waves_a/pallas_call | solution.py:774
  45.3 2.2 %collective-permute-start.10 = (bf16[2,512,128]{2,1,0:T(8,128)(2,1)S(1)}, bf16[2,512,128]{2,1,0:T(8,128)(2,1)S(1)}, u32[]{:S(2)}, u32[]{:S(2)}) collective-permute-start(bf16[2,512,128]{2,1,0:T(8,128)(2,1)S(1)} %get-tuple-element.42), channel_id=1, source_target_pairs={{0,1},{1,2},{2,3},{3,4},{4,5},{5,6},{6,7},{7,8},{8,9},{9,10},{10,1... | collective-permute-start | bytes 786440 | tf_op jit(solution)/shard_map/ppermute | solution.py:31
  47.5 4.4 %collective-permute-start.11 = (bf16[2,512,128]{2,1,0:T(8,128)(2,1)S(1)}, bf16[2,512,128]{2,1,0:T(8,128)(2,1)S(1)}, u32[]{:S(2)}, u32[]{:S(2)}) collective-permute-start(bf16[2,512,128]{2,1,0:T(8,128)(2,1)S(1)} %get-tuple-element.43), channel_id=1, source_target_pairs={{0,17},{1,18},{2,19},{3,20},{4,21},{5,22},{6,23},{7,24},{8,25},{9,... | collective-permute-start | bytes 786440 | tf_op jit(solution)/shard_map/ppermute | solution.py:31
  51.9 0.0 collective-permute-done.6.b_back
  51.9 0.1 collective-permute-start.9
  52.0 0.0 collective-permute-done.7.b_back_cross
  52.0 0.0 collective-permute-done.5.b_swap
  52.0 1.8 %gather.1._ = f32[1,2,2048,256]{3,2,1,0:T(8,128)S(1)} custom-call(s32[1,64]{1,0:T(1,128)S(1)} %get-tuple-element.25.own_ref.behind_ref.refs_1_, s32[8,128]{1,0:T(8,128)S(1)} %get-tuple-element.29.behind_ref.refs_0_, bf16[3,2,256,256]{3,2,1,0:T(8,128)(2,1)S(1)} %get-tuple-element.33.refs_9_.b_self, ...), custom_call_target="tpu_custom_call" | custom-call | flops 10000000000 | bytes 30000000 | tf_op jit(solution)/shard_map/gather/pallas_call | solution.py:774
  53.9 0.0 collective-permute-done.9.a_swap
  53.9 2.9 %merge.1 = (f32[1,2,2048,256]{3,2,1,0:T(8,128)S(1)}, f32[1,2,2048,256]{3,2,1,0:T(8,128)}) custom-call(s32[1,64]{1,0:T(1,128)S(1)} %get-tuple-element.25.own_ref.behind_ref.refs_1_, f32[1,2,2048,256]{3,2,1,0:T(8,128)S(1)} %gather.1._, bf16[2,2,256,256]{3,2,1,0:T(8,128)(2,1)S(1)} %collective-permute-done.9.a_swap), custom_call_target="tpu_custom_call", output_to_operand_aliasing={{0}: (1, {})} | custom-call | tf_op jit(solution)/shard_map/merge/pallas_call | solution.py:774
  56.8 0.0 collective-permute-done.10.a_back
  56.8 5.8 %collective-permute-done.11.a_back_cross = bf16[2,512,128]{2,1,0:T(8,128)(2,1)S(1)} collective-permute-done((bf16[2,512,128]{2,1,0:T(8,128)(2,1)S(1)}, bf16[2,512,128]{2,1,0:T(8,128)(2,1)S(1)}, u32[]{:S(2)}, u32[]{:S(2)}) %collective-permute-start.11) | collective-permute-done | bytes 262176 | tf_op jit(solution)/shard_map/ppermute | solution.py:31
  62.6 2.1 %finish.1 = (f32[1,2,2048,256]{3,2,1,0:T(8,128)S(1)}, f32[1,2,2048,256]{3,2,1,0:T(8,128)}) custom-call(s32[1,64]{1,0:T(1,128)S(1)} %get-tuple-element.25.own_ref.behind_ref.refs_1_, s32[8,128]{1,0:T(8,128)S(1)} %get-tuple-element.29.behind_ref.refs_0_, f32[1,2,2048,256]{3,2,1,0:T(8,128)S(1)} %get-tuple-element.40._, ...), custom_call_target="tpu_custom_call", output_to_operand_aliasing={{0}: (2, {}), {1}: (3, {})} | custom-call | tf_op jit(solution)/shard_map/finish/pallas_call | solution.py:774
Async XLA Ops:
  0.0 10.7 %copy-start = (f32[1,256,256]{2,1,0:T(8,128)S(1)}, f32[1,256,256]{2,1,0:T(8,128)}, u32[]{:S(2)}) copy-start(f32[1,256,256]{2,1,0:T(8,128)} %self_ref.1) | copy-start | bytes 786436
  3.6 13.4 %collective-permute-start = (bf16[2,2048,256]{2,1,0:T(8,128)(2,1)S(1)}, bf16[2,2048,256]{2,1,0:T(8,128)(2,1)S(1)}, u32[]{:S(2)}, u32[]{:S(2)}) collective-permute-start(bf16[2,2048,256]{2,1,0:T(8,128)(2,1)S(1)} %get-tuple-element.26.self_ref), channel_id=1, source_target_pairs={{0,16},{1,17},{2,18},{3,19},{4,20},{5,21},{6,22},{7,23},{8,24},{9,... | collective-permute-start | bytes 6291464 | tf_op jit(solution)/shard_map/ppermute | solution.py:31
  4.3 13.9 %collective-permute-start.1 = (bf16[1040,128]{1,0:T(8,128)(2,1)S(1)}, bf16[1040,128]{1,0:T(8,128)(2,1)S(1)}, u32[]{:S(2)}, u32[]{:S(2)}) collective-permute-start(bf16[1040,128]{1,0:T(8,128)(2,1)S(1)} %get-tuple-element.27), channel_id=1, source_target_pairs={{0,1},{1,2},{2,3},{3,4},{4,5},{5,6},{6,7},{7,8},{8,9},{9,10},{10,1... | collective-permute-start | bytes 798728 | tf_op jit(solution)/shard_map/ppermute | solution.py:31
  7.4 16.7 %collective-permute-start.4 = (bf16[1040,128]{1,0:T(8,128)(2,1)S(1)}, bf16[1040,128]{1,0:T(8,128)(2,1)S(1)}, u32[]{:S(2)}, u32[]{:S(2)}) collective-permute-start(bf16[1040,128]{1,0:T(8,128)(2,1)S(1)} %get-tuple-element.28._), channel_id=1, source_target_pairs={{0,17},{1,18},{2,19},{3,20},{4,21},{5,22},{6,23},{7,24},{8,25},{9,... | collective-permute-start | bytes 798728 | tf_op jit(solution)/shard_map/ppermute | solution.py:31
  10.8 5.0 %collective-permute-start.2 = (f32[1,256,256]{2,1,0:T(8,128)S(1)}, f32[1,256,256]{2,1,0:T(8,128)S(1)}, u32[]{:S(2)}, u32[]{:S(2)}) collective-permute-start(f32[1,256,256]{2,1,0:T(8,128)S(1)} %copy-done), channel_id=1, source_target_pairs={{0,16},{1,17},{2,18},{3,19},{4,20},{5,21},{6,22},{7,23},{8,24},{9,... | collective-permute-start | bytes 786440 | tf_op jit(solution)/shard_map/ppermute | solution.py:31
  12.6 15.7 %collective-permute-start.3 = (bf16[2,256,256]{2,1,0:T(8,128)(2,1)S(1)}, bf16[2,256,256]{2,1,0:T(8,128)(2,1)S(1)}, u32[]{:S(2)}, u32[]{:S(2)}) collective-permute-start(bf16[2,256,256]{2,1,0:T(8,128)(2,1)S(1)} %levels.1._), channel_id=1, source_target_pairs={{0,1},{1,2},{2,3},{3,4},{4,5},{5,6},{6,7},{7,8},{8,9},{9,10},{10,1... | collective-permute-start | bytes 786440 | tf_op jit(solution)/shard_map/ppermute | solution.py:31
  18.2 5.9 %copy-start.1 = (f32[2,256,256]{2,1,0:T(8,128)S(1)}, f32[2,256,256]{2,1,0:T(8,128)}, u32[]{:S(2)}) copy-start(f32[2,256,256]{2,1,0:T(8,128)} %refs_5_.1) | copy-start | bytes 1572868
  18.2 5.9 %copy-start.2 = (bf16[512,512]{1,0:T(8,128)(2,1)S(1)}, bf16[512,512]{1,0:T(8,128)(2,1)}, u32[]{:S(2)}) copy-start(bf16[512,512]{1,0:T(8,128)(2,1)} %constant.5.clone.two_ref.refs_7_) | copy-start | bytes 1572868
  18.2 5.9 %copy-start.3 = (bf16[512,512]{1,0:T(8,128)(2,1)S(1)}, bf16[512,512]{1,0:T(8,128)(2,1)}, u32[]{:S(2)}) copy-start(bf16[512,512]{1,0:T(8,128)(2,1)} %constant.4.clone.one_ref.refs_6_) | copy-start | bytes 1572868
  20.2 18.6 %collective-permute-start.8 = (bf16[2,2,512,128]{3,2,1,0:T(8,128)(2,1)S(1)}, bf16[2,2,512,128]{3,2,1,0:T(8,128)(2,1)S(1)}, u32[]{:S(2)}, u32[]{:S(2)}) collective-permute-start(bf16[2,2,512,128]{3,2,1,0:T(8,128)(2,1)S(1)} %get-tuple-element.37), channel_id=1, source_target_pairs={{1,0},{2,1},{3,2},{4,3},{5,4},{6,5},{7,6},{8,7},{9,8},{10,9},{11,1... | collective-permute-start | bytes 1572872 | tf_op jit(solution)/shard_map/ppermute | solution.py:31
  32.2 19.9 %collective-permute-start.5 = (bf16[3,2,256,256]{3,2,1,0:T(8,128)(2,1)S(1)}, bf16[3,2,256,256]{3,2,1,0:T(8,128)(2,1)S(1)}, u32[]{:S(2)}, u32[]{:S(2)}) collective-permute-start(bf16[3,2,256,256]{3,2,1,0:T(8,128)(2,1)S(1)} %get-tuple-element.34), channel_id=1, source_target_pairs={{0,16},{1,17},{2,18},{3,19},{4,20},{5,21},{6,22},{7,23},{8,24},{9,... | collective-permute-start | bytes 2359304 | tf_op jit(solution)/shard_map/ppermute | solution.py:31
  33.1 18.8 %collective-permute-start.6 = (bf16[2,512,128]{2,1,0:T(8,128)(2,1)S(1)}, bf16[2,512,128]{2,1,0:T(8,128)(2,1)S(1)}, u32[]{:S(2)}, u32[]{:S(2)}) collective-permute-start(bf16[2,512,128]{2,1,0:T(8,128)(2,1)S(1)} %get-tuple-element.35), channel_id=1, source_target_pairs={{1,0},{2,1},{3,2},{4,3},{5,4},{6,5},{7,6},{8,7},{9,8},{10,9},{11,1... | collective-permute-start | bytes 786440 | tf_op jit(solution)/shard_map/ppermute | solution.py:31
  35.3 16.8 %collective-permute-start.7 = (bf16[2,512,128]{2,1,0:T(8,128)(2,1)S(1)}, bf16[2,512,128]{2,1,0:T(8,128)(2,1)S(1)}, u32[]{:S(2)}, u32[]{:S(2)}) collective-permute-start(bf16[2,512,128]{2,1,0:T(8,128)(2,1)S(1)} %get-tuple-element.36), channel_id=1, source_target_pairs={{1,16},{2,17},{3,18},{4,19},{5,20},{6,21},{7,22},{8,23},{9,24},{10... | collective-permute-start | bytes 786440 | tf_op jit(solution)/shard_map/ppermute | solution.py:31
  45.3 11.5 %collective-permute-start.10 = (bf16[2,512,128]{2,1,0:T(8,128)(2,1)S(1)}, bf16[2,512,128]{2,1,0:T(8,128)(2,1)S(1)}, u32[]{:S(2)}, u32[]{:S(2)}) collective-permute-start(bf16[2,512,128]{2,1,0:T(8,128)(2,1)S(1)} %get-tuple-element.42), channel_id=1, source_target_pairs={{0,1},{1,2},{2,3},{3,4},{4,5},{5,6},{6,7},{7,8},{8,9},{9,10},{10,1... | collective-permute-start | bytes 786440 | tf_op jit(solution)/shard_map/ppermute | solution.py:31
  47.5 15.1 %collective-permute-start.11 = (bf16[2,512,128]{2,1,0:T(8,128)(2,1)S(1)}, bf16[2,512,128]{2,1,0:T(8,128)(2,1)S(1)}, u32[]{:S(2)}, u32[]{:S(2)}) collective-permute-start(bf16[2,512,128]{2,1,0:T(8,128)(2,1)S(1)} %get-tuple-element.43), channel_id=1, source_target_pairs={{0,17},{1,18},{2,19},{3,20},{4,21},{5,22},{6,23},{7,24},{8,25},{9,... | collective-permute-start | bytes 786440 | tf_op jit(solution)/shard_map/ppermute | solution.py:31
  51.9 2.0 %collective-permute-start.9 = (bf16[2,2,256,256]{3,2,1,0:T(8,128)(2,1)S(1)}, bf16[2,2,256,256]{3,2,1,0:T(8,128)(2,1)S(1)}, u32[]{:S(2)}, u32[]{:S(2)}) collective-permute-start(bf16[2,2,256,256]{3,2,1,0:T(8,128)(2,1)S(1)} %get-tuple-element.39), channel_id=1, source_target_pairs={{0,16},{1,17},{2,18},{3,19},{4,20},{5,21},{6,22},{7,23},{8,24},{9,... | collective-permute-start | bytes 1572872 | tf_op jit(solution)/shard_map/ppermute | solution.py:31

commit v6 on v5

--- a/solution.py
+++ b/solution.py
@@ -333,15 +333,14 @@
             out_ref[source, plane] = fold(page, reach).astype(BF16)
 
 
-def parts_kernel(kind, behind_ref, own_ref, self_ref, other_ref, _, out_ref):
+def parts_kernel(own_ref, self_ref, other_ref, angle_ref, angle_other_ref, _, out_ref, turned_ref):
     height, width = self_ref.shape[1:]
     core = own_ref[0, 0]
     own = Table(own_ref)
-    if kind == "A":
-        items = [own.item("A", core, place) for place in range(2)]
-    else:
-        behind = Table(behind_ref)
-        items = [behind.item("B", core, place) for place in range(2)] + [own.item("A", core, 2)]
+    kind = "A"
+    items = [own.item("A", core, place) for place in range(2)]
+    for source, ref in ((core, angle_ref), (1 - core, angle_other_ref)):
+        turned_ref[source, 0], turned_ref[source, 1] = cos_sin(ref[0])
     lane = columns((width, width))
 
     def write(place):
@@ -787,11 +786,6 @@
         folded = lambda *lead: jax.ShapeDtypeStruct((*lead, 2 * reach, LANES), BF16)
         message = jax.ShapeDtypeStruct((4 * reach + HALVES, LANES), BF16)
 
-        def parts(kind, idx, after):
-            operands = [(smem, idx), (smem, own), (vmem, small), (vmem, small_other), (anywhere, after)]
-            shape = planes(2 if kind == "A" else 3, 2, 2)
-            return call(functools.partial(parts_kernel, kind), "parts_" + kind.lower(), operands, shape, [])
-
         def waves(kind, pages, part, *after):
             count = 2 if kind == "A" else 3
             operands = [(smem, behind), (smem, own)]
@@ -835,16 +829,17 @@
             planes(2),
             [pltpu.VMEM((2, width, width), F32), dma(2)],
         )
-        turned = call(
-            angles_kernel,
-            "angles",
-            [(smem, own), (vmem, slice_phase), (vmem, phase_other), (anywhere, level)],
-            jax.ShapeDtypeStruct((2, 2, width, width), F32),
+        b_straight, b_cross = send(b_straight, 0, 1), send(b_cross, 1, 1)
+        level_page = level
+        level = send(level, 0, 1)
+        a_part, turned = call(
+            parts_kernel,
+            "parts_a",
+            [(smem, own), (vmem, small), (vmem, small_other), (vmem, slice_phase), (vmem, phase_other)]
+            + [(anywhere, level_page)],
+            [planes(2, 2, 2), jax.ShapeDtypeStruct((2, 2, width, width), F32)],
             [],
         )
-        b_straight, b_cross = send(b_straight, 0, 1), send(b_cross, 1, 1)
-        level = send(level, 0, 1)
-        a_part = parts("A", own, turned)
         page, behind = call(
             functools.partial(pages_kernel, reach),
             "pages",

time: 65.2 us -> 65.4 us (level)
    pallas_call x11 -> x10, Pallas kernels: 30.1 us -> 30.5 us  [call(): pl.pallas_call(kernel, out_shape=out_shape, in_specs=[spec for spec, _ in...]
where the time goes in v6:
time: 65.4 us; the launch traced here: 65 us
  Pallas kernels  30.5 us (47%)
  starting transfers between devices  27.8 us (43%)
  waiting for transfers between devices  5.59 us (9%)
  between operations  1.12 us (2%)
    pallas_call x10, Pallas kernels, call(): pl.pallas_call(kernel, out_shape=out_shape, in_specs=[spec for spec, _ in...  30.5 us
    ppermute x12, starting transfers between devices, send(): return lax.ppermute(value, ('cuts', 'tile'), pairs)  27.8 us
    ppermute x12, waiting for transfers between devices, send(): return lax.ppermute(value, ('cuts', 'tile'), pairs)  5.59 us
  transfers between devices with their start and end apart: 12, of which 1 were waited for; matrix products, arithmetic and copies ran while one was open for 0% of the time, Pallas kernels for 39%

profile of v6, /device:TPU:17, one launch (start us, length us, event | category | flops | bytes accessed | tf_op | source)
XLA Modules:
  0.0 65.0 jit_solution(1761990149137017483)
XLA Ops:
  0.0 0.0 copy-start
  0.7 2.9 %first.1 = (s32[1,64]{1,0:T(1,128)S(1)}, bf16[2,2048,256]{2,1,0:T(8,128)(2,1)S(1)}, bf16[1040,128]{1,0:T(8,128)(2,1)S(1)}, bf16[1040,128]{1,0:T(8,128)(2,1)S(1)}) custom-call(s32[1]{0:T(128)S(6)} %copy.17.counts_ref, s32[1,6]{1,0:T(1,128)} %chosen_hbm.1, s32[1,8]{1,0:T(1,128)} %row_hbm.1, s32[1,8]{1,0:T(1,128)} %col_hbm.1, f32[1,2,2048,256]{3,2,1,0:T(8,128)} %object_ref.1), custom_call_target="tpu_custom_call" | custom-call | tf_op jit(solution)/shard_map/first/pallas_call | solution.py:773
  3.6 0.7 %collective-permute-start = (bf16[2,2048,256]{2,1,0:T(8,128)(2,1)S(1)}, bf16[2,2048,256]{2,1,0:T(8,128)(2,1)S(1)}, u32[]{:S(2)}, u32[]{:S(2)}) collective-permute-start(bf16[2,2048,256]{2,1,0:T(8,128)(2,1)S(1)} %get-tuple-element.28.self_ref), channel_id=1, source_target_pairs={{0,16},{1,17},{2,18},{3,19},{4,20},{5,21},{6,22},{7,23},{8,24},{9,... | collective-permute-start | bytes 6291464 | tf_op jit(solution)/shard_map/ppermute | solution.py:31
  4.3 3.1 %collective-permute-start.1 = (bf16[1040,128]{1,0:T(8,128)(2,1)S(1)}, bf16[1040,128]{1,0:T(8,128)(2,1)S(1)}, u32[]{:S(2)}, u32[]{:S(2)}) collective-permute-start(bf16[1040,128]{1,0:T(8,128)(2,1)S(1)} %get-tuple-element.29), channel_id=1, source_target_pairs={{0,1},{1,2},{2,3},{3,4},{4,5},{5,6},{6,7},{7,8},{8,9},{9,10},{10,1... | collective-permute-start | bytes 798728 | tf_op jit(solution)/shard_map/ppermute | solution.py:31
  7.4 3.3 %collective-permute-start.4 = (bf16[1040,128]{1,0:T(8,128)(2,1)S(1)}, bf16[1040,128]{1,0:T(8,128)(2,1)S(1)}, u32[]{:S(2)}, u32[]{:S(2)}) collective-permute-start(bf16[1040,128]{1,0:T(8,128)(2,1)S(1)} %get-tuple-element.30._), channel_id=1, source_target_pairs={{0,17},{1,18},{2,19},{3,20},{4,21},{5,22},{6,23},{7,24},{8,25},{9,... | collective-permute-start | bytes 798728 | tf_op jit(solution)/shard_map/ppermute | solution.py:31
  10.7 0.0 copy-done
  10.8 0.3 collective-permute-start.2
  11.0 1.6 %levels.1._ = bf16[2,256,256]{2,1,0:T(8,128)(2,1)S(1)} custom-call(s32[1,64]{1,0:T(1,128)S(1)} %get-tuple-element.27.own_ref.refs_1_, f32[1,8,256,256]{3,2,1,0:T(8,128)} %refs_8_.1, bf16[1040,128]{1,0:T(8,128)(2,1)S(1)} %get-tuple-element.30._), custom_call_target="tpu_custom_call" | custom-call | tf_op jit(solution)/shard_map/levels/pallas_call | solution.py:773
  12.6 0.0 copy-start.1
  12.7 0.0 copy-start.2
  12.7 0.0 copy-start.3
  12.7 3.3 %collective-permute-start.3 = (bf16[2,256,256]{2,1,0:T(8,128)(2,1)S(1)}, bf16[2,256,256]{2,1,0:T(8,128)(2,1)S(1)}, u32[]{:S(2)}, u32[]{:S(2)}) collective-permute-start(bf16[2,256,256]{2,1,0:T(8,128)(2,1)S(1)} %levels.1._), channel_id=1, source_target_pairs={{0,1},{1,2},{2,3},{3,4},{4,5},{5,6},{6,7},{7,8},{8,9},{9,10},{10,1... | collective-permute-start | bytes 786440 | tf_op jit(solution)/shard_map/ppermute | solution.py:31
  15.9 0.0 collective-permute-done.2.angle_other_ref
  15.9 0.0 collective-permute-done.other_ref
  16.0 2.3 %parts_a.1 = (bf16[2,2,2,256,256]{4,3,2,1,0:T(8,128)(2,1)S(1)}, f32[2,2,256,256]{3,2,1,0:T(8,128)S(1)}) custom-call(s32[1,64]{1,0:T(1,128)S(1)} %get-tuple-element.27.own_ref.refs_1_, bf16[2,2048,256]{2,1,0:T(8,128)(2,1)S(1)} %get-tuple-element.28.self_ref, bf16[2,2048,256]{2,1,0:T(8,128)(2,1)S(1)} %collective-permute-done.other_ref, ...), custom_call_target="tpu_custom_call" | custom-call | tf_op jit(solution)/shard_map/parts_a/pallas_call | solution.py:773
  18.2 0.0 collective-permute-done.1.message_ref.straight_ref
  18.2 1.9 %pages.1 = (bf16[2,2,512,128]{3,2,1,0:T(8,128)(2,1)S(1)}, s32[8,128]{1,0:T(8,128)S(1)}) custom-call(s32[1,64]{1,0:T(1,128)S(1)} %get-tuple-element.27.own_ref.refs_1_, bf16[2,2048,256]{2,1,0:T(8,128)(2,1)S(1)} %get-tuple-element.28.self_ref, bf16[2,2048,256]{2,1,0:T(8,128)(2,1)S(1)} %collective-permute-done.other_ref, ...), custom_call_target="tpu_custom_call" | custom-call | tf_op jit(solution)/shard_map/pages/pallas_call | solution.py:773
  20.1 4.0 %collective-permute-start.8 = (bf16[2,2,512,128]{3,2,1,0:T(8,128)(2,1)S(1)}, bf16[2,2,512,128]{3,2,1,0:T(8,128)(2,1)S(1)}, u32[]{:S(2)}, u32[]{:S(2)}) collective-permute-start(bf16[2,2,512,128]{3,2,1,0:T(8,128)(2,1)S(1)} %get-tuple-element.41), channel_id=1, source_target_pairs={{1,0},{2,1},{3,2},{4,3},{5,4},{6,5},{7,6},{8,7},{9,8},{10,9},{11,1... | collective-permute-start | bytes 1572872 | tf_op jit(solution)/shard_map/ppermute | solution.py:31
  24.1 0.0 collective-permute-done.4.cross_ref
  24.1 0.0 copy-done.1
  24.1 0.0 copy-done.2
  24.1 0.0 copy-done.3
  24.2 4.2 %waves_forward.1 = (bf16[2,2,2,2,256,256]{5,4,3,2,1,0:T(8,128)(2,1)S(1)}, bf16[2,2,2,256,256]{4,3,2,1,0:T(8,128)(2,1)S(1)}, bf16[2,2,2,256,256]{4,3,2,1,0:T(8,128)(2,1)S(1)}) custom-call(s32[8,128]{1,0:T(8,128)S(1)} %get-tuple-element.32.behind_ref.refs_0_, s32[1,64]{1,0:T(1,128)S(1)} %get-tuple-element.27.own_ref.refs_1_, ...), custom_call_target="tpu_custom_call" | custom-call | flops 3000000000 | bytes 9000000 | tf_op jit(solution)/shard_map/waves_forward/pallas_call | solution.py:773
  28.3 0.0 collective-permute-done.3.level_ref
  28.3 3.7 %waves_back.1 = (bf16[2,512,128]{2,1,0:T(8,128)(2,1)S(1)}, bf16[2,512,128]{2,1,0:T(8,128)(2,1)S(1)}, bf16[3,2,256,256]{3,2,1,0:T(8,128)(2,1)S(1)}, bf16[3,2,256,256]{3,2,1,0:T(8,128)(2,1)S(1)}) custom-call(s32[8,128]{1,0:T(8,128)S(1)} %get-tuple-element.32.behind_ref.refs_0_, s32[1,64]{1,0:T(1,128)S(1)} %get-tuple-element.27.own_ref.refs_1_, ...), custom_call_target="tpu_custom_call" | custom-call | flops 4000000000 | bytes 12000000 | tf_op jit(solution)/shard_map/waves_back/pallas_call | solution.py:773
  32.0 0.9 %collective-permute-start.5 = (bf16[3,2,256,256]{3,2,1,0:T(8,128)(2,1)S(1)}, bf16[3,2,256,256]{3,2,1,0:T(8,128)(2,1)S(1)}, u32[]{:S(2)}, u32[]{:S(2)}) collective-permute-start(bf16[3,2,256,256]{3,2,1,0:T(8,128)(2,1)S(1)} %get-tuple-element.38), channel_id=1, source_target_pairs={{0,16},{1,17},{2,18},{3,19},{4,20},{5,21},{6,22},{7,23},{8,24},{9,... | collective-permute-start | bytes 2359304 | tf_op jit(solution)/shard_map/ppermute | solution.py:31
  33.0 2.2 %collective-permute-start.6 = (bf16[2,512,128]{2,1,0:T(8,128)(2,1)S(1)}, bf16[2,512,128]{2,1,0:T(8,128)(2,1)S(1)}, u32[]{:S(2)}, u32[]{:S(2)}) collective-permute-start(bf16[2,512,128]{2,1,0:T(8,128)(2,1)S(1)} %get-tuple-element.39), channel_id=1, source_target_pairs={{1,0},{2,1},{3,2},{4,3},{5,4},{6,5},{7,6},{8,7},{9,8},{10,9},{11,1... | collective-permute-start | bytes 786440 | tf_op jit(solution)/shard_map/ppermute | solution.py:31
  35.1 3.4 %collective-permute-start.7 = (bf16[2,512,128]{2,1,0:T(8,128)(2,1)S(1)}, bf16[2,512,128]{2,1,0:T(8,128)(2,1)S(1)}, u32[]{:S(2)}, u32[]{:S(2)}) collective-permute-start(bf16[2,512,128]{2,1,0:T(8,128)(2,1)S(1)} %get-tuple-element.40), channel_id=1, source_target_pairs={{1,16},{2,17},{3,18},{4,19},{5,20},{6,21},{7,22},{8,23},{9,24},{10... | collective-permute-start | bytes 786440 | tf_op jit(solution)/shard_map/ppermute | solution.py:31
  38.6 0.0 collective-permute-done.8.refs_2_
  38.6 6.5 %waves_a.1 = (bf16[2,512,128]{2,1,0:T(8,128)(2,1)S(1)}, bf16[2,512,128]{2,1,0:T(8,128)(2,1)S(1)}, bf16[2,2,256,256]{3,2,1,0:T(8,128)(2,1)S(1)}, bf16[2,2,256,256]{3,2,1,0:T(8,128)(2,1)S(1)}) custom-call(s32[8,128]{1,0:T(8,128)S(1)} %get-tuple-element.32.behind_ref.refs_0_, s32[1,64]{1,0:T(1,128)S(1)} %get-tuple-element.27.own_ref.refs_1_, ...), custom_call_target="tpu_custom_call" | custom-call | flops 7000000000 | bytes 21000000 | tf_op jit(solution)/shard_map/waves_a/pallas_call | solution.py:773
  45.1 2.2 %collective-permute-start.10 = (bf16[2,512,128]{2,1,0:T(8,128)(2,1)S(1)}, bf16[2,512,128]{2,1,0:T(8,128)(2,1)S(1)}, u32[]{:S(2)}, u32[]{:S(2)}) collective-permute-start(bf16[2,512,128]{2,1,0:T(8,128)(2,1)S(1)} %get-tuple-element.46), channel_id=1, source_target_pairs={{0,1},{1,2},{2,3},{3,4},{4,5},{5,6},{6,7},{7,8},{8,9},{9,10},{10,1... | collective-permute-start | bytes 786440 | tf_op jit(solution)/shard_map/ppermute | solution.py:31
  47.3 4.4 %collective-permute-start.11 = (bf16[2,512,128]{2,1,0:T(8,128)(2,1)S(1)}, bf16[2,512,128]{2,1,0:T(8,128)(2,1)S(1)}, u32[]{:S(2)}, u32[]{:S(2)}) collective-permute-start(bf16[2,512,128]{2,1,0:T(8,128)(2,1)S(1)} %get-tuple-element.47), channel_id=1, source_target_pairs={{0,17},{1,18},{2,19},{3,20},{4,21},{5,22},{6,23},{7,24},{8,25},{9,... | collective-permute-start | bytes 786440 | tf_op jit(solution)/shard_map/ppermute | solution.py:31
  51.7 0.0 collective-permute-done.6.b_back
  51.7 0.1 collective-permute-start.9
  51.8 0.0 collective-permute-done.7.b_back_cross
  51.8 0.0 collective-permute-done.5.b_swap
  51.8 2.1 %gather.1._ = f32[1,2,2048,256]{3,2,1,0:T(8,128)S(1)} custom-call(s32[1,64]{1,0:T(1,128)S(1)} %get-tuple-element.27.own_ref.refs_1_, s32[8,128]{1,0:T(8,128)S(1)} %get-tuple-element.32.behind_ref.refs_0_, bf16[3,2,256,256]{3,2,1,0:T(8,128)(2,1)S(1)} %get-tuple-element.37.refs_9_.b_self, bf16[3,2,256,256]{3,2,1,0:T(8,128)(2,1)S(1)} %collective-permute-done.5.b_swap, ...), custom_call_target="tpu_custom_call" | custom-call | flops 10000000000 | bytes 30000000 | tf_op jit(solution)/shard_map/gather/pallas_call | solution.py:773
  53.9 0.0 collective-permute-done.9.a_swap
  53.9 2.9 %merge.1 = (f32[1,2,2048,256]{3,2,1,0:T(8,128)S(1)}, f32[1,2,2048,256]{3,2,1,0:T(8,128)}) custom-call(s32[1,64]{1,0:T(1,128)S(1)} %get-tuple-element.27.own_ref.refs_1_, f32[1,2,2048,256]{3,2,1,0:T(8,128)S(1)} %gather.1._, bf16[2,2,256,256]{3,2,1,0:T(8,128)(2,1)S(1)} %collective-permute-done.9.a_swap), custom_call_target="tpu_custom_call", output_to_operand_aliasing={{0}: (1, {})} | custom-call | tf_op jit(solution)/shard_map/merge/pallas_call | solution.py:773
  56.8 0.0 collective-permute-done.10.a_back
  56.8 5.6 %collective-permute-done.11.a_back_cross = bf16[2,512,128]{2,1,0:T(8,128)(2,1)S(1)} collective-permute-done((bf16[2,512,128]{2,1,0:T(8,128)(2,1)S(1)}, bf16[2,512,128]{2,1,0:T(8,128)(2,1)S(1)}, u32[]{:S(2)}, u32[]{:S(2)}) %collective-permute-start.11) | collective-permute-done | bytes 262176 | tf_op jit(solution)/shard_map/ppermute | solution.py:31
  62.4 2.5 %finish.1 = (f32[1,2,2048,256]{3,2,1,0:T(8,128)S(1)}, f32[1,2,2048,256]{3,2,1,0:T(8,128)}) custom-call(s32[1,64]{1,0:T(1,128)S(1)} %get-tuple-element.27.own_ref.refs_1_, s32[8,128]{1,0:T(8,128)S(1)} %get-tuple-element.32.behind_ref.refs_0_, f32[1,2,2048,256]{3,2,1,0:T(8,128)S(1)} %get-tuple-element.44._, ...), custom_call_target="tpu_custom_call", output_to_operand_aliasing={{0}: (2, {}), {1}: (3, {})} | custom-call | tf_op jit(solution)/shard_map/finish/pallas_call | solution.py:773
Async XLA Ops:
  0.0 10.7 %copy-start = (f32[1,256,256]{2,1,0:T(8,128)S(1)}, f32[1,256,256]{2,1,0:T(8,128)}, u32[]{:S(2)}) copy-start(f32[1,256,256]{2,1,0:T(8,128)} %angle_ref.1) | copy-start | bytes 786436
  3.6 12.4 %collective-permute-start = (bf16[2,2048,256]{2,1,0:T(8,128)(2,1)S(1)}, bf16[2,2048,256]{2,1,0:T(8,128)(2,1)S(1)}, u32[]{:S(2)}, u32[]{:S(2)}) collective-permute-start(bf16[2,2048,256]{2,1,0:T(8,128)(2,1)S(1)} %get-tuple-element.28.self_ref), channel_id=1, source_target_pairs={{0,16},{1,17},{2,18},{3,19},{4,20},{5,21},{6,22},{7,23},{8,24},{9,... | collective-permute-start | bytes 6291464 | tf_op jit(solution)/shard_map/ppermute | solution.py:31
  4.3 13.9 %collective-permute-start.1 = (bf16[1040,128]{1,0:T(8,128)(2,1)S(1)}, bf16[1040,128]{1,0:T(8,128)(2,1)S(1)}, u32[]{:S(2)}, u32[]{:S(2)}) collective-permute-start(bf16[1040,128]{1,0:T(8,128)(2,1)S(1)} %get-tuple-element.29), channel_id=1, source_target_pairs={{0,1},{1,2},{2,3},{3,4},{4,5},{5,6},{6,7},{7,8},{8,9},{9,10},{10,1... | collective-permute-start | bytes 798728 | tf_op jit(solution)/shard_map/ppermute | solution.py:31
  7.4 16.7 %collective-permute-start.4 = (bf16[1040,128]{1,0:T(8,128)(2,1)S(1)}, bf16[1040,128]{1,0:T(8,128)(2,1)S(1)}, u32[]{:S(2)}, u32[]{:S(2)}) collective-permute-start(bf16[1040,128]{1,0:T(8,128)(2,1)S(1)} %get-tuple-element.30._), channel_id=1, source_target_pairs={{0,17},{1,18},{2,19},{3,20},{4,21},{5,22},{6,23},{7,24},{8,25},{9,... | collective-permute-start | bytes 798728 | tf_op jit(solution)/shard_map/ppermute | solution.py:31
  10.8 5.2 %collective-permute-start.2 = (f32[1,256,256]{2,1,0:T(8,128)S(1)}, f32[1,256,256]{2,1,0:T(8,128)S(1)}, u32[]{:S(2)}, u32[]{:S(2)}) collective-permute-start(f32[1,256,256]{2,1,0:T(8,128)S(1)} %copy-done), channel_id=1, source_target_pairs={{0,16},{1,17},{2,18},{3,19},{4,20},{5,21},{6,22},{7,23},{8,24},{9,... | collective-permute-start | bytes 786440 | tf_op jit(solution)/shard_map/ppermute | solution.py:31
  12.6 11.5 %copy-start.1 = (f32[2,256,256]{2,1,0:T(8,128)S(1)}, f32[2,256,256]{2,1,0:T(8,128)}, u32[]{:S(2)}) copy-start(f32[2,256,256]{2,1,0:T(8,128)} %refs_5_.1) | copy-start | bytes 1572868
  12.7 11.5 %copy-start.2 = (bf16[512,512]{1,0:T(8,128)(2,1)S(1)}, bf16[512,512]{1,0:T(8,128)(2,1)}, u32[]{:S(2)}) copy-start(bf16[512,512]{1,0:T(8,128)(2,1)} %constant.5.clone.two_ref.refs_7_) | copy-start | bytes 1572868
  12.7 11.5 %copy-start.3 = (bf16[512,512]{1,0:T(8,128)(2,1)S(1)}, bf16[512,512]{1,0:T(8,128)(2,1)}, u32[]{:S(2)}) copy-start(bf16[512,512]{1,0:T(8,128)(2,1)} %constant.4.clone.one_ref.refs_6_) | copy-start | bytes 1572868
  12.7 15.7 %collective-permute-start.3 = (bf16[2,256,256]{2,1,0:T(8,128)(2,1)S(1)}, bf16[2,256,256]{2,1,0:T(8,128)(2,1)S(1)}, u32[]{:S(2)}, u32[]{:S(2)}) collective-permute-start(bf16[2,256,256]{2,1,0:T(8,128)(2,1)S(1)} %levels.1._), channel_id=1, source_target_pairs={{0,1},{1,2},{2,3},{3,4},{4,5},{5,6},{6,7},{7,8},{8,9},{9,10},{10,1... | collective-permute-start | bytes 786440 | tf_op jit(solution)/shard_map/ppermute | solution.py:31
  20.1 18.4 %collective-permute-start.8 = (bf16[2,2,512,128]{3,2,1,0:T(8,128)(2,1)S(1)}, bf16[2,2,512,128]{3,2,1,0:T(8,128)(2,1)S(1)}, u32[]{:S(2)}, u32[]{:S(2)}) collective-permute-start(bf16[2,2,512,128]{3,2,1,0:T(8,128)(2,1)S(1)} %get-tuple-element.41), channel_id=1, source_target_pairs={{1,0},{2,1},{3,2},{4,3},{5,4},{6,5},{7,6},{8,7},{9,8},{10,9},{11,1... | collective-permute-start | bytes 1572872 | tf_op jit(solution)/shard_map/ppermute | solution.py:31
  32.0 19.7 %collective-permute-start.5 = (bf16[3,2,256,256]{3,2,1,0:T(8,128)(2,1)S(1)}, bf16[3,2,256,256]{3,2,1,0:T(8,128)(2,1)S(1)}, u32[]{:S(2)}, u32[]{:S(2)}) collective-permute-start(bf16[3,2,256,256]{3,2,1,0:T(8,128)(2,1)S(1)} %get-tuple-element.38), channel_id=1, source_target_pairs={{0,16},{1,17},{2,18},{3,19},{4,20},{5,21},{6,22},{7,23},{8,24},{9,... | collective-permute-start | bytes 2359304 | tf_op jit(solution)/shard_map/ppermute | solution.py:31
  33.0 18.7 %collective-permute-start.6 = (bf16[2,512,128]{2,1,0:T(8,128)(2,1)S(1)}, bf16[2,512,128]{2,1,0:T(8,128)(2,1)S(1)}, u32[]{:S(2)}, u32[]{:S(2)}) collective-permute-start(bf16[2,512,128]{2,1,0:T(8,128)(2,1)S(1)} %get-tuple-element.39), channel_id=1, source_target_pairs={{1,0},{2,1},{3,2},{4,3},{5,4},{6,5},{7,6},{8,7},{9,8},{10,9},{11,1... | collective-permute-start | bytes 786440 | tf_op jit(solution)/shard_map/ppermute | solution.py:31
  35.1 16.7 %collective-permute-start.7 = (bf16[2,512,128]{2,1,0:T(8,128)(2,1)S(1)}, bf16[2,512,128]{2,1,0:T(8,128)(2,1)S(1)}, u32[]{:S(2)}, u32[]{:S(2)}) collective-permute-start(bf16[2,512,128]{2,1,0:T(8,128)(2,1)S(1)} %get-tuple-element.40), channel_id=1, source_target_pairs={{1,16},{2,17},{3,18},{4,19},{5,20},{6,21},{7,22},{8,23},{9,24},{10... | collective-permute-start | bytes 786440 | tf_op jit(solution)/shard_map/ppermute | solution.py:31
  45.1 11.8 %collective-permute-start.10 = (bf16[2,512,128]{2,1,0:T(8,128)(2,1)S(1)}, bf16[2,512,128]{2,1,0:T(8,128)(2,1)S(1)}, u32[]{:S(2)}, u32[]{:S(2)}) collective-permute-start(bf16[2,512,128]{2,1,0:T(8,128)(2,1)S(1)} %get-tuple-element.46), channel_id=1, source_target_pairs={{0,1},{1,2},{2,3},{3,4},{4,5},{5,6},{6,7},{7,8},{8,9},{9,10},{10,1... | collective-permute-start | bytes 786440 | tf_op jit(solution)/shard_map/ppermute | solution.py:31
  47.3 15.1 %collective-permute-start.11 = (bf16[2,512,128]{2,1,0:T(8,128)(2,1)S(1)}, bf16[2,512,128]{2,1,0:T(8,128)(2,1)S(1)}, u32[]{:S(2)}, u32[]{:S(2)}) collective-permute-start(bf16[2,512,128]{2,1,0:T(8,128)(2,1)S(1)} %get-tuple-element.47), channel_id=1, source_target_pairs={{0,17},{1,18},{2,19},{3,20},{4,21},{5,22},{6,23},{7,24},{8,25},{9,... | collective-permute-start | bytes 786440 | tf_op jit(solution)/shard_map/ppermute | solution.py:31
  51.7 2.2 %collective-permute-start.9 = (bf16[2,2,256,256]{3,2,1,0:T(8,128)(2,1)S(1)}, bf16[2,2,256,256]{3,2,1,0:T(8,128)(2,1)S(1)}, u32[]{:S(2)}, u32[]{:S(2)}) collective-permute-start(bf16[2,2,256,256]{3,2,1,0:T(8,128)(2,1)S(1)} %get-tuple-element.43), channel_id=1, source_target_pairs={{0,16},{1,17},{2,18},{3,19},{4,20},{5,21},{6,22},{7,23},{8,24},{9,... | collective-permute-start | bytes 1572872 | tf_op jit(solution)/shard_map/ppermute | solution.py:31
